TPU v7x, 512 devices: a whole 4x8x8 slice. The times are simulated.
512 devices in a mesh: pre: 32 (over y, z_lo, core), rep: 16 (over z_hi, x).
Axes of the slice: x: 4, y: 8, z: 8 (z_hi: 4, z_lo: 2; z = z_hi * 2 + z_lo), core: 2. Of those that a mesh axis runs over, the one named last changes fastest.
Arguments:
- grads: bfloat16 [32, 32, 512, 512], P('rep', 'pre')
- owner: int32 [32], replicated, may hold values from 0 to 31, as said below
- state: float32 [32, 2, 512, 512], P('pre', None, 'rep'), as said below
Outputs:
- new_state: float32 [32, 2, 512, 512], P('pre', None, 'rep')
- update: bfloat16 [32, 512, 512], P('pre', 'rep')
Inputs may be any that keep to these rules, and one draw needn't show every extreme that they name: Each owner index is named by at most 2 blocks, and some owner by exactly 2. `state`: each matrix is symmetric.
All inputs are finite; a program needn't handle non-finite values.
Results may differ from a plain program's by a relative error of at most 0.006.
Values sent between devices are 32-bit elements; how exact they have to be, the bound alone decides.
No kernel may reach another device: no remote copies, remote signals or barrier semaphores. Data moves between devices by JAX's collectives and lax.ppermute only.
A program may use at most 64 MiB of HBM per device.

v0:
```python
import jax
import jax.numpy as jnp
from jax import lax
from jax.sharding import PartitionSpec as P

ITERS = 4


DAMP = 0.05


def inverse_root_rows(stat_rows):
    row_count = stat_rows.shape[1]
    order_size = stat_rows.shape[2]
    offset = lax.axis_index("rep") * row_count
    identity = jnp.eye(order_size, dtype=jnp.float32)
    row_ids = lax.broadcasted_iota(jnp.int32, (row_count, order_size), 0) + offset
    col_ids = lax.broadcasted_iota(jnp.int32, (row_count, order_size), 1)
    eye_rows = (row_ids == col_ids).astype(jnp.float32)
    squares = lax.psum(jnp.sum(stat_rows * stat_rows, axis=(1, 2)), "rep")
    norm_stat = jnp.sqrt(squares)
    damped = stat_rows + (DAMP * norm_stat)[:, None, None] * eye_rows
    scale_norm = jnp.sqrt(lax.psum(jnp.sum(damped * damped, axis=(1, 2)), "rep"))
    iterate = damped / scale_norm[:, None, None]
    root_rows = (scale_norm ** (-0.25))[:, None, None] * eye_rows
    for rounds in range(ITERS):
        whole_iterate = lax.all_gather(iterate, "rep", axis=1, tiled=True)
        factor = (5.0 * identity - whole_iterate) * 0.25
        root_rows = jnp.einsum("srk,skj->srj", root_rows, factor, precision=lax.Precision.HIGHEST)
        if rounds + 1 < ITERS:
            for repeat in range(4):
                iterate = jnp.einsum(
                    "srk,skj->srj", iterate, factor, precision=lax.Precision.HIGHEST
                )
    return root_rows


def body(grads, owner, state):
    local_grads = grads[:, 0]
    micro_count = local_grads.shape[0]
    capacity = state.shape[1]
    gram_rows = lax.psum_scatter(
        lax.dot_general(
            local_grads,
            local_grads,
            (((0, 2), (0, 2)), ((), ())),
            preferred_element_type=jnp.float32,
        ),
        "rep",
        scatter_dimension=0,
        tiled=True,
    )
    grad_total = lax.psum(jnp.sum(local_grads, axis=0, dtype=jnp.float32), "rep")
    mean_grad = (grad_total / (micro_count * lax.axis_size("rep"))).astype(jnp.bfloat16)
    own_index = lax.axis_index("pre")
    blocks = owner.shape[0]
    block_ids = jnp.arange(blocks, dtype=jnp.int32)
    earlier = (owner[None, :] == owner[:, None]) & (block_ids[None, :] < block_ids[:, None])
    slot_of = jnp.sum(earlier.astype(jnp.int32), axis=1)
    my_owner = owner[own_index]
    target = (block_ids == my_owner).astype(jnp.float32)
    outgoing = target[:, None, None] * gram_rows[None]
    incoming = lax.all_to_all(outgoing, "pre", split_axis=0, concat_axis=0, tiled=True)
    slot_ids = jnp.arange(capacity, dtype=jnp.int32)
    held_slots = ((owner[:, None] == own_index) & (slot_of[:, None] == slot_ids[None, :])).astype(
        jnp.float32
    )
    new_state = state[0] + jnp.einsum(
        "qs,qrk->srk", held_slots, incoming, precision=lax.Precision.HIGHEST
    )
    outbound = jnp.einsum(
        "qs,srk->qrk", held_slots, inverse_root_rows(new_state), precision=lax.Precision.HIGHEST
    )
    precond = jnp.sum(
        lax.all_to_all(outbound, "pre", split_axis=0, concat_axis=0, tiled=True), axis=0
    )
    update = jnp.dot(
        precond.astype(jnp.bfloat16), mean_grad, preferred_element_type=jnp.float32
    ).astype(jnp.bfloat16)
    return (new_state[None], update[None])


def solution(mesh):
    placed = (P("rep", "pre", None, None), P(), P("pre", None, "rep", None))
    return jax.shard_map(
        body,
        mesh=mesh,
        in_specs=placed,
        out_specs=(P("pre", None, "rep", None), P("pre", "rep", None)),
        check_vma=False,
    )
```

profile of v0, /device:TPU:1, one launch (start us, length us, event | category | flops | bytes accessed | tf_op | source)
XLA Modules:
  0.0 729.0 jit_solution(14940018733314180214)
XLA Ops:
  7.2 0.0 copy-start.8
  7.2 0.0 reduce-scatter.2.cloned.1.call-start
  7.2 3.2 convolution_bitcast_fusion
  10.5 0.0 reduce-scatter.2.cloned.1.call-update
  10.5 0.0 copy-done.8
  10.5 0.6 dynamic_slice.3
  11.1 0.6 compare_convert_fusion
  11.8 96.2 %reduce-scatter.2.cloned.1.call-done = f32[32,512]{1,0:T(8,128)} async-done(((f32[512,512]{1,0:T(8,128)}), f32[32,512]{1,0:T(8,128)}) %reduce-scatter.2.cloned.1.call-update) | async-done | bytes 65552 | tf_op jit(solution)/shard_map/reduce_scatter | solution.py:42
  108.0 2.4 broadcast_multiply_fusion
  110.4 9.7 %all-to-all-start = ((f32[32,32,512]{2,1,0:T(8,128)}), f32[32,32,512]{2,1,0:T(8,128)S(1)}, u32[]{:S(2)}, u32[]{:S(2)}) async-start(f32[32,32,512]{2,1,0:T(8,128)} %broadcast_multiply_fusion), calls=%async_computation.1 | async-start | bytes 4194304 | tf_op jit(solution)/shard_map/all_to_all | solution.py:63
  120.1 0.0 copy-start.7
  120.1 0.0 all-gather.5.cloned.1.call-start
  120.2 0.2 convert_reduce_fusion.1
  120.4 0.1 fusion.21
  120.4 49.7 %all-to-all-done = f32[32,32,512]{2,1,0:T(8,128)S(1)} async-done(((f32[32,32,512]{2,1,0:T(8,128)}), f32[32,32,512]{2,1,0:T(8,128)S(1)}, u32[]{:S(2)}, u32[]{:S(2)}) %all-to-all-start) | async-done | bytes 2097184 | tf_op jit(solution)/shard_map/all_to_all | solution.py:63
  170.2 2.0 fusion.6
  172.1 0.0 copy-done.7
  172.1 0.1 multiply_reduce_fusion.1
  172.3 35.4 %psum.21 = f32[2]{0:T(128)S(1)} all-reduce(f32[2]{0:T(128)S(1)} %get-tuple-element.10), channel_id=1, replica_groups=mesh['pre'=32,'rep'=16] {'rep'}, use_global_device_ids=true, to_apply=%region_3.0 | all-reduce | flops 2 | bytes 16 | tf_op jit(solution)/shard_map/psum | solution.py:20
  207.7 0.2 multiply_reduce_fusion
  207.9 32.1 %psum.22 = f32[2]{0:T(128)S(1)} all-reduce(f32[2]{0:T(128)S(1)} %multiply_reduce_fusion), channel_id=1, replica_groups=mesh['pre'=32,'rep'=16] {'rep'}, use_global_device_ids=true, to_apply=%region_5.0 | all-reduce | flops 2 | bytes 16 | tf_op jit(solution)/shard_map/psum | solution.py:23
  240.0 0.1 fusion.18
  240.1 0.8 copy.72
  240.8 0.0 all-gather.5.cloned.1.call-update
  240.9 0.0 all-gather.7.cloned.1.call-start
  240.9 0.1 fusion.12
  241.0 72.8 %all-gather.5.cloned.1.call-done = f32[2,512,512]{2,0,1:T(2,128)} async-done(((f32[2,32,512]{2,0,1:T(2,128)}), f32[2,512,512]{2,0,1:T(2,128)}) %all-gather.5.cloned.1.call-update) | async-done | bytes 2097168 | tf_op jit(solution)/shard_map/all_gather | solution.py:27
  313.8 3.4 fusion.38
  317.3 1.7 fusion.36
  318.9 1.7 fusion.34
  320.6 1.7 fusion.32
  322.3 0.8 copy.74
  323.0 0.0 all-gather.7.cloned.1.call-update
  323.1 0.2 all-gather.9.cloned.1.call-start
  323.3 63.2 %all-gather.7.cloned.1.call-done = f32[2,512,512]{2,0,1:T(2,128)} async-done(((f32[2,32,512]{2,0,1:T(2,128)}), f32[2,512,512]{2,0,1:T(2,128)}) %all-gather.7.cloned.1.call-update) | async-done | bytes 2097168 | tf_op jit(solution)/shard_map/all_gather | solution.py:27
  386.5 3.4 fusion.47
  389.9 1.7 fusion.45
  391.6 1.7 fusion.43
  393.3 1.7 fusion.41
  395.0 0.7 copy.76
  395.7 0.0 all-gather.9.cloned.1.call-update
  395.7 0.0 all-gather.11.cloned.1.call-start
  395.8 63.4 %all-gather.9.cloned.1.call-done = f32[2,512,512]{2,0,1:T(2,128)} async-done(((f32[2,32,512]{2,0,1:T(2,128)}), f32[2,512,512]{2,0,1:T(2,128)}) %all-gather.9.cloned.1.call-update) | async-done | bytes 2097168 | tf_op jit(solution)/shard_map/all_gather | solution.py:27
  459.2 3.4 fusion.57
  462.6 1.7 fusion.55
  464.3 1.7 fusion.53
  466.0 1.7 fusion.51
  467.6 0.8 copy.78
  468.4 0.0 all-gather.11.cloned.1.call-update
  468.4 1.7 fusion.16
  470.1 1.7 fusion.49
  471.8 1.7 fusion.59
  473.5 58.4 %all-gather.11.cloned.1.call-done = f32[2,512,512]{2,0,1:T(2,128)} async-done(((f32[2,32,512]{2,0,1:T(2,128)}), f32[2,512,512]{2,0,1:T(2,128)}) %all-gather.11.cloned.1.call-update) | async-done | bytes 2097168 | tf_op jit(solution)/shard_map/all_gather | solution.py:27
  531.9 3.5 fusion.1
  535.4 1.1 fusion.14
  536.4 2.6 copy.81
  539.0 8.7 %all-to-all-start.1 = ((f32[32,32,512]{2,1,0:T(8,128)}), f32[32,32,512]{2,1,0:T(8,128)S(1)}, u32[]{:S(2)}, u32[]{:S(2)}) async-start(f32[32,32,512]{2,1,0:T(8,128)} %copy.81), calls=%async_computation.2 | async-start | bytes 4194304 | tf_op jit(solution)/shard_map/all_to_all | solution.py:75
  547.7 0.0 all-reduce.2.cloned.1.call-start
  547.8 1.2 convert_reduce_fusion
  548.9 0.0 all-reduce.2.cloned.1.call-update
  549.0 48.8 %all-to-all-done.1 = f32[32,32,512]{2,1,0:T(8,128)S(1)} async-done(((f32[32,32,512]{2,1,0:T(8,128)}), f32[32,32,512]{2,1,0:T(8,128)S(1)}, u32[]{:S(2)}, u32[]{:S(2)}) %all-to-all-start.1) | async-done | bytes 2097184 | tf_op jit(solution)/shard_map/all_to_all | solution.py:75
  597.8 0.2 reduce_sum.48
  597.9 122.1 %all-reduce.2.cloned.1.call-done = f32[512,512]{1,0:T(8,128)} async-done(((f32[512,512]{1,0:T(8,128)}), f32[512,512]{1,0:T(8,128)}) %all-reduce.2.cloned.1.call-update) | async-done | bytes 1048592 | tf_op jit(solution)/shard_map/psum | solution.py:53
  720.1 2.0 fusion.8
  (18 shorter events, 0.1 us)
Async XLA Ops:
  7.2 3.3 copy-start.8
  7.2 100.8 %reduce-scatter.2.cloned.1.call-start = ((), (), s32[]{:S(2)}) async-start(), calls=%async_computation.3 | async-start | bytes 1114112 | tf_op jit(solution)/shard_map/reduce_scatter | solution.py:42
  110.4 59.8 %all-to-all-start = ((f32[32,32,512]{2,1,0:T(8,128)}), f32[32,32,512]{2,1,0:T(8,128)S(1)}, u32[]{:S(2)}, u32[]{:S(2)}) async-start(f32[32,32,512]{2,1,0:T(8,128)} %broadcast_multiply_fusion), calls=%async_computation.1 | async-start | bytes 4194304 | tf_op jit(solution)/shard_map/all_to_all | solution.py:63
  120.1 52.0 %copy-start.7 = (f32[1,2,32,512]{3,2,1,0:T(8,128)S(1)}, f32[1,2,32,512]{3,2,1,0:T(8,128)}, u32[]{:S(2)}) copy-start(f32[1,2,32,512]{3,2,1,0:T(8,128)} %param.5) | copy-start | bytes 393220
  120.1 193.7 %all-gather.5.cloned.1.call-start = ((), (), s32[]{:S(2)}) async-start(), calls=%async_computation.4 | async-start | bytes 2228224 | tf_op jit(solution)/shard_map/all_gather | solution.py:27
  172.3 145.0 %copy-start.5 = (f32[2,32,512]{2,1,0:T(8,128)}, f32[2,32,512]{2,1,0:T(8,128)S(1)}, u32[]{:S(2)}) copy-start(f32[2,32,512]{2,1,0:T(8,128)S(1)} %get-tuple-element.11) | copy-start | bytes 393220
  240.9 145.7 %all-gather.7.cloned.1.call-start = ((), (), s32[]{:S(2)}) async-start(), calls=%async_computation.5 | async-start | bytes 2228224 | tf_op jit(solution)/shard_map/all_gather | solution.py:27
  313.8 3.4 copy-start
  323.1 136.1 %all-gather.9.cloned.1.call-start = ((), (), s32[]{:S(2)}) async-start(), calls=%async_computation.6 | async-start | bytes 2228224 | tf_op jit(solution)/shard_map/all_gather | solution.py:27
  386.5 3.4 copy-start.1
  395.7 136.2 %all-gather.11.cloned.1.call-start = ((), (), s32[]{:S(2)}) async-start(), calls=%async_computation.7 | async-start | bytes 2228224 | tf_op jit(solution)/shard_map/all_gather | solution.py:27
  459.2 3.4 copy-start.3
  468.4 1.7 copy-start.2
  470.1 1.7 copy-start.4
  539.0 8.8 %copy-start.6 = (bf16[2,1,512,512]{3,2,1,0:T(8,128)(2,1)S(1)}, bf16[2,1,512,512]{3,2,1,0:T(8,128)(2,1)}, u32[]{:S(2)}) copy-start(bf16[2,1,512,512]{3,2,1,0:T(8,128)(2,1)} %param.3) | copy-start | bytes 3145732
  539.0 58.8 %all-to-all-start.1 = ((f32[32,32,512]{2,1,0:T(8,128)}), f32[32,32,512]{2,1,0:T(8,128)S(1)}, u32[]{:S(2)}, u32[]{:S(2)}) async-start(f32[32,32,512]{2,1,0:T(8,128)} %copy.81), calls=%async_computation.2 | async-start | bytes 4194304 | tf_op jit(solution)/shard_map/all_to_all | solution.py:75
  547.7 172.4 %all-reduce.2.cloned.1.call-start = ((), (), s32[]{:S(2)}) async-start(), calls=%async_computation.8 | async-start | bytes 2097152 | tf_op jit(solution)/shard_map/psum | solution.py:53
Sparse Core Ops, SparseCore 0:
  12.1 95.8 reduce-scatter.1
  241.0 72.7 all-gather.4
  323.2 63.2 all-gather.6
  395.9 63.2 all-gather.8
  468.5 63.2 all-gather.10
  551.4 168.6 all-reduce.1
where the time goes:
time: 738 us; the launch traced here: 729 us
  waiting for transfers between devices  575 us (78%)
  blocking collectives  67.5 us (9%)
  matrix products  42 us (6%)
  starting transfers between devices  18.8 us (3%)
  between operations  14.4 us (2%)
    all_gather x4, waiting for transfers between devices, inverse_root_rows(): whole_iterate = lax.all_gather(iterate, 'rep', axis=1, tiled=True)  258 us
    psum x1, waiting for transfers between devices, body(): lax.psum(jnp.sum(local_grads, axis=0, dtype=jnp.float32), 'rep')  122 us
    reduce_scatter x1, waiting for transfers between devices, body(): lax.psum_scatter(lax.dot_general(local_grads, local_grads, (((0, 2), (0,...  96.2 us
    all_to_all x1, waiting for transfers between devices, body(): lax.all_to_all(outgoing, 'pre', split_axis=0, concat_axis=0, tiled=True)  49.7 us
    all_to_all x1, waiting for transfers between devices, body(): lax.all_to_all(outbound, 'pre', split_axis=0, concat_axis=0, tiled=True)  48.8 us
    psum x1, blocking collectives, inverse_root_rows(): squares = lax.psum(jnp.sum(stat_rows * stat_rows, axis=(1, 2)), 'rep')  35.4 us
    psum x1, blocking collectives, inverse_root_rows(): lax.psum(jnp.sum(damped * damped, axis=(1, 2)), 'rep')  32.1 us
    dot_general x12, matrix products, inverse_root_rows(): jnp.einsum('srk,skj->srj', iterate, factor, precision=lax.Precision.HIGHEST)  25.2 us
  transfers between devices with their start and end apart: 8, of which 8 were waited for; matrix products, arithmetic and copies ran while one was open for 1% of the time, Pallas kernels for 0%

commit v1 on v0

v1 whole, which is shorter than its diff:
```python
import jax
import jax.numpy as jnp
from jax import lax
from jax.experimental import pallas as pl
from jax.experimental.pallas import tpu as pltpu
from jax.sharding import PartitionSpec as P

ITERS = 4
DAMP = 0.05
GROUP = 4
f32 = jnp.float32
bf16 = jnp.bfloat16

VMEM = pl.BlockSpec(memory_space=pltpu.VMEM)
SMEM = pl.BlockSpec(memory_space=pltpu.SMEM)
PARAMS = pltpu.CompilerParams(vmem_limit_bytes=40 * 2**20)


def call(kernel, out_shape, in_specs, cost, *args):
    multiple = isinstance(out_shape, (list, tuple))
    return pl.pallas_call(
        kernel,
        out_shape=out_shape,
        in_specs=in_specs,
        out_specs=[VMEM] * len(out_shape) if multiple else VMEM,
        compiler_params=PARAMS,
        cost_estimate=pl.CostEstimate(flops=cost[0], bytes_accessed=cost[1], transcendentals=0),
    )(*args)


def gram_kernel(grads_ref, gram_ref, total_ref):
    shards, size, _ = grads_ref.shape
    parts = gram_ref.shape[0]
    rows = size // parts
    gram = None
    total = None
    for s in range(shards):
        g = grads_ref[s]
        term = lax.dot_general(g, g, (((1,), (1,)), ((), ())), preferred_element_type=f32)
        gram = term if gram is None else gram + term
        wide = g.astype(f32)
        total = wide if total is None else total + wide
    gram_ref[...] = gram.reshape(parts, rows, size)
    total_ref[...] = total.reshape(parts, rows, size)


def choose(k, options):
    value = options[0]
    for i in range(1, len(options)):
        value = jnp.where(k == i, options[i], value)
    return value


def spread_kernel(where_ref, held0, held1, held2, held3, out_ref):
    held = (held0, held1, held2, held3)
    for y in range(out_ref.shape[0]):
        k = where_ref[0, y]
        j = where_ref[1, y]
        out_ref[y] = choose(k, [h[pl.ds(j, 1)][0] for h in held])


def stat_kernel(source_ref, gram_ref, state_ref, wide_ref, owner_ref):
    stat = jnp.sum(gram_ref[...], axis=0) + state_ref[pl.ds(source_ref[0], 1)][0]
    wide_ref[...] = jnp.broadcast_to(stat[None], wide_ref.shape)
    owner_ref[...] = jnp.broadcast_to(stat[None], owner_ref.shape)


def total_kernel(total_ref, wide_ref):
    wide_ref[...] = jnp.broadcast_to(jnp.sum(total_ref[...], axis=0)[None], wide_ref.shape)


def return_kernel(source_ref, rows_ref, out0, out1, out2, out3):
    for k, out in enumerate((out0, out1, out2, out3)):
        for j in range(out.shape[0]):
            out[j] = rows_ref[pl.ds(source_ref[k, j], 1)][0]


def state_kernel(sender_ref, state_ref, got0, got1, got2, got3, out_ref):
    for j in range(out_ref.shape[0]):
        out_ref[j] = choose(
            sender_ref[j], [got0[j], got1[j], got2[j], got3[j], state_ref[j]]
        )


def product(a, b):
    a_high = a.astype(bf16)
    a_low = (a - a_high.astype(f32)).astype(bf16)
    b_high = b.astype(bf16)
    b_low = (b - b_high.astype(f32)).astype(bf16)
    return jnp.dot(
        jnp.concatenate([a_high, a_high, a_low], axis=1),
        jnp.concatenate([b_high, b_low, b_high], axis=0),
        preferred_element_type=f32,
    )


def newton_kernel(place_ref, stat_ref, root_ref):
    parts, rows, size = stat_ref.shape
    stat = stat_ref[...].reshape(size, size)
    row_ids = lax.broadcasted_iota(jnp.int32, (size, size), 0)
    col_ids = lax.broadcasted_iota(jnp.int32, (size, size), 1)
    eye = (row_ids == col_ids).astype(f32)
    norm = jnp.sqrt(jnp.sum(stat * stat))
    damped = stat + (DAMP * norm) * eye
    scale = jnp.sqrt(jnp.sum(damped * damped))
    iterate = damped / scale
    root = 1.25 * eye - 0.25 * iterate
    for _ in range(1, ITERS):
        square = product(iterate, iterate)
        factor2 = 1.5625 * eye - 0.625 * iterate + 0.0625 * square
        iterate = product(iterate, product(factor2, factor2))
        root = 1.25 * root - 0.25 * product(root, iterate)
    root = (root * jnp.exp(-0.25 * jnp.log(scale))).astype(bf16)
    root_ref[...] = root.reshape(parts, rows, size)


def update_kernel(count, place_ref, root_ref, total_ref, out_ref):
    parts, rows, size = total_ref.shape
    mean = (total_ref[...].reshape(size, size) / count).astype(bf16)
    mine = root_ref[pl.ds(place_ref[0], 1)][0]
    out_ref[0] = jnp.dot(mine, mean, preferred_element_type=f32).astype(bf16)


def body(grads, owner, state):
    local = grads[:, 0]
    shards, size, _ = local.shape
    held = state[0]
    capacity, rows, _ = held.shape
    reps = lax.axis_size("rep")
    blocks = owner.shape[0]
    groups = blocks // GROUP
    shape = lambda *s: jax.ShapeDtypeStruct(s, f32)

    me = lax.axis_index("pre")
    my_y, my_q = me // GROUP, me % GROUP
    place = lax.axis_index("rep").reshape(1).astype(jnp.int32)
    ids = jnp.arange(blocks, dtype=jnp.int32)
    slot = jnp.sum(
        ((owner[None, :] == owner[:, None]) & (ids[None, :] < ids[:, None])).astype(jnp.int32), axis=1
    )
    mine = ids % GROUP == my_q
    by_y = lambda v: jnp.sum(
        jnp.where(mine[None, :] & (ids[None, :] // GROUP == jnp.arange(groups)[:, None]), v[None, :], 0), axis=1
    )
    wanted, wanted_slot = by_y(owner), by_y(slot)
    where = jnp.stack([(wanted % GROUP) ^ my_q, wanted_slot]).astype(jnp.int32)
    my_owner = jnp.sum(jnp.where(ids == me, owner, 0))
    source = (my_owner // GROUP).reshape(1).astype(jnp.int32)
    q_ids = jnp.arange(GROUP, dtype=jnp.int32)
    targets = my_y * GROUP + (q_ids ^ my_q)
    slots = jnp.arange(capacity, dtype=jnp.int32)
    block_of = jnp.max(
        jnp.where(
            (owner[None, None, :] == targets[:, None, None]) & (slot[None, None, :] == slots[None, :, None]),
            ids[None, None, :],
            -1,
        ),
        axis=2,
    )
    return_source = jnp.maximum(block_of, 0) // GROUP
    sender = jnp.where(block_of[0] >= 0, (block_of[0] % GROUP) ^ my_q, GROUP).astype(jnp.int32)

    def across(x, k):
        return lax.ppermute(x, "pre", [(i, i ^ k) for i in range(blocks)])

    y_groups = [[y * GROUP + q for y in range(groups)] for q in range(GROUP)]

    gram, total = call(
        gram_kernel,
        [shape(reps, rows, size), shape(reps, rows, size)],
        [VMEM],
        (2 * shards * size**3, 4 * size * size * (shards + 2)),
        local,
    )
    gram = lax.all_to_all(gram, "rep", 0, 0, tiled=True)
    shared = [held] + [across(held, k) for k in range(1, GROUP)]
    chosen = call(
        spread_kernel,
        shape(groups, rows, size),
        [SMEM] + [VMEM] * GROUP,
        (0, 4 * size * rows * 16),
        where,
        *shared,
    )
    chosen = lax.all_to_all(chosen, "pre", 0, 0, tiled=True, axis_index_groups=y_groups)
    stat, outgoing = call(
        stat_kernel,
        [shape(reps, rows, size), shape(groups, rows, size)],
        [SMEM, VMEM, VMEM],
        (0, 4 * size * rows * 48),
        source,
        gram,
        chosen,
    )
    stat = lax.all_to_all(stat, "rep", 0, 0, tiled=True)
    total = lax.all_to_all(total, "rep", 0, 0, tiled=True)
    total = call(
        total_kernel, shape(reps, rows, size), [VMEM], (0, 4 * size * rows * 32), total
    )
    total = lax.all_to_all(total, "rep", 0, 0, tiled=True)
    outgoing = lax.all_to_all(outgoing, "pre", 0, 0, tiled=True, axis_index_groups=y_groups)
    returned = call(
        return_kernel,
        [shape(capacity, rows, size)] * GROUP,
        [SMEM, VMEM],
        (0, 4 * size * rows * 16),
        return_source.astype(jnp.int32),
        outgoing,
    )
    returned = [returned[0]] + [across(returned[k], k) for k in range(1, GROUP)]
    new_state = call(
        state_kernel,
        shape(capacity, rows, size),
        [SMEM] + [VMEM] * (GROUP + 1),
        (0, 4 * size * rows * 12),
        sender,
        held,
        *returned,
    )
    root = call(
        newton_kernel,
        jax.ShapeDtypeStruct((reps, rows, size), bf16),
        [SMEM, VMEM],
        (2 * 36 * size**3, 6 * size * size),
        place,
        stat,
    )
    count = shards * reps
    update = call(
        lambda *refs: update_kernel(count, *refs),
        jax.ShapeDtypeStruct((1, rows, size), bf16),
        [SMEM, VMEM, VMEM],
        (2 * rows * size * size, 6 * size * size),
        place,
        root,
        total,
    )
    return (new_state[None], update)


def solution(mesh):
    placed = (P("rep", "pre", None, None), P(), P("pre", None, "rep", None))
    return jax.shard_map(
        body,
        mesh=mesh,
        in_specs=placed,
        out_specs=(P("pre", None, "rep", None), P("pre", "rep", None)),
        check_vma=False,
    )
```

time: 738 us -> 207 us (0.28); the launches traced: 729 us -> 207 us
  waiting for transfers between devices: 575 us -> 60.9 us
  starting transfers between devices: 18.8 us -> 71.8 us
  matrix products: 42 us -> 0 us
  blocking collectives: 67.5 us -> 47.6 us
  Pallas kernels: 0 us -> 17.8 us
  between operations: 14.4 us -> 3.49 us
    all_gather x4 -> x0, waiting for transfers between devices: 258 us -> none  [inverse_root_rows(): whole_iterate = lax.all_gather(iterate, 'rep', axis=1, tiled=True)]
    psum x1 -> x0, waiting for transfers between devices: 122 us -> none  [body(): lax.psum(jnp.sum(local_grads, axis=0, dtype=jnp.float32), 'rep')]
    reduce_scatter x1 -> x0, waiting for transfers between devices: 96.2 us -> none  [body(): lax.psum_scatter(lax.dot_general(local_grads, local_grads, (((0, 2), (0,...]
    psum x2 -> x0, blocking collectives: 67.5 us -> none  [the longest x1 35.4 us: inverse_root_rows(): squares = lax.psum(jnp.sum(stat_rows * stat_rows, axis=(1, 2)), 'rep')]
    all_to_all x2 -> x4, waiting for transfers between devices: 98.5 us -> 44.5 us  [the longest x1 16.2 us: body(): lax.all_to_all(chosen, 'pre', 0, 0, tiled=True, axis_index_groups=y_groups)]
    ppermute x0 -> x6, starting transfers between devices: none -> 51.5 us  [across(): return lax.ppermute(x, 'pre', [(i, i ^ k) for i in range(blocks)])]
    all_to_all x0 -> x2, blocking collectives: none -> 47.6 us  [the longest x1 33.1 us: body(): gram = lax.all_to_all(gram, 'rep', 0, 0, tiled=True)]
    dot_general x20 -> x0, matrix products: 42 us -> none  [the longest x12 25.2 us: inverse_root_rows(): jnp.einsum('srk,skj->srj', iterate, factor, precision=lax.Precision.HIGHEST)]
  transfers between devices with their start and end apart: 8 -> 10, of which waited for: 8 -> 6; matrix products, arithmetic and copies ran while one was open for 1% -> 1% of each run, Pallas kernels for 0% -> 8%
where the time goes in v1:
time: 207 us
  starting transfers between devices  71.8 us (35%)
  waiting for transfers between devices  60.9 us (29%)
  blocking collectives  47.6 us (23%)
  Pallas kernels  17.8 us (9%)
  local copies, waits for them, and re-layouts  3.77 us (2%)
  between operations  3.49 us (2%)
    ppermute x6, starting transfers between devices, across(): return lax.ppermute(x, 'pre', [(i, i ^ k) for i in range(blocks)])  51.5 us
    all_to_all x1, blocking collectives, body(): gram = lax.all_to_all(gram, 'rep', 0, 0, tiled=True)  33.1 us
    pallas_call x8, Pallas kernels, call(): pl.pallas_call(kernel, out_shape=out_shape, in_specs=in_specs, out_specs=...  17.8 us
    ppermute x6, waiting for transfers between devices, across(): return lax.ppermute(x, 'pre', [(i, i ^ k) for i in range(blocks)])  16.3 us
    all_to_all x1, waiting for transfers between devices, body(): lax.all_to_all(chosen, 'pre', 0, 0, tiled=True, axis_index_groups=y_groups)  16.2 us
    all_to_all x1, blocking collectives, body(): lax.all_to_all(outgoing, 'pre', 0, 0, tiled=True, axis_index_groups=y_gro...  14.5 us
    all_to_all x1, waiting for transfers between devices, body(): stat = lax.all_to_all(stat, 'rep', 0, 0, tiled=True)  14.3 us
    all_to_all x2, waiting for transfers between devices, body(): total = lax.all_to_all(total, 'rep', 0, 0, tiled=True)  14.1 us
  transfers between devices with their start and end apart: 10, of which 6 were waited for; matrix products, arithmetic and copies ran while one was open for 1% of the time, Pallas kernels for 8%

profile of v1, /device:TPU:1, one launch (start us, length us, event | category | flops | bytes accessed | tf_op | source)
XLA Modules:
  0.0 206.6 jit_solution(18112373136693267327)
XLA Ops:
  0.6 5.4 %collective-permute-start.2 = (f32[2,32,512]{2,1,0:T(8,128)}, f32[2,32,512]{2,1,0:T(8,128)S(1)}, u32[]{:S(2)}, u32[]{:S(2)}) collective-permute-start(f32[2,32,512]{2,1,0:T(8,128)} %bitcast.8), channel_id=1, source_target_pairs={{0,48},{16,32},{32,16},{48,0},{64,112},{80,96},{96,80},{112,64},{1... | collective-permute-start | bytes 393224 | tf_op jit(solution)/shard_map/ppermute | solution.py:164
  6.0 6.7 %collective-permute-start.1 = (f32[2,32,512]{2,1,0:T(8,128)}, f32[2,32,512]{2,1,0:T(8,128)S(1)}, u32[]{:S(2)}, u32[]{:S(2)}) collective-permute-start(f32[2,32,512]{2,1,0:T(8,128)} %bitcast.9), channel_id=1, source_target_pairs={{0,32},{16,48},{32,0},{48,16},{64,96},{80,112},{96,64},{112,80},{1... | collective-permute-start | bytes 393224 | tf_op jit(solution)/shard_map/ppermute | solution.py:164
  12.7 1.9 collective-permute-start
  14.6 0.0 copy-start.5
  14.7 0.6 copy-done.5
  15.3 0.2 convert_reduce_fusion
  15.5 0.1 select_reduce_fusion.1
  15.7 0.0 collective-permute-done.2.held3
  15.7 0.7 collective-permute-done.1.held2
  16.4 0.0 collective-permute-done.held1
  16.4 0.0 copy-start.2
  16.4 0.9 copy-done.2
  17.3 0.0 copy-start.4
  17.3 1.4 shard_map.51
  18.8 3.7 %all-to-all-start.1 = ((f32[8,32,512]{2,1,0:T(8,128)}), f32[8,32,512]{2,1,0:T(8,128)S(1)}, u32[]{:S(2)}, u32[]{:S(2)}) async-start(f32[8,32,512]{2,1,0:T(8,128)} %shard_map.51), calls=%async_computation.1 | async-start | bytes 1048576 | tf_op jit(solution)/shard_map/all_to_all | solution.py:185
  22.5 0.0 copy-done.4
  22.5 0.7 shard_map.50
  23.3 0.0 copy-start
  23.3 1.0 copy-done
  24.3 16.2 %all-to-all-done.1.state_ref = f32[8,32,512]{2,1,0:T(8,128)S(1)} async-done(((f32[8,32,512]{2,1,0:T(8,128)}), f32[8,32,512]{2,1,0:T(8,128)S(1)}, u32[]{:S(2)}, u32[]{:S(2)}) %all-to-all-start.1) | async-done | bytes 524320 | tf_op jit(solution)/shard_map/all_to_all | solution.py:185
  40.5 33.1 %all_to_all.30.gram_ref = f32[16,32,512]{2,1,0:T(8,128)S(1)} all-to-all(f32[16,32,512]{2,1,0:T(8,128)S(1)} %get-tuple-element.10), channel_id=1, replica_groups=mesh['pre'=32,'rep'=16] {'rep'}, dimensions={0} | all-to-all | bytes 2097152 | tf_op jit(solution)/shard_map/all_to_all | solution.py:175
  73.6 7.6 %all-to-all-start.4 = ((f32[16,32,512]{2,1,0:T(8,128)}), f32[16,32,512]{2,1,0:T(8,128)S(1)}, u32[]{:S(2)}, u32[]{:S(2)}) async-start(f32[16,32,512]{2,1,0:T(8,128)} %copy-done), calls=%async_computation.4 | async-start | bytes 2097152 | tf_op jit(solution)/shard_map/all_to_all | solution.py:196
  81.2 0.6 fusion.4
  84.4 0.2 shard_map.52
  84.6 0.0 copy-start.1
  84.6 1.0 copy-done.1
  85.6 14.1 %all-to-all-done.4.total_ref = f32[16,32,512]{2,1,0:T(8,128)S(1)} async-done(((f32[16,32,512]{2,1,0:T(8,128)}), f32[16,32,512]{2,1,0:T(8,128)S(1)}, u32[]{:S(2)}, u32[]{:S(2)}) %all-to-all-start.4) | async-done | bytes 1048608 | tf_op jit(solution)/shard_map/all_to_all | solution.py:196
  99.7 14.5 %all_to_all.31.rows_ref = f32[8,32,512]{2,1,0:T(8,128)S(1)} all-to-all(f32[8,32,512]{2,1,0:T(8,128)S(1)} %get-tuple-element.11), channel_id=1, replica_groups={{0,64,128,192,256,320,384,448},{16,80,144,208,272,336,400,464},{32,96,1..., dimensions={0} | all-to-all | bytes 1048576 | tf_op jit(solution)/shard_map/all_to_all | solution.py:201
  114.2 5.2 %all-to-all-start.3 = ((f32[16,32,512]{2,1,0:T(8,128)}), f32[16,32,512]{2,1,0:T(8,128)S(1)}, u32[]{:S(2)}, u32[]{:S(2)}) async-start(f32[16,32,512]{2,1,0:T(8,128)} %copy-done.1), calls=%async_computation.3 | async-start | bytes 2097152 | tf_op jit(solution)/shard_map/all_to_all | solution.py:195
  119.4 1.2 shard_map.56
  120.6 14.3 %all-to-all-done.3.stat_ref = f32[16,32,512]{2,1,0:T(8,128)S(1)} async-done(((f32[16,32,512]{2,1,0:T(8,128)}), f32[16,32,512]{2,1,0:T(8,128)S(1)}, u32[]{:S(2)}, u32[]{:S(2)}) %all-to-all-start.3) | async-done | bytes 1048608 | tf_op jit(solution)/shard_map/all_to_all | solution.py:195
  134.9 3.7 %all-to-all-start.5 = ((f32[16,32,512]{2,1,0:T(8,128)}), f32[16,32,512]{2,1,0:T(8,128)S(1)}, u32[]{:S(2)}, u32[]{:S(2)}) async-start(f32[16,32,512]{2,1,0:T(8,128)} %shard_map.56), calls=%async_computation.5 | async-start | bytes 2097152 | tf_op jit(solution)/shard_map/all_to_all | solution.py:200
  138.6 0.1 broadcast_compare_fusion
  138.7 0.1 select_reduce_fusion.2
  138.8 0.1 copy.6
  138.9 0.1 slice_reduce_fusion
  139.0 0.0 copy-start.3
  139.0 0.6 shard_map.53
  139.6 23.4 %collective-permute-start.3 = (f32[2,32,512]{2,1,0:T(8,128)S(1)}, f32[2,32,512]{2,1,0:T(8,128)S(1)}, u32[]{:S(2)}, u32[]{:S(2)}) collective-permute-start(f32[2,32,512]{2,1,0:T(8,128)S(1)} %get-tuple-element.13), channel_id=1, source_target_pairs={{0,16},{16,0},{32,48},{48,32},{64,80},{80,64},{96,112},{112,96},{1... | collective-permute-start | bytes 393224 | tf_op jit(solution)/shard_map/ppermute | solution.py:164
  163.1 12.2 %collective-permute-start.4 = (f32[2,32,512]{2,1,0:T(8,128)S(1)}, f32[2,32,512]{2,1,0:T(8,128)S(1)}, u32[]{:S(2)}, u32[]{:S(2)}) collective-permute-start(f32[2,32,512]{2,1,0:T(8,128)S(1)} %get-tuple-element.14), channel_id=1, source_target_pairs={{0,32},{16,48},{32,0},{48,16},{64,96},{80,112},{96,64},{112,80},{1... | collective-permute-start | bytes 393224 | tf_op jit(solution)/shard_map/ppermute | solution.py:164
  175.3 1.9 collective-permute-start.5
  177.2 0.0 collective-permute-done.3.got1
  177.3 11.8 %collective-permute-done.4.got2 = f32[2,32,512]{2,1,0:T(8,128)S(1)} collective-permute-done((f32[2,32,512]{2,1,0:T(8,128)S(1)}, f32[2,32,512]{2,1,0:T(8,128)S(1)}, u32[]{:S(2)}, u32[]{:S(2)}) %collective-permute-start.4) | collective-permute-done | bytes 131104 | tf_op jit(solution)/shard_map/ppermute | solution.py:164
  189.1 3.8 %collective-permute-done.5.got3 = f32[2,32,512]{2,1,0:T(8,128)S(1)} collective-permute-done((f32[2,32,512]{2,1,0:T(8,128)S(1)}, f32[2,32,512]{2,1,0:T(8,128)S(1)}, u32[]{:S(2)}, u32[]{:S(2)}) %collective-permute-start.5) | collective-permute-done | bytes 131104 | tf_op jit(solution)/shard_map/ppermute | solution.py:164
  192.9 0.0 copy-done.3
  192.9 1.2 shard_map.54
  194.1 11.7 %shard_map.55.refs_1_ = bf16[16,32,512]{2,1,0:T(8,128)(2,1)S(1)} custom-call(s32[1]{0:T(128)} %bitcast.6.place_ref.refs_0_, f32[16,32,512]{2,1,0:T(8,128)S(1)} %all-to-all-done.3.stat_ref), custom_call_target="tpu_custom_call" | custom-call | flops 9663676416 | bytes 1572864 | tf_op jit(solution)/shard_map/pallas_call | solution.py:21
  205.8 0.0 all-to-all-done.5.refs_2_
  205.8 0.8 shard_map.57
  (8 shorter events, 0.1 us)
Async XLA Ops:
  0.6 15.1 %collective-permute-start.2 = (f32[2,32,512]{2,1,0:T(8,128)}, f32[2,32,512]{2,1,0:T(8,128)S(1)}, u32[]{:S(2)}, u32[]{:S(2)}) collective-permute-start(f32[2,32,512]{2,1,0:T(8,128)} %bitcast.8), channel_id=1, source_target_pairs={{0,48},{16,32},{32,16},{48,0},{64,112},{80,96},{96,80},{112,64},{1... | collective-permute-start | bytes 393224 | tf_op jit(solution)/shard_map/ppermute | solution.py:164
  6.0 10.4 %collective-permute-start.1 = (f32[2,32,512]{2,1,0:T(8,128)}, f32[2,32,512]{2,1,0:T(8,128)S(1)}, u32[]{:S(2)}, u32[]{:S(2)}) collective-permute-start(f32[2,32,512]{2,1,0:T(8,128)} %bitcast.9), channel_id=1, source_target_pairs={{0,32},{16,48},{32,0},{48,16},{64,96},{80,112},{96,64},{112,80},{1... | collective-permute-start | bytes 393224 | tf_op jit(solution)/shard_map/ppermute | solution.py:164
  12.7 3.7 %collective-permute-start = (f32[2,32,512]{2,1,0:T(8,128)}, f32[2,32,512]{2,1,0:T(8,128)S(1)}, u32[]{:S(2)}, u32[]{:S(2)}) collective-permute-start(f32[2,32,512]{2,1,0:T(8,128)} %bitcast.10), channel_id=1, source_target_pairs={{0,16},{16,0},{32,48},{48,32},{64,80},{80,64},{96,112},{112,96},{1... | collective-permute-start | bytes 393224 | tf_op jit(solution)/shard_map/ppermute | solution.py:164
  14.6 0.7 copy-start.5
  16.4 0.9 copy-start.2
  17.3 5.2 %copy-start.4 = (bf16[2,1,512,512]{3,2,1,0:T(8,128)(2,1)S(1)}, bf16[2,1,512,512]{3,2,1,0:T(8,128)(2,1)}, u32[]{:S(2)}) copy-start(bf16[2,1,512,512]{3,2,1,0:T(8,128)(2,1)} %param.3) | copy-start | bytes 3145732
  18.8 21.7 %all-to-all-start.1 = ((f32[8,32,512]{2,1,0:T(8,128)}), f32[8,32,512]{2,1,0:T(8,128)S(1)}, u32[]{:S(2)}, u32[]{:S(2)}) async-start(f32[8,32,512]{2,1,0:T(8,128)} %shard_map.51), calls=%async_computation.1 | async-start | bytes 1048576 | tf_op jit(solution)/shard_map/all_to_all | solution.py:185
  23.3 1.0 copy-start
  73.6 26.1 %all-to-all-start.4 = ((f32[16,32,512]{2,1,0:T(8,128)}), f32[16,32,512]{2,1,0:T(8,128)S(1)}, u32[]{:S(2)}, u32[]{:S(2)}) async-start(f32[16,32,512]{2,1,0:T(8,128)} %copy-done), calls=%async_computation.4 | async-start | bytes 2097152 | tf_op jit(solution)/shard_map/all_to_all | solution.py:196
  84.6 1.0 copy-start.1
  114.2 20.7 %all-to-all-start.3 = ((f32[16,32,512]{2,1,0:T(8,128)}), f32[16,32,512]{2,1,0:T(8,128)S(1)}, u32[]{:S(2)}, u32[]{:S(2)}) async-start(f32[16,32,512]{2,1,0:T(8,128)} %copy-done.1), calls=%async_computation.3 | async-start | bytes 2097152 | tf_op jit(solution)/shard_map/all_to_all | solution.py:195
  134.9 70.9 %all-to-all-start.5 = ((f32[16,32,512]{2,1,0:T(8,128)}), f32[16,32,512]{2,1,0:T(8,128)S(1)}, u32[]{:S(2)}, u32[]{:S(2)}) async-start(f32[16,32,512]{2,1,0:T(8,128)} %shard_map.56), calls=%async_computation.5 | async-start | bytes 2097152 | tf_op jit(solution)/shard_map/all_to_all | solution.py:200
  139.0 53.8 %copy-start.3 = (f32[1,2,32,512]{3,2,1,0:T(8,128)S(1)}, f32[1,2,32,512]{3,2,1,0:T(8,128)}, u32[]{:S(2)}) copy-start(f32[1,2,32,512]{3,2,1,0:T(8,128)} %param.5) | copy-start | bytes 393220
  139.6 37.6 %collective-permute-start.3 = (f32[2,32,512]{2,1,0:T(8,128)S(1)}, f32[2,32,512]{2,1,0:T(8,128)S(1)}, u32[]{:S(2)}, u32[]{:S(2)}) collective-permute-start(f32[2,32,512]{2,1,0:T(8,128)S(1)} %get-tuple-element.13), channel_id=1, source_target_pairs={{0,16},{16,0},{32,48},{48,32},{64,80},{80,64},{96,112},{112,96},{1... | collective-permute-start | bytes 393224 | tf_op jit(solution)/shard_map/ppermute | solution.py:164
  163.1 26.0 %collective-permute-start.4 = (f32[2,32,512]{2,1,0:T(8,128)S(1)}, f32[2,32,512]{2,1,0:T(8,128)S(1)}, u32[]{:S(2)}, u32[]{:S(2)}) collective-permute-start(f32[2,32,512]{2,1,0:T(8,128)S(1)} %get-tuple-element.14), channel_id=1, source_target_pairs={{0,32},{16,48},{32,0},{48,16},{64,96},{80,112},{96,64},{112,80},{1... | collective-permute-start | bytes 393224 | tf_op jit(solution)/shard_map/ppermute | solution.py:164
  175.3 17.5 %collective-permute-start.5 = (f32[2,32,512]{2,1,0:T(8,128)S(1)}, f32[2,32,512]{2,1,0:T(8,128)S(1)}, u32[]{:S(2)}, u32[]{:S(2)}) collective-permute-start(f32[2,32,512]{2,1,0:T(8,128)S(1)} %get-tuple-element.15), channel_id=1, source_target_pairs={{0,48},{16,32},{32,16},{48,0},{64,112},{80,96},{96,80},{112,64},{1... | collective-permute-start | bytes 393224 | tf_op jit(solution)/shard_map/ppermute | solution.py:164

commit v2 on v1

v2 whole, which is shorter than its diff:
```python
import jax
import jax.numpy as jnp
from jax import lax
from jax.experimental import pallas as pl
from jax.experimental.pallas import tpu as pltpu
from jax.sharding import PartitionSpec as P

ITERS = 4
DAMP = 0.05
GROUP = 4
f32 = jnp.float32
bf16 = jnp.bfloat16

VMEM = pl.BlockSpec(memory_space=pltpu.VMEM)
SMEM = pl.BlockSpec(memory_space=pltpu.SMEM)
PARAMS = pltpu.CompilerParams(vmem_limit_bytes=40 * 2**20)


def call(kernel, out_shape, in_specs, cost, *args):
    multiple = isinstance(out_shape, (list, tuple))
    return pl.pallas_call(
        kernel,
        out_shape=out_shape,
        in_specs=in_specs,
        out_specs=[VMEM] * len(out_shape) if multiple else VMEM,
        compiler_params=PARAMS,
        cost_estimate=pl.CostEstimate(flops=cost[0], bytes_accessed=cost[1], transcendentals=0),
    )(*args)


def gram_kernel(grads_ref, out_ref):
    shards, size, _ = grads_ref.shape
    parts = out_ref.shape[0]
    rows = size // parts
    gram = None
    total = None
    for s in range(shards):
        g = grads_ref[s]
        term = lax.dot_general(g, g, (((1,), (1,)), ((), ())), preferred_element_type=f32)
        gram = term if gram is None else gram + term
        wide = g.astype(f32)
        total = wide if total is None else total + wide
    out_ref[:, :rows, :] = gram.reshape(parts, rows, size)
    out_ref[:, rows:, :] = total.T.reshape(parts, rows, size)


def choose(k, options):
    value = options[0]
    for i in range(1, len(options)):
        value = jnp.where(k == i, options[i], value)
    return value


def spread_kernel(where_ref, held_ref, out0, out1, out2, out3):
    for k, out in enumerate((out0, out1, out2, out3)):
        out[...] = held_ref[where_ref[0, k], where_ref[1, k]]


def stat_kernel(sender_ref, sums_ref, state0, state1, state2, state3, wide_ref, owner_ref, total_ref):
    rows = state0.shape[0]
    sums = jnp.sum(sums_ref[...], axis=0)
    state = choose(sender_ref[0], [s[...] for s in (state0, state1, state2, state3)])
    stat = sums[:rows] + state
    wide_ref[...] = jnp.broadcast_to(stat[None], wide_ref.shape)
    owner_ref[0] = stat
    owner_ref[1] = stat
    total_ref[...] = sums[rows:]


def return_kernel(source_ref, rows_ref, out0, out1, out2, out3):
    for k, out in enumerate((out0, out1, out2, out3)):
        for j in range(out.shape[0]):
            out[j] = rows_ref[source_ref[k, j], 0]


def state_kernel(sender_ref, state_ref, got0, got1, got2, got3, out_ref):
    for j in range(out_ref.shape[0]):
        out_ref[j] = choose(
            sender_ref[j], [got0[j], got1[j], got2[j], got3[j], state_ref[j]]
        )


def split(a):
    high = a.astype(bf16)
    return high, (a - high.astype(f32)).astype(bf16)


def product(a, b):
    (a_high, a_low), (b_high, b_low) = a, b
    dot = lambda x, y: jnp.dot(x, y, preferred_element_type=f32)
    return dot(a_high, b_high) + (dot(a_high, b_low) + dot(a_low, b_high))


def newton_kernel(count, stat_ref, total_ref, out_ref):
    parts, rows, size = stat_ref.shape
    stat = stat_ref[...].reshape(size, size)
    row_ids = lax.broadcasted_iota(jnp.int32, (size, size), 0)
    col_ids = lax.broadcasted_iota(jnp.int32, (size, size), 1)
    eye = (row_ids == col_ids).astype(f32)
    norm = jnp.sqrt(jnp.sum(stat * stat))
    damped = stat + (DAMP * norm) * eye
    scale = jnp.sqrt(jnp.sum(damped * damped))
    iterate = damped / scale
    thin = (total_ref[...] / count).astype(bf16).astype(f32)
    for rounds in range(ITERS - 1):
        parts_of = split(iterate)
        thin = 1.25 * thin - 0.25 * product(split(thin), parts_of)
        if rounds + 2 < ITERS:
            square = product(parts_of, parts_of)
            factor2 = split(1.5625 * eye - 0.625 * iterate + 0.0625 * square)
            iterate = product(parts_of, split(product(factor2, factor2)))
    last = product(split(thin), parts_of)
    for _ in range(4):
        last = 1.25 * last - 0.25 * product(split(last), parts_of)
    thin = (1.25 * thin - 0.25 * last) * jnp.exp(-0.25 * jnp.log(scale))
    groups = out_ref.shape[2] // rows
    tall = thin.T.reshape(parts, groups, rows // groups, rows)
    out_ref[...] = jnp.concatenate([tall[:, i] for i in range(groups)], axis=2)


def update_kernel(got_ref, out_ref):
    _, rows, size = out_ref.shape
    parts, height, width = got_ref.shape
    groups = width // rows
    for i in range(groups):
        strip = jnp.concatenate([got_ref[r][:, i * rows : (i + 1) * rows] for r in range(parts)], axis=1)
        out_ref[0, i * height : (i + 1) * height, :] = strip.astype(bf16)


def body(grads, owner, state):
    local = grads[:, 0]
    shards, size, _ = local.shape
    held = state[0]
    capacity, rows, _ = held.shape
    reps = lax.axis_size("rep")
    blocks = owner.shape[0]
    groups = blocks // GROUP
    shape = lambda *s: jax.ShapeDtypeStruct(s, f32)
    y_groups = [[y * GROUP + q for y in range(groups)] for q in range(GROUP)]

    def across(x, k):
        return lax.ppermute(x, "pre", [(i, i ^ k) for i in range(blocks)])

    def over_y(x):
        return lax.all_gather(x, "pre", axis=0, axis_index_groups=y_groups)

    me = lax.axis_index("pre")
    my_y, my_q = me // GROUP, me % GROUP
    ids = jnp.arange(blocks, dtype=jnp.int32)
    slot = jnp.sum(
        ((owner[None, :] == owner[:, None]) & (ids[None, :] < ids[:, None])).astype(jnp.int32), axis=1
    )
    partners = my_y * GROUP + (jnp.arange(GROUP, dtype=jnp.int32) ^ my_q)
    at_partner = lambda v: jnp.sum(jnp.where(ids[None, :] == partners[:, None], v[None, :], 0), axis=1)
    wanted = at_partner(owner)
    where = jnp.stack([wanted // GROUP, at_partner(slot)]).astype(jnp.int32)
    state_sender = ((wanted[:1] % GROUP) ^ my_q).astype(jnp.int32)
    slots = jnp.arange(capacity, dtype=jnp.int32)
    block_of = jnp.max(
        jnp.where(
            (owner[None, None, :] == partners[:, None, None]) & (slot[None, None, :] == slots[None, :, None]),
            ids[None, None, :],
            -1,
        ),
        axis=2,
    )
    return_source = (jnp.maximum(block_of, 0) // GROUP).astype(jnp.int32)
    stat_sender = jnp.where(block_of[0] >= 0, (block_of[0] % GROUP) ^ my_q, GROUP).astype(jnp.int32)

    all_held = over_y(held)
    sums = call(
        gram_kernel,
        shape(reps, 2 * rows, size),
        [VMEM],
        (2 * shards * size**3, 4 * size * size * (shards + 2)),
        local,
    )
    sums = lax.all_to_all(sums, "rep", 0, 0, tiled=True)
    sent = call(
        spread_kernel,
        [shape(rows, size)] * GROUP,
        [SMEM, VMEM],
        (0, 4 * size * rows * 8),
        where,
        all_held,
    )
    got = [sent[0]] + [across(sent[k], k) for k in range(1, GROUP)]
    stat, outgoing, total = call(
        stat_kernel,
        [shape(reps, rows, size), shape(2, rows, size), shape(rows, size)],
        [SMEM] + [VMEM] * (GROUP + 1),
        (0, 4 * size * rows * 48),
        state_sender,
        sums,
        *got,
    )
    stat = lax.all_to_all(stat, "rep", 0, 0, tiled=True)
    outgoing = over_y(outgoing)
    count = shards * reps
    groups_of = 128 // rows
    columns = call(
        lambda *refs: newton_kernel(count, *refs),
        shape(reps, rows // groups_of, groups_of * rows),
        [VMEM, VMEM],
        (2 * 20 * size**3, 4 * size * size),
        stat,
        total,
    )
    columns = lax.all_to_all(columns, "rep", 0, 0, tiled=True)
    returned = call(
        return_kernel,
        [shape(capacity, rows, size)] * GROUP,
        [SMEM, VMEM],
        (0, 4 * size * rows * 16),
        return_source,
        outgoing,
    )
    returned = [returned[0]] + [across(returned[k], k) for k in range(1, GROUP)]
    new_state = call(
        state_kernel,
        shape(capacity, rows, size),
        [SMEM] + [VMEM] * (GROUP + 1),
        (0, 4 * size * rows * 12),
        stat_sender,
        held,
        *returned,
    )
    update = call(
        update_kernel,
        jax.ShapeDtypeStruct((1, rows, size), bf16),
        [VMEM],
        (0, 6 * rows * size),
        columns,
    )
    return (new_state[None], update)


def solution(mesh):
    placed = (P("rep", "pre", None, None), P(), P("pre", None, "rep", None))
    return jax.shard_map(
        body,
        mesh=mesh,
        in_specs=placed,
        out_specs=(P("pre", None, "rep", None), P("pre", "rep", None)),
        check_vma=False,
    )
```

time: 207 us -> 183 us (0.88)
  blocking collectives: 47.6 us -> 0 us
  waiting for transfers between devices: 60.9 us -> 91 us
  starting transfers between devices: 71.8 us -> 56.2 us
  between operations: 3.49 us -> 14.4 us
  Pallas kernels: 17.8 us -> 14.9 us
    all_gather x0 -> x2, waiting for transfers between devices: none -> 78.5 us  [over_y(): return lax.all_gather(x, 'pre', axis=0, axis_index_groups=y_groups)]
    all_to_all x2 -> x0, blocking collectives: 47.6 us -> none  [the longest x1 33.1 us: body(): gram = lax.all_to_all(gram, 'rep', 0, 0, tiled=True)]
    ppermute x6, starting transfers between devices: 51.5 us -> 24.2 us  [across(): return lax.ppermute(x, 'pre', [(i, i ^ k) for i in range(blocks)])]
    all_to_all x3 -> x2, waiting for transfers between devices: 30.2 us -> 7.66 us  [the longest x1 7.66 us: body(): columns = lax.all_to_all(columns, 'rep', 0, 0, tiled=True)]
    all_to_all x1, waiting for transfers between devices: 14.3 us -> 0.01 us  [body(): stat = lax.all_to_all(stat, 'rep', 0, 0, tiled=True)]
    ppermute x6, waiting for transfers between devices: 16.3 us -> 3.41 us  [across(): return lax.ppermute(x, 'pre', [(i, i ^ k) for i in range(blocks)])]
    all_to_all x3 -> x2, starting transfers between devices: 15 us -> 23.2 us  [the longest x1 13.6 us: body(): sums = lax.all_to_all(sums, 'rep', 0, 0, tiled=True)]
    all_to_all x1, starting transfers between devices: 5.22 us -> 8.72 us  [body(): stat = lax.all_to_all(stat, 'rep', 0, 0, tiled=True)]
  transfers between devices with their start and end apart: 10 -> 11, of which waited for: 6 -> 4; matrix products, arithmetic and copies ran while one was open for 1% -> 0% of each run, Pallas kernels for 8% -> 7%
where the time goes in v2:
time: 183 us; the launch traced here: 182 us
  waiting for transfers between devices  91 us (50%)
  starting transfers between devices  56.2 us (31%)
  Pallas kernels  14.9 us (8%)
  between operations  14.4 us (8%)
  local copies, waits for them, and re-layouts  5.2 us (3%)
    all_gather x2, waiting for transfers between devices, over_y(): return lax.all_gather(x, 'pre', axis=0, axis_index_groups=y_groups)  78.5 us
    ppermute x6, starting transfers between devices, across(): return lax.ppermute(x, 'pre', [(i, i ^ k) for i in range(blocks)])  24.2 us
    pallas_call x7, Pallas kernels, call(): pl.pallas_call(kernel, out_shape=out_shape, in_specs=in_specs, out_specs=...  14.9 us
    all_to_all x1, starting transfers between devices, body(): sums = lax.all_to_all(sums, 'rep', 0, 0, tiled=True)  13.6 us
    all_to_all x1, starting transfers between devices, body(): columns = lax.all_to_all(columns, 'rep', 0, 0, tiled=True)  9.63 us
    all_to_all x1, starting transfers between devices, body(): stat = lax.all_to_all(stat, 'rep', 0, 0, tiled=True)  8.72 us
    all_to_all x1, waiting for transfers between devices, body(): columns = lax.all_to_all(columns, 'rep', 0, 0, tiled=True)  7.66 us
    unnamed x12, local copies, waits for them, and re-layouts  5 us
  transfers between devices with their start and end apart: 11, of which 4 were waited for; matrix products, arithmetic and copies ran while one was open for 0% of the time, Pallas kernels for 7%

profile of v2, /device:TPU:1, one launch (start us, length us, event | category | flops | bytes accessed | tf_op | source)
XLA Modules:
  0.0 182.3 jit_solution(9331576003836159946)
XLA Ops:
  7.2 0.0 copy-start.1
  7.2 1.2 copy-done.1
  8.4 0.7 shard_map.50
  9.1 0.0 copy-start
  9.1 1.3 copy-done
  10.5 0.0 copy-start.5
  10.5 13.6 %all-to-all-start = ((f32[16,64,512]{2,1,0:T(8,128)}), f32[16,64,512]{2,1,0:T(8,128)S(1)}, u32[]{:S(2)}, u32[]{:S(2)}) async-start(f32[16,64,512]{2,1,0:T(8,128)} %copy-done), calls=%async_computation | async-start | bytes 4194304 | tf_op jit(solution)/shard_map/all_to_all | solution.py:178
  24.0 0.0 all-gather.4.cloned.1.call-start
  24.1 0.7 all-gather.4.cloned.1.call-update
  24.8 0.0 copy-done.5
  24.8 0.2 convert_reduce_fusion
  25.0 0.2 select_reduce_fusion.1
  25.2 40.4 %all-gather.4.cloned.1.call-done.held_ref = f32[8,2,32,512]{3,2,1,0:T(8,128)} async-done(((f32[1,2,32,512]{3,2,1,0:T(8,128)}), f32[8,2,32,512]{3,2,1,0:T(8,128)}) %all-gather.4.cloned.1.call-update) | async-done | bytes 1048592 | tf_op jit(solution)/shard_map/all_gather | solution.py:145
  65.6 0.0 copy-start.2
  65.6 1.2 copy-done.2
  66.8 0.6 shard_map.51
  67.4 6.7 %collective-permute-start = (f32[32,512]{1,0:T(8,128)S(1)}, f32[32,512]{1,0:T(8,128)S(1)}, u32[]{:S(2)}, u32[]{:S(2)}) collective-permute-start(f32[32,512]{1,0:T(8,128)S(1)} %get-tuple-element.14), channel_id=1, source_target_pairs={{0,16},{16,0},{32,48},{48,32},{64,80},{80,64},{96,112},{112,96},{1... | collective-permute-start | bytes 196616 | tf_op jit(solution)/shard_map/ppermute | solution.py:142
  74.1 3.1 %collective-permute-start.1 = (f32[32,512]{1,0:T(8,128)S(1)}, f32[32,512]{1,0:T(8,128)S(1)}, u32[]{:S(2)}, u32[]{:S(2)}) collective-permute-start(f32[32,512]{1,0:T(8,128)S(1)} %get-tuple-element.15), channel_id=1, source_target_pairs={{0,32},{16,48},{32,0},{48,16},{64,96},{80,112},{96,64},{112,80},{1... | collective-permute-start | bytes 196616 | tf_op jit(solution)/shard_map/ppermute | solution.py:142
  77.2 2.3 %collective-permute-start.2 = (f32[32,512]{1,0:T(8,128)S(1)}, f32[32,512]{1,0:T(8,128)S(1)}, u32[]{:S(2)}, u32[]{:S(2)}) collective-permute-start(f32[32,512]{1,0:T(8,128)S(1)} %get-tuple-element.16), channel_id=1, source_target_pairs={{0,48},{16,32},{32,16},{48,0},{64,112},{80,96},{96,80},{112,64},{1... | collective-permute-start | bytes 196616 | tf_op jit(solution)/shard_map/ppermute | solution.py:142
  79.7 0.0 collective-permute-done.state1
  79.7 0.0 collective-permute-done.1.state2
  79.7 3.4 %collective-permute-done.2.state3 = f32[32,512]{1,0:T(8,128)S(1)} collective-permute-done((f32[32,512]{1,0:T(8,128)S(1)}, f32[32,512]{1,0:T(8,128)S(1)}, u32[]{:S(2)}, u32[]{:S(2)}) %collective-permute-start.2) | collective-permute-done | bytes 65568 | tf_op jit(solution)/shard_map/ppermute | solution.py:142
  83.1 0.0 all-to-all-done.sums_ref
  83.1 1.2 shard_map.52
  84.3 8.7 %all-to-all-start.1 = ((f32[16,32,512]{2,1,0:T(8,128)}), f32[16,32,512]{2,1,0:T(8,128)S(1)}, u32[]{:S(2)}, u32[]{:S(2)}) async-start(f32[16,32,512]{2,1,0:T(8,128)} %get-tuple-element.22), calls=%async_computation.1 | async-start | bytes 2097152 | tf_op jit(solution)/shard_map/all_to_all | solution.py:197
  93.0 0.0 all-gather.6.cloned.1.call-start
  93.0 0.7 all-gather.6.cloned.1.call-update
  93.8 0.1 broadcast_compare_fusion
  93.8 0.1 select_reduce_fusion
  94.0 0.1 copy.6
  94.1 0.1 slice_reduce_fusion
  94.2 38.2 %all-gather.6.cloned.1.call-done = f32[16,32,512]{2,1,0:T(8,128)} async-done(((f32[2,32,512]{2,1,0:T(8,128)}), f32[16,32,512]{2,1,0:T(8,128)}) %all-gather.6.cloned.1.call-update) | async-done | bytes 1048592 | tf_op jit(solution)/shard_map/all_gather | solution.py:145
  132.3 0.0 copy-start.3
  132.3 1.2 copy-done.3
  133.6 0.6 shard_map.53
  134.2 6.6 %collective-permute-start.3 = (f32[2,32,512]{2,1,0:T(8,128)S(1)}, f32[2,32,512]{2,1,0:T(8,128)S(1)}, u32[]{:S(2)}, u32[]{:S(2)}) collective-permute-start(f32[2,32,512]{2,1,0:T(8,128)S(1)} %get-tuple-element.19), channel_id=1, source_target_pairs={{0,16},{16,0},{32,48},{48,32},{64,80},{80,64},{96,112},{112,96},{1... | collective-permute-start | bytes 393224 | tf_op jit(solution)/shard_map/ppermute | solution.py:142
  140.8 3.4 %collective-permute-start.4 = (f32[2,32,512]{2,1,0:T(8,128)S(1)}, f32[2,32,512]{2,1,0:T(8,128)S(1)}, u32[]{:S(2)}, u32[]{:S(2)}) collective-permute-start(f32[2,32,512]{2,1,0:T(8,128)S(1)} %get-tuple-element.20), channel_id=1, source_target_pairs={{0,32},{16,48},{32,0},{48,16},{64,96},{80,112},{96,64},{112,80},{1... | collective-permute-start | bytes 393224 | tf_op jit(solution)/shard_map/ppermute | solution.py:142
  144.2 2.0 %collective-permute-start.5 = (f32[2,32,512]{2,1,0:T(8,128)S(1)}, f32[2,32,512]{2,1,0:T(8,128)S(1)}, u32[]{:S(2)}, u32[]{:S(2)}) collective-permute-start(f32[2,32,512]{2,1,0:T(8,128)S(1)} %get-tuple-element.21), channel_id=1, source_target_pairs={{0,48},{16,32},{32,16},{48,0},{64,112},{80,96},{96,80},{112,64},{1... | collective-permute-start | bytes 393224 | tf_op jit(solution)/shard_map/ppermute | solution.py:142
  146.3 0.0 all-to-all-done.1.refs_0_
  146.3 0.0 copy-start.4
  146.3 9.9 %shard_map.55 = f32[16,8,128]{2,1,0:T(8,128)} custom-call(f32[16,32,512]{2,1,0:T(8,128)S(1)} %all-to-all-done.1.refs_0_, f32[32,512]{1,0:T(8,128)S(1)} %get-tuple-element.23.refs_1_), custom_call_target="tpu_custom_call" | custom-call | flops 5368709120 | bytes 1048576 | tf_op jit(solution)/shard_map/pallas_call | solution.py:21
  156.2 9.6 %all-to-all-start.2 = ((f32[16,8,128]{2,1,0:T(8,128)}), f32[16,8,128]{2,1,0:T(8,128)S(1)}, u32[]{:S(2)}, u32[]{:S(2)}) async-start(f32[16,8,128]{2,1,0:T(8,128)} %shard_map.55), calls=%async_computation.2 | async-start | bytes 131072 | tf_op jit(solution)/shard_map/all_to_all | solution.py:209
  165.8 0.0 collective-permute-done.3.got1
  165.8 0.0 collective-permute-done.4.got2
  165.8 0.0 collective-permute-done.5.got3
  165.9 0.0 copy-done.4
  165.9 1.2 shard_map.54
  167.1 7.7 %all-to-all-done.2.got_ref = f32[16,8,128]{2,1,0:T(8,128)S(1)} async-done(((f32[16,8,128]{2,1,0:T(8,128)}), f32[16,8,128]{2,1,0:T(8,128)S(1)}, u32[]{:S(2)}, u32[]{:S(2)}) %all-to-all-start.2) | async-done | bytes 65568 | tf_op jit(solution)/shard_map/all_to_all | solution.py:209
  174.7 0.7 shard_map.56
  (6 shorter events, 0.1 us)
Async XLA Ops:
  7.2 1.2 copy-start.1
  9.1 1.3 copy-start
  10.5 14.3 %copy-start.5 = (s32[32]{0:T(128)S(1)}, s32[32]{0:T(128)}, u32[]{:S(2)}) copy-start(s32[32]{0:T(128)} %param.4) | copy-start | bytes 388
  10.5 72.6 %all-to-all-start = ((f32[16,64,512]{2,1,0:T(8,128)}), f32[16,64,512]{2,1,0:T(8,128)S(1)}, u32[]{:S(2)}, u32[]{:S(2)}) async-start(f32[16,64,512]{2,1,0:T(8,128)} %copy-done), calls=%async_computation | async-start | bytes 4194304 | tf_op jit(solution)/shard_map/all_to_all | solution.py:178
  24.0 41.5 %all-gather.4.cloned.1.call-start = ((), (), s32[]{:S(2)}) async-start(), calls=%async_computation.3 | async-start | bytes 1179648 | tf_op jit(solution)/shard_map/all_gather | solution.py:145
  65.6 1.2 copy-start.2
  67.4 12.3 %collective-permute-start = (f32[32,512]{1,0:T(8,128)S(1)}, f32[32,512]{1,0:T(8,128)S(1)}, u32[]{:S(2)}, u32[]{:S(2)}) collective-permute-start(f32[32,512]{1,0:T(8,128)S(1)} %get-tuple-element.14), channel_id=1, source_target_pairs={{0,16},{16,0},{32,48},{48,32},{64,80},{80,64},{96,112},{112,96},{1... | collective-permute-start | bytes 196616 | tf_op jit(solution)/shard_map/ppermute | solution.py:142
  74.1 5.6 %collective-permute-start.1 = (f32[32,512]{1,0:T(8,128)S(1)}, f32[32,512]{1,0:T(8,128)S(1)}, u32[]{:S(2)}, u32[]{:S(2)}) collective-permute-start(f32[32,512]{1,0:T(8,128)S(1)} %get-tuple-element.15), channel_id=1, source_target_pairs={{0,32},{16,48},{32,0},{48,16},{64,96},{80,112},{96,64},{112,80},{1... | collective-permute-start | bytes 196616 | tf_op jit(solution)/shard_map/ppermute | solution.py:142
  77.2 5.9 %collective-permute-start.2 = (f32[32,512]{1,0:T(8,128)S(1)}, f32[32,512]{1,0:T(8,128)S(1)}, u32[]{:S(2)}, u32[]{:S(2)}) collective-permute-start(f32[32,512]{1,0:T(8,128)S(1)} %get-tuple-element.16), channel_id=1, source_target_pairs={{0,48},{16,32},{32,16},{48,0},{64,112},{80,96},{96,80},{112,64},{1... | collective-permute-start | bytes 196616 | tf_op jit(solution)/shard_map/ppermute | solution.py:142
  84.3 62.0 %all-to-all-start.1 = ((f32[16,32,512]{2,1,0:T(8,128)}), f32[16,32,512]{2,1,0:T(8,128)S(1)}, u32[]{:S(2)}, u32[]{:S(2)}) async-start(f32[16,32,512]{2,1,0:T(8,128)} %get-tuple-element.22), calls=%async_computation.1 | async-start | bytes 2097152 | tf_op jit(solution)/shard_map/all_to_all | solution.py:197
  93.0 39.3 %all-gather.6.cloned.1.call-start = ((), (), s32[]{:S(2)}) async-start(), calls=%async_computation.4 | async-start | bytes 1179648 | tf_op jit(solution)/shard_map/all_gather | solution.py:145
  132.3 1.2 copy-start.3
  134.2 31.6 %collective-permute-start.3 = (f32[2,32,512]{2,1,0:T(8,128)S(1)}, f32[2,32,512]{2,1,0:T(8,128)S(1)}, u32[]{:S(2)}, u32[]{:S(2)}) collective-permute-start(f32[2,32,512]{2,1,0:T(8,128)S(1)} %get-tuple-element.19), channel_id=1, source_target_pairs={{0,16},{16,0},{32,48},{48,32},{64,80},{80,64},{96,112},{112,96},{1... | collective-permute-start | bytes 393224 | tf_op jit(solution)/shard_map/ppermute | solution.py:142
  140.8 25.1 %collective-permute-start.4 = (f32[2,32,512]{2,1,0:T(8,128)S(1)}, f32[2,32,512]{2,1,0:T(8,128)S(1)}, u32[]{:S(2)}, u32[]{:S(2)}) collective-permute-start(f32[2,32,512]{2,1,0:T(8,128)S(1)} %get-tuple-element.20), channel_id=1, source_target_pairs={{0,32},{16,48},{32,0},{48,16},{64,96},{80,112},{96,64},{112,80},{1... | collective-permute-start | bytes 393224 | tf_op jit(solution)/shard_map/ppermute | solution.py:142
  144.2 21.6 %collective-permute-start.5 = (f32[2,32,512]{2,1,0:T(8,128)S(1)}, f32[2,32,512]{2,1,0:T(8,128)S(1)}, u32[]{:S(2)}, u32[]{:S(2)}) collective-permute-start(f32[2,32,512]{2,1,0:T(8,128)S(1)} %get-tuple-element.21), channel_id=1, source_target_pairs={{0,48},{16,32},{32,16},{48,0},{64,112},{80,96},{96,80},{112,64},{1... | collective-permute-start | bytes 393224 | tf_op jit(solution)/shard_map/ppermute | solution.py:142
  146.3 19.6 %copy-start.4 = (f32[1,2,32,512]{3,2,1,0:T(8,128)S(1)}, f32[1,2,32,512]{3,2,1,0:T(8,128)}, u32[]{:S(2)}) copy-start(f32[1,2,32,512]{3,2,1,0:T(8,128)} %param.5) | copy-start | bytes 393220
  156.2 18.6 %all-to-all-start.2 = ((f32[16,8,128]{2,1,0:T(8,128)}), f32[16,8,128]{2,1,0:T(8,128)S(1)}, u32[]{:S(2)}, u32[]{:S(2)}) async-start(f32[16,8,128]{2,1,0:T(8,128)} %shard_map.55), calls=%async_computation.2 | async-start | bytes 131072 | tf_op jit(solution)/shard_map/all_to_all | solution.py:209
Sparse Core Ops, SparseCore 0:
  26.9 38.5 all-gather.3
  96.5 35.7 all-gather.5

commit v3 on v2

v3 whole, which is shorter than its diff:
```python
import jax
import jax.numpy as jnp
from jax import lax
from jax.experimental import pallas as pl
from jax.experimental.pallas import tpu as pltpu
from jax.sharding import PartitionSpec as P

ITERS = 4
DAMP = 0.05
GROUP = 4
ACROSS = 4
f32 = jnp.float32
bf16 = jnp.bfloat16

VMEM = pl.BlockSpec(memory_space=pltpu.VMEM)
ANY = pl.BlockSpec(memory_space=pl.ANY)
SMEM = pl.BlockSpec(memory_space=pltpu.SMEM)
PARAMS = pltpu.CompilerParams(vmem_limit_bytes=40 * 2**20)


def call(kernel, out_shape, in_specs, cost, *args, scratch=()):
    multiple = isinstance(out_shape, (list, tuple))
    return pl.pallas_call(
        kernel,
        out_shape=out_shape,
        in_specs=in_specs,
        out_specs=[VMEM] * len(out_shape) if multiple else VMEM,
        scratch_shapes=list(scratch),
        compiler_params=PARAMS,
        cost_estimate=pl.CostEstimate(flops=cost[0], bytes_accessed=cost[1], transcendentals=0),
    )(*args)


def gram_kernel(grads_ref, out_ref):
    shards, size, _ = grads_ref.shape
    xs, zs, double, _ = out_ref.shape
    rows = double // 2
    gram = None
    total = None
    for s in range(shards):
        g = grads_ref[s]
        term = lax.dot_general(g, g, (((1,), (1,)), ((), ())), preferred_element_type=f32)
        gram = term if gram is None else gram + term
        wide = g.astype(f32)
        total = wide if total is None else total + wide
    gram = gram.reshape(zs, xs, rows, size)
    total = total.reshape(zs, xs, rows, size)
    for x in range(xs):
        out_ref[x, :, :rows, :] = gram[:, x]
        out_ref[x, :, rows:, :] = total[:, x]


def sum_kernel(parts_ref, after_ref, out_ref):
    del after_ref
    out_ref[...] = jnp.sum(parts_ref[...], axis=0)


def choose(k, options):
    value = options[0]
    for i in range(1, len(options)):
        value = jnp.where(k == i, options[i], value)
    return value


def spread_kernel(where_ref, *refs):
    held, outs = refs[:GROUP], refs[GROUP:]
    for y, out in enumerate(outs):
        j = where_ref[1, y]
        out[...] = choose(where_ref[0, y], [h[j] for h in held])


def stat_kernel(sender_ref, sums_ref, *refs):
    states, (wide_ref, gram_ref) = refs[:-2], refs[-2:]
    parts, _, _ = wide_ref.shape
    rows = gram_ref.shape[0]
    sums = jnp.sum(sums_ref[...], axis=0)
    gram_ref[...] = sums[:rows]
    stat = sums[:rows] + choose(sender_ref[0], [s[...] for s in states])
    both = jnp.concatenate([stat, sums[rows:]], axis=0)
    wide_ref[...] = jnp.broadcast_to(both[None], wide_ref.shape)


def return_kernel(source_ref, gram0, gram1, gram2, gram3, after_ref, out_ref):
    del after_ref
    grams = (gram0, gram1, gram2, gram3)
    ys, capacity, _, _ = out_ref.shape
    for y in range(ys):
        for j in range(capacity):
            out_ref[y, j] = choose(source_ref[y * capacity + j], [g[...] for g in grams])


def state_kernel(source_ref, state_ref, got_ref, after_ref, out_ref):
    del after_ref
    for j in range(out_ref.shape[0]):
        y = source_ref[j]
        gram = got_ref[jnp.maximum(y, 0), j]
        out_ref[j] = state_ref[j] + jnp.where(y >= 0, gram, 0.0)


def split(a):
    high = a.astype(bf16)
    return high, (a - high.astype(f32)).astype(bf16)


def product(a, b):
    (a_high, a_low), (b_high, b_low) = a, b
    dot = lambda x, y: jnp.dot(x, y, preferred_element_type=f32)
    return dot(a_high, b_high) + (dot(a_high, b_low) + dot(a_low, b_high))


def assemble(place, refs, whole_ref):
    for k, ref in enumerate(refs):
        x = (place + ACROSS - k) % ACROSS
        for z in range(ref.shape[0]):
            whole_ref[z * ACROSS + x] = ref[z]


def newton_kernel(place_ref, *refs):
    stat_refs, (out_ref, stat_ref) = refs[:ACROSS], refs[ACROSS:]
    parts, rows, size = stat_ref.shape
    place = place_ref[0]
    assemble(place, stat_refs, stat_ref)
    stat = stat_ref[...].reshape(size, size)
    row_ids = lax.broadcasted_iota(jnp.int32, (size, size), 0)
    col_ids = lax.broadcasted_iota(jnp.int32, (size, size), 1)
    eye = (row_ids == col_ids).astype(f32)
    thin_rows = lax.broadcasted_iota(jnp.int32, (rows, size), 0) + place * rows
    thin_cols = lax.broadcasted_iota(jnp.int32, (rows, size), 1)
    thin_eye = (thin_rows == thin_cols).astype(f32)
    norm = jnp.sqrt(jnp.sum(stat * stat))
    damped = stat + (DAMP * norm) * eye
    scale = jnp.sqrt(jnp.sum(damped * damped))
    iterate = damped / scale
    mine = (stat_ref[place] + (DAMP * norm) * thin_eye) / scale
    thin = 1.25 * thin_eye - 0.25 * mine
    parts_of = split(iterate)
    for _ in range(ITERS - 2):
        square = product(parts_of, parts_of)
        factor2 = split(1.5625 * eye - 0.625 * iterate + 0.0625 * square)
        iterate = product(parts_of, split(product(factor2, factor2)))
        parts_of = split(iterate)
        thin = 1.25 * thin - 0.25 * product(split(thin), parts_of)
    last = product(split(thin), parts_of)
    for _ in range(4):
        last = 1.25 * last - 0.25 * product(split(last), parts_of)
    thin = (1.25 * thin - 0.25 * last) * jnp.exp(-0.25 * jnp.log(scale))
    out_ref[...] = thin.astype(bf16)


def update_kernel(count, place_ref, root_ref, *refs):
    total_refs, (out_ref, total_ref) = refs[:ACROSS], refs[ACROSS:]
    _, _, size = total_ref.shape
    assemble(place_ref[0], total_refs, total_ref)
    mean = (total_ref[...].reshape(size, size) / count).astype(bf16)
    out_ref[0] = jnp.dot(root_ref[...], mean, preferred_element_type=f32).astype(bf16)


def body(grads, owner, state):
    local = grads[:, 0]
    shards, size, _ = local.shape
    held = state[0]
    capacity, rows, _ = held.shape
    reps = lax.axis_size("rep")
    blocks = owner.shape[0]
    groups = blocks // GROUP
    shape = lambda *s: jax.ShapeDtypeStruct(s, f32)

    def across(x, k):
        return lax.ppermute(x, "pre", [(i, i ^ k) for i in range(blocks)])

    def along_y(x, k):
        return lax.ppermute(x, "pre", [(i, (i + k * GROUP) % blocks) for i in range(blocks)])

    def along_x(x, k):
        return lax.ppermute(
            x, "rep", [(i, i // ACROSS * ACROSS + (i + k) % ACROSS) for i in range(reps)]
        )

    zs = reps // ACROSS
    y_groups = [[y * GROUP + q for y in range(groups)] for q in range(GROUP)]
    x_groups = [[z * ACROSS + x for x in range(ACROSS)] for z in range(zs)]
    z_groups = [[z * ACROSS + x for z in range(zs)] for x in range(ACROSS)]

    def exchange(x, which):
        return lax.all_to_all(x, "rep", 0, 0, tiled=True, axis_index_groups=which)

    me = lax.axis_index("pre")
    my_y, my_q = me // GROUP, me % GROUP
    place = lax.axis_index("rep").reshape(1).astype(jnp.int32)
    ids = jnp.arange(blocks, dtype=jnp.int32)
    slot = jnp.sum(
        ((owner[None, :] == owner[:, None]) & (ids[None, :] < ids[:, None])).astype(jnp.int32), axis=1
    )
    ahead = (me + GROUP * jnp.arange(groups, dtype=jnp.int32)) % blocks
    at_ahead = lambda v: jnp.sum(jnp.where(ids[None, :] == ahead[:, None], v[None, :], 0), axis=1)
    wanted = at_ahead(owner)
    where = jnp.stack([(wanted % GROUP) ^ my_q, at_ahead(slot)]).astype(jnp.int32)
    state_sender = ((my_y - wanted[:1] // GROUP) % groups).astype(jnp.int32)
    slots = jnp.arange(capacity, dtype=jnp.int32)
    plane = jnp.arange(groups, dtype=jnp.int32) * GROUP + my_q
    block_of = jnp.max(
        jnp.where(
            (owner[None, None, :] == plane[:, None, None]) & (slot[None, None, :] == slots[None, :, None]),
            ids[None, None, :],
            -1,
        ),
        axis=2,
    )
    return_source = ((block_of % GROUP) ^ my_q).reshape(-1).astype(jnp.int32)
    mine = jnp.max(jnp.where(plane[:, None] == me, block_of, -1), axis=0)
    stat_source = jnp.where(mine >= 0, mine // GROUP, -1).astype(jnp.int32)

    held_z = across(held, 2)
    sums = call(
        gram_kernel,
        shape(ACROSS, zs, 2 * rows, size),
        [VMEM],
        (2 * shards * size**3, 4 * size * size * (shards + 2)),
        local,
    )
    sums = exchange(sums, x_groups)
    sent = call(
        spread_kernel,
        [shape(rows, size)] * groups,
        [SMEM] + [VMEM] * GROUP,
        (0, 4 * size * rows * 16),
        where,
        held,
        across(held, 1),
        held_z,
        across(held_z, 1),
    )
    sums = call(
        sum_kernel,
        shape(zs, 2 * rows, size),
        [VMEM, ANY],
        (0, 4 * size * rows * 40),
        sums,
        sent[0],
    )
    sums = exchange(sums, z_groups)
    got = [sent[0]] + [along_y(sent[k], k) for k in range(1, groups)]
    both, gram = call(
        stat_kernel,
        [shape(zs, 2 * rows, size), shape(rows, size)],
        [SMEM] + [VMEM] * (groups + 1),
        (0, 4 * size * rows * 25),
        state_sender,
        sums,
        *got,
    )
    both = exchange(both, z_groups)
    stat, total = both[:, :rows], both[:, rows:]
    stats = [stat] + [along_x(stat, k) for k in range(1, ACROSS)]
    totals = [total] + [along_x(total, k) for k in range(1, ACROSS)]
    returned = call(
        return_kernel,
        shape(groups, capacity, rows, size),
        [SMEM] + [VMEM] * GROUP + [ANY],
        (0, 4 * size * rows * 20),
        return_source,
        gram,
        *[across(gram, k) for k in range(1, GROUP)],
        both,
    )
    returned = lax.all_to_all(returned, "pre", 0, 0, tiled=True, axis_index_groups=y_groups)
    count = shards * reps
    root = call(
        newton_kernel,
        jax.ShapeDtypeStruct((rows, size), bf16),
        [SMEM] + [VMEM] * ACROSS,
        (2 * 20 * size**3, 4 * size * size),
        place,
        *stats,
        scratch=[pltpu.VMEM((reps, rows, size), f32)],
    )
    update = call(
        lambda *refs: update_kernel(count, *refs),
        jax.ShapeDtypeStruct((1, rows, size), bf16),
        [SMEM] + [VMEM] * (ACROSS + 1),
        (2 * rows * size * size, 4 * size * size),
        place,
        root,
        *totals,
        scratch=[pltpu.VMEM((reps, rows, size), f32)],
    )
    new_state = call(
        state_kernel,
        shape(capacity, rows, size),
        [SMEM, VMEM, VMEM, ANY],
        (0, 4 * size * rows * 8),
        stat_source,
        held,
        returned,
        root,
    )
    return (new_state[None], update)


def solution(mesh):
    placed = (P("rep", "pre", None, None), P(), P("pre", None, "rep", None))
    return jax.shard_map(
        body,
        mesh=mesh,
        in_specs=placed,
        out_specs=(P("pre", None, "rep", None), P("pre", "rep", None)),
        check_vma=False,
    )
```

time: 183 us -> 142 us (0.78)
  the two profiles are of different devices: /device:TPU:1 before, /device:TPU:14 now
where the time goes in v3:
time: 142 us; the launch traced here: 141 us
  starting transfers between devices  92.9 us (65%)
  waiting for transfers between devices  27.6 us (19%)
  Pallas kernels  15.7 us (11%)
  local copies, waits for them, and re-layouts  2.76 us (2%)
    ppermute x7, starting transfers between devices, along_y(): lax.ppermute(x, 'pre', [(i, (i + k * GROUP) % blocks) for i in range(bloc...  29.5 us
    all_to_all x3, starting transfers between devices, exchange(): return lax.all_to_all(x, 'rep', 0, 0, tiled=True, axis_index_groups=which)  22.4 us
    ppermute x6, starting transfers between devices, along_x(): lax.ppermute(x, 'rep', [(i, i // ACROSS * ACROSS + (i + k) % ACROSS) for...  19.1 us
    pallas_call x8, Pallas kernels, call(): pl.pallas_call(kernel, out_shape=out_shape, in_specs=in_specs, out_specs=...  15.7 us
    ppermute x6, starting transfers between devices, across(): return lax.ppermute(x, 'pre', [(i, i ^ k) for i in range(blocks)])  15.7 us
    all_to_all x3, waiting for transfers between devices, exchange(): return lax.all_to_all(x, 'rep', 0, 0, tiled=True, axis_index_groups=which)  11.2 us
    ppermute x6, waiting for transfers between devices, across(): return lax.ppermute(x, 'pre', [(i, i ^ k) for i in range(blocks)])  9.91 us
    all_to_all x1, starting transfers between devices, body(): lax.all_to_all(returned, 'pre', 0, 0, tiled=True, axis_index_groups=y_gro...  6.26 us
  transfers between devices with their start and end apart: 23, of which 7 were waited for; matrix products, arithmetic and copies ran while one was open for 1% of the time, Pallas kernels for 7%

profile of v3, /device:TPU:14, one launch (start us, length us, event | category | flops | bytes accessed | tf_op | source)
XLA Modules:
  0.0 140.9 jit_solution(14003062060412666341)
XLA Ops:
  0.6 0.0 copy-start.1
  0.6 1.2 copy-done.1
  1.9 0.7 shard_map.50
  2.6 1.3 copy-done
  3.9 4.9 %all-to-all-start = ((f32[4,4,64,512]{3,2,1,0:T(8,128)}), f32[4,4,64,512]{3,2,1,0:T(8,128)S(1)}, u32[]{:S(2)}, u32[]{:S(2)}) async-start(f32[4,4,64,512]{3,2,1,0:T(8,128)} %copy-done), calls=%async_computation | async-start | bytes 4194304 | tf_op jit(solution)/shard_map/all_to_all | solution.py:185
  8.8 1.9 %collective-permute-start = (f32[2,32,512]{2,1,0:T(8,128)S(1)}, f32[2,32,512]{2,1,0:T(8,128)S(1)}, u32[]{:S(2)}, u32[]{:S(2)}) collective-permute-start(f32[2,32,512]{2,1,0:T(8,128)S(1)} %bitcast.10), channel_id=1, source_target_pairs={{0,16},{16,0},{32,48},{48,32},{64,80},{80,64},{96,112},{112,96},{1... | collective-permute-start | bytes 393224 | tf_op jit(solution)/shard_map/ppermute | solution.py:169
  10.8 4.3 %collective-permute-start.1 = (f32[2,32,512]{2,1,0:T(8,128)S(1)}, f32[2,32,512]{2,1,0:T(8,128)S(1)}, u32[]{:S(2)}, u32[]{:S(2)}) collective-permute-start(f32[2,32,512]{2,1,0:T(8,128)S(1)} %bitcast.11), channel_id=1, source_target_pairs={{0,32},{16,48},{32,0},{48,16},{64,96},{80,112},{96,64},{112,80},{1... | collective-permute-start | bytes 393224 | tf_op jit(solution)/shard_map/ppermute | solution.py:169
  15.1 0.2 convert_reduce_fusion
  15.3 0.2 select_reduce_fusion.1
  15.5 3.7 %collective-permute-done.1.refs_2_ = f32[2,32,512]{2,1,0:T(8,128)S(1)} collective-permute-done((f32[2,32,512]{2,1,0:T(8,128)S(1)}, f32[2,32,512]{2,1,0:T(8,128)S(1)}, u32[]{:S(2)}, u32[]{:S(2)}) %collective-permute-start.1) | collective-permute-done | bytes 131104 | tf_op jit(solution)/shard_map/ppermute | solution.py:169
  19.2 1.9 %collective-permute-start.2 = (f32[2,32,512]{2,1,0:T(8,128)S(1)}, f32[2,32,512]{2,1,0:T(8,128)S(1)}, u32[]{:S(2)}, u32[]{:S(2)}) collective-permute-start(f32[2,32,512]{2,1,0:T(8,128)S(1)} %collective-permute-done.1.refs_2_), channel_id=1, source_target_pairs={{0,16},{16,0},{32,48},{48,32},{64,80},{80,64},{96,112},{112,96},{1... | collective-permute-start | bytes 393224 | tf_op jit(solution)/shard_map/ppermute | solution.py:169
  21.1 0.0 collective-permute-done.refs_1_
  21.2 1.3 collective-permute-done.2.refs_3_
  22.4 0.6 shard_map.51
  23.1 10.0 %all-to-all-done.parts_ref = f32[4,4,64,512]{3,2,1,0:T(8,128)S(1)} async-done(((f32[4,4,64,512]{3,2,1,0:T(8,128)}), f32[4,4,64,512]{3,2,1,0:T(8,128)S(1)}, u32[]{:S(2)}, u32[]{:S(2)}) %all-to-all-start) | async-done | bytes 2097184 | tf_op jit(solution)/shard_map/all_to_all | solution.py:185
  33.1 0.9 shard_map.52
  34.0 10.3 %all-to-all-start.1 = ((f32[4,64,512]{2,1,0:T(8,128)}), f32[4,64,512]{2,1,0:T(8,128)S(1)}, u32[]{:S(2)}, u32[]{:S(2)}) async-start(f32[4,64,512]{2,1,0:T(8,128)} %shard_map.52), calls=%async_computation.1 | async-start | bytes 1048576 | tf_op jit(solution)/shard_map/all_to_all | solution.py:185
  44.3 3.5 %collective-permute-start.3 = (f32[32,512]{1,0:T(8,128)S(1)}, f32[32,512]{1,0:T(8,128)S(1)}, u32[]{:S(2)}, u32[]{:S(2)}) collective-permute-start(f32[32,512]{1,0:T(8,128)S(1)} %get-tuple-element.13), channel_id=1, source_target_pairs={{0,64},{16,80},{32,96},{48,112},{64,128},{80,144},{96,160},{112,17... | collective-permute-start | bytes 196616 | tf_op jit(solution)/shard_map/ppermute | solution.py:172
  47.8 5.7 %collective-permute-start.4 = (f32[32,512]{1,0:T(8,128)S(1)}, f32[32,512]{1,0:T(8,128)S(1)}, u32[]{:S(2)}, u32[]{:S(2)}) collective-permute-start(f32[32,512]{1,0:T(8,128)S(1)} %get-tuple-element.14), channel_id=1, source_target_pairs={{0,128},{16,144},{32,160},{48,176},{64,192},{80,208},{96,224},{112... | collective-permute-start | bytes 196616 | tf_op jit(solution)/shard_map/ppermute | solution.py:172
  53.5 2.8 %collective-permute-start.5 = (f32[32,512]{1,0:T(8,128)S(1)}, f32[32,512]{1,0:T(8,128)S(1)}, u32[]{:S(2)}, u32[]{:S(2)}) collective-permute-start(f32[32,512]{1,0:T(8,128)S(1)} %get-tuple-element.15), channel_id=1, source_target_pairs={{0,192},{16,208},{32,224},{48,240},{64,256},{80,272},{96,288},{112... | collective-permute-start | bytes 196616 | tf_op jit(solution)/shard_map/ppermute | solution.py:172
  56.3 4.7 %collective-permute-start.6 = (f32[32,512]{1,0:T(8,128)S(1)}, f32[32,512]{1,0:T(8,128)S(1)}, u32[]{:S(2)}, u32[]{:S(2)}) collective-permute-start(f32[32,512]{1,0:T(8,128)S(1)} %get-tuple-element.16), channel_id=1, source_target_pairs={{0,256},{16,272},{32,288},{48,304},{64,320},{80,336},{96,352},{112... | collective-permute-start | bytes 196616 | tf_op jit(solution)/shard_map/ppermute | solution.py:172
  61.0 3.6 %collective-permute-start.7 = (f32[32,512]{1,0:T(8,128)S(1)}, f32[32,512]{1,0:T(8,128)S(1)}, u32[]{:S(2)}, u32[]{:S(2)}) collective-permute-start(f32[32,512]{1,0:T(8,128)S(1)} %get-tuple-element.17), channel_id=1, source_target_pairs={{0,320},{16,336},{32,352},{48,368},{64,384},{80,400},{96,416},{112... | collective-permute-start | bytes 196616 | tf_op jit(solution)/shard_map/ppermute | solution.py:172
  64.6 0.0 collective-permute-done.3.refs_1_
  64.6 4.7 %collective-permute-start.8 = (f32[32,512]{1,0:T(8,128)S(1)}, f32[32,512]{1,0:T(8,128)S(1)}, u32[]{:S(2)}, u32[]{:S(2)}) collective-permute-start(f32[32,512]{1,0:T(8,128)S(1)} %get-tuple-element.18), channel_id=1, source_target_pairs={{0,384},{16,400},{32,416},{48,432},{64,448},{80,464},{96,480},{112... | collective-permute-start | bytes 196616 | tf_op jit(solution)/shard_map/ppermute | solution.py:172
  69.4 0.0 collective-permute-done.4.refs_2_
  69.4 4.5 %collective-permute-start.9 = (f32[32,512]{1,0:T(8,128)S(1)}, f32[32,512]{1,0:T(8,128)S(1)}, u32[]{:S(2)}, u32[]{:S(2)}) collective-permute-start(f32[32,512]{1,0:T(8,128)S(1)} %get-tuple-element.19), channel_id=1, source_target_pairs={{0,448},{16,464},{32,480},{48,496},{64,0},{80,16},{96,32},{112,48}... | collective-permute-start | bytes 196616 | tf_op jit(solution)/shard_map/ppermute | solution.py:172
  74.0 0.0 collective-permute-done.5.refs_3_
  74.0 0.0 collective-permute-done.6.refs_4_
  74.0 0.0 collective-permute-done.7.refs_5_
  74.1 0.0 collective-permute-done.8.refs_6_
  74.1 1.7 %collective-permute-done.9.refs_7_ = f32[32,512]{1,0:T(8,128)S(1)} collective-permute-done((f32[32,512]{1,0:T(8,128)S(1)}, f32[32,512]{1,0:T(8,128)S(1)}, u32[]{:S(2)}, u32[]{:S(2)}) %collective-permute-start.9) | collective-permute-done | bytes 65568 | tf_op jit(solution)/shard_map/ppermute | solution.py:172
  75.7 0.0 all-to-all-done.1.sums_ref
  75.7 0.9 shard_map.53
  76.6 7.2 %all-to-all-start.2 = ((f32[4,64,512]{2,1,0:T(8,128)}), f32[4,64,512]{2,1,0:T(8,128)S(1)}, u32[]{:S(2)}, u32[]{:S(2)}) async-start(f32[4,64,512]{2,1,0:T(8,128)} %get-tuple-element.21), calls=%async_computation.2 | async-start | bytes 1048576 | tf_op jit(solution)/shard_map/all_to_all | solution.py:185
  83.8 0.1 broadcast_compare_fusion
  83.9 0.1 select_reduce_fusion
  84.0 0.1 copy.5
  84.1 0.1 reduce_max.22
  84.2 1.9 %collective-permute-start.10 = (f32[32,512]{1,0:T(8,128)S(1)}, f32[32,512]{1,0:T(8,128)S(1)}, u32[]{:S(2)}, u32[]{:S(2)}) collective-permute-start(f32[32,512]{1,0:T(8,128)S(1)} %get-tuple-element.20.gram0), channel_id=1, source_target_pairs={{0,16},{16,0},{32,48},{48,32},{64,80},{80,64},{96,112},{112,96},{1... | collective-permute-start | bytes 196616 | tf_op jit(solution)/shard_map/ppermute | solution.py:169
  86.1 3.4 %collective-permute-start.11 = (f32[32,512]{1,0:T(8,128)S(1)}, f32[32,512]{1,0:T(8,128)S(1)}, u32[]{:S(2)}, u32[]{:S(2)}) collective-permute-start(f32[32,512]{1,0:T(8,128)S(1)} %get-tuple-element.20.gram0), channel_id=1, source_target_pairs={{0,32},{16,48},{32,0},{48,16},{64,96},{80,112},{96,64},{112,80},{1... | collective-permute-start | bytes 196616 | tf_op jit(solution)/shard_map/ppermute | solution.py:169
  89.5 2.3 %collective-permute-start.12 = (f32[32,512]{1,0:T(8,128)S(1)}, f32[32,512]{1,0:T(8,128)S(1)}, u32[]{:S(2)}, u32[]{:S(2)}) collective-permute-start(f32[32,512]{1,0:T(8,128)S(1)} %get-tuple-element.20.gram0), channel_id=1, source_target_pairs={{0,48},{16,32},{32,16},{48,0},{64,112},{80,96},{96,80},{112,64},{1... | collective-permute-start | bytes 196616 | tf_op jit(solution)/shard_map/ppermute | solution.py:169
  91.8 0.0 collective-permute-done.10.gram1
  91.8 4.9 %collective-permute-done.11.gram2 = f32[32,512]{1,0:T(8,128)S(1)} collective-permute-done((f32[32,512]{1,0:T(8,128)S(1)}, f32[32,512]{1,0:T(8,128)S(1)}, u32[]{:S(2)}, u32[]{:S(2)}) %collective-permute-start.11) | collective-permute-done | bytes 65568 | tf_op jit(solution)/shard_map/ppermute | solution.py:169
  96.7 0.0 collective-permute-done.12.gram3
  96.7 1.2 all-to-all-done.2.after_ref
  97.9 1.7 %shard_map.54 = f32[8,2,32,512]{3,2,1,0:T(8,128)} custom-call(s32[16]{0:T(128)S(1)} %fusion.1.source_ref, f32[32,512]{1,0:T(8,128)S(1)} %get-tuple-element.20.gram0, f32[32,512]{1,0:T(8,128)S(1)} %collective-permute-done.10.gram1, f32[32,512]{1,0:T(8,128)S(1)} %collective-permute-done.11.gram2, f32[32,512]{1,0:T(8,128)S(1)} %collective-permute-done.12.gram3, ...), custom_call_target="tpu_custom_call" | custom-call | bytes 1310720 | tf_op jit(solution)/shard_map/pallas_call | solution.py:23
  99.6 6.3 %all-to-all-start.3 = ((f32[8,2,32,512]{3,2,1,0:T(8,128)}), f32[8,2,32,512]{3,2,1,0:T(8,128)S(1)}, u32[]{:S(2)}, u32[]{:S(2)}) async-start(f32[8,2,32,512]{3,2,1,0:T(8,128)} %shard_map.54), calls=%async_computation.3 | async-start | bytes 2097152 | tf_op jit(solution)/shard_map/all_to_all | solution.py:266
  105.9 4.0 %collective-permute-start.13 = (f32[4,32,512]{2,1,0:T(8,128)S(1)}, f32[4,32,512]{2,1,0:T(8,128)S(1)}, u32[]{:S(2)}, u32[]{:S(2)}) collective-permute-start(f32[4,32,512]{2,1,0:T(8,128)S(1)} %get-tuple-element.25.refs_0_), channel_id=1, source_target_pairs={{0,1},{1,2},{2,3},{3,0},{4,5},{5,6},{6,7},{7,4},{8,9},{9,10},{10,1... | collective-permute-start | bytes 786440 | tf_op jit(solution)/shard_map/ppermute | solution.py:175
  109.9 1.9 %collective-permute-start.14 = (f32[4,32,512]{2,1,0:T(8,128)S(1)}, f32[4,32,512]{2,1,0:T(8,128)S(1)}, u32[]{:S(2)}, u32[]{:S(2)}) collective-permute-start(f32[4,32,512]{2,1,0:T(8,128)S(1)} %get-tuple-element.25.refs_0_), channel_id=1, source_target_pairs={{0,2},{1,3},{2,0},{3,1},{4,6},{5,7},{6,4},{7,5},{8,10},{9,11},{10,... | collective-permute-start | bytes 786440 | tf_op jit(solution)/shard_map/ppermute | solution.py:175
  111.8 3.3 %collective-permute-start.15 = (f32[4,32,512]{2,1,0:T(8,128)S(1)}, f32[4,32,512]{2,1,0:T(8,128)S(1)}, u32[]{:S(2)}, u32[]{:S(2)}) collective-permute-start(f32[4,32,512]{2,1,0:T(8,128)S(1)} %get-tuple-element.25.refs_0_), channel_id=1, source_target_pairs={{0,3},{1,0},{2,1},{3,2},{4,7},{5,4},{6,5},{7,6},{8,11},{9,8},{10,9... | collective-permute-start | bytes 786440 | tf_op jit(solution)/shard_map/ppermute | solution.py:175
  115.1 0.1 select_reduce_fusion.3
  115.3 3.7 %collective-permute-start.16 = (f32[4,32,512]{2,1,0:T(8,128)S(1)}, f32[4,32,512]{2,1,0:T(8,128)S(1)}, u32[]{:S(2)}, u32[]{:S(2)}) collective-permute-start(f32[4,32,512]{2,1,0:T(8,128)S(1)} %get-tuple-element.24.refs_2_), channel_id=1, source_target_pairs={{0,1},{1,2},{2,3},{3,0},{4,5},{5,6},{6,7},{7,4},{8,9},{9,10},{10,1... | collective-permute-start | bytes 786440 | tf_op jit(solution)/shard_map/ppermute | solution.py:175
  119.0 4.2 %collective-permute-start.17 = (f32[4,32,512]{2,1,0:T(8,128)S(1)}, f32[4,32,512]{2,1,0:T(8,128)S(1)}, u32[]{:S(2)}, u32[]{:S(2)}) collective-permute-start(f32[4,32,512]{2,1,0:T(8,128)S(1)} %get-tuple-element.24.refs_2_), channel_id=1, source_target_pairs={{0,2},{1,3},{2,0},{3,1},{4,6},{5,7},{6,4},{7,5},{8,10},{9,11},{10,... | collective-permute-start | bytes 786440 | tf_op jit(solution)/shard_map/ppermute | solution.py:175
  123.2 0.0 collective-permute-done.13.refs_1_
  123.2 1.9 %collective-permute-start.18 = (f32[4,32,512]{2,1,0:T(8,128)S(1)}, f32[4,32,512]{2,1,0:T(8,128)S(1)}, u32[]{:S(2)}, u32[]{:S(2)}) collective-permute-start(f32[4,32,512]{2,1,0:T(8,128)S(1)} %get-tuple-element.24.refs_2_), channel_id=1, source_target_pairs={{0,3},{1,0},{2,1},{3,2},{4,7},{5,4},{6,5},{7,6},{8,11},{9,8},{10,9... | collective-permute-start | bytes 786440 | tf_op jit(solution)/shard_map/ppermute | solution.py:175
  125.2 0.0 collective-permute-done.14.refs_2_
  125.2 4.7 %collective-permute-done.15.refs_3_ = f32[4,32,512]{2,1,0:T(8,128)S(1)} collective-permute-done((f32[4,32,512]{2,1,0:T(8,128)S(1)}, f32[4,32,512]{2,1,0:T(8,128)S(1)}, u32[]{:S(2)}, u32[]{:S(2)}) %collective-permute-start.15) | collective-permute-done | bytes 262176 | tf_op jit(solution)/shard_map/ppermute | solution.py:175
  129.9 8.8 %shard_map.55.after_ref.refs_1_ = bf16[32,512]{1,0:T(8,128)(2,1)S(1)} custom-call(s32[1]{0:T(128)} %bitcast.5.place_ref.refs_0_, f32[4,32,512]{2,1,0:T(8,128)S(1)} %get-tuple-element.25.refs_0_, f32[4,32,512]{2,1,0:T(8,128)S(1)} %collective-permute-done.13.refs_1_, f32[4,32,512]{2,1,0:T(8,128)S(1)} %collective-permute-done.14.refs_2_, ...), custom_call_target="tpu_custom_call" | custom-call | flops 5368709120 | bytes 1048576 | tf_op jit(solution)/shard_map/pallas_call | solution.py:23
  138.7 0.0 collective-permute-done.16.refs_3_
  138.7 0.0 collective-permute-done.17.refs_4_
  138.7 0.0 collective-permute-done.18.refs_5_
  138.8 0.9 shard_map.57
  139.6 0.0 all-to-all-done.3.got_ref
  139.7 1.2 shard_map.56
  (14 shorter events, 0.1 us)
Async XLA Ops:
  0.6 1.2 copy-start.1
  2.6 1.3 copy-start
  3.9 4.9 %copy-start.2 = (f32[1,2,32,512]{3,2,1,0:T(8,128)S(1)}, f32[1,2,32,512]{3,2,1,0:T(8,128)}, u32[]{:S(2)}) copy-start(f32[1,2,32,512]{3,2,1,0:T(8,128)} %param.5) | copy-start | bytes 393220
  3.9 11.1 %copy-start.3 = (s32[32]{0:T(128)S(1)}, s32[32]{0:T(128)}, u32[]{:S(2)}) copy-start(s32[32]{0:T(128)} %param.4) | copy-start | bytes 388
  3.9 29.2 %all-to-all-start = ((f32[4,4,64,512]{3,2,1,0:T(8,128)}), f32[4,4,64,512]{3,2,1,0:T(8,128)S(1)}, u32[]{:S(2)}, u32[]{:S(2)}) async-start(f32[4,4,64,512]{3,2,1,0:T(8,128)} %copy-done), calls=%async_computation | async-start | bytes 4194304 | tf_op jit(solution)/shard_map/all_to_all | solution.py:185
  8.8 12.3 %collective-permute-start = (f32[2,32,512]{2,1,0:T(8,128)S(1)}, f32[2,32,512]{2,1,0:T(8,128)S(1)}, u32[]{:S(2)}, u32[]{:S(2)}) collective-permute-start(f32[2,32,512]{2,1,0:T(8,128)S(1)} %bitcast.10), channel_id=1, source_target_pairs={{0,16},{16,0},{32,48},{48,32},{64,80},{80,64},{96,112},{112,96},{1... | collective-permute-start | bytes 393224 | tf_op jit(solution)/shard_map/ppermute | solution.py:169
  10.8 8.4 %collective-permute-start.1 = (f32[2,32,512]{2,1,0:T(8,128)S(1)}, f32[2,32,512]{2,1,0:T(8,128)S(1)}, u32[]{:S(2)}, u32[]{:S(2)}) collective-permute-start(f32[2,32,512]{2,1,0:T(8,128)S(1)} %bitcast.11), channel_id=1, source_target_pairs={{0,32},{16,48},{32,0},{48,16},{64,96},{80,112},{96,64},{112,80},{1... | collective-permute-start | bytes 393224 | tf_op jit(solution)/shard_map/ppermute | solution.py:169
  19.2 3.2 %collective-permute-start.2 = (f32[2,32,512]{2,1,0:T(8,128)S(1)}, f32[2,32,512]{2,1,0:T(8,128)S(1)}, u32[]{:S(2)}, u32[]{:S(2)}) collective-permute-start(f32[2,32,512]{2,1,0:T(8,128)S(1)} %collective-permute-done.1.refs_2_), channel_id=1, source_target_pairs={{0,16},{16,0},{32,48},{48,32},{64,80},{80,64},{96,112},{112,96},{1... | collective-permute-start | bytes 393224 | tf_op jit(solution)/shard_map/ppermute | solution.py:169
  34.0 41.7 %all-to-all-start.1 = ((f32[4,64,512]{2,1,0:T(8,128)}), f32[4,64,512]{2,1,0:T(8,128)S(1)}, u32[]{:S(2)}, u32[]{:S(2)}) async-start(f32[4,64,512]{2,1,0:T(8,128)} %shard_map.52), calls=%async_computation.1 | async-start | bytes 1048576 | tf_op jit(solution)/shard_map/all_to_all | solution.py:185
  44.3 20.3 %collective-permute-start.3 = (f32[32,512]{1,0:T(8,128)S(1)}, f32[32,512]{1,0:T(8,128)S(1)}, u32[]{:S(2)}, u32[]{:S(2)}) collective-permute-start(f32[32,512]{1,0:T(8,128)S(1)} %get-tuple-element.13), channel_id=1, source_target_pairs={{0,64},{16,80},{32,96},{48,112},{64,128},{80,144},{96,160},{112,17... | collective-permute-start | bytes 196616 | tf_op jit(solution)/shard_map/ppermute | solution.py:172
  47.8 21.6 %collective-permute-start.4 = (f32[32,512]{1,0:T(8,128)S(1)}, f32[32,512]{1,0:T(8,128)S(1)}, u32[]{:S(2)}, u32[]{:S(2)}) collective-permute-start(f32[32,512]{1,0:T(8,128)S(1)} %get-tuple-element.14), channel_id=1, source_target_pairs={{0,128},{16,144},{32,160},{48,176},{64,192},{80,208},{96,224},{112... | collective-permute-start | bytes 196616 | tf_op jit(solution)/shard_map/ppermute | solution.py:172
  53.5 20.5 %collective-permute-start.5 = (f32[32,512]{1,0:T(8,128)S(1)}, f32[32,512]{1,0:T(8,128)S(1)}, u32[]{:S(2)}, u32[]{:S(2)}) collective-permute-start(f32[32,512]{1,0:T(8,128)S(1)} %get-tuple-element.15), channel_id=1, source_target_pairs={{0,192},{16,208},{32,224},{48,240},{64,256},{80,272},{96,288},{112... | collective-permute-start | bytes 196616 | tf_op jit(solution)/shard_map/ppermute | solution.py:172
  56.3 17.7 %collective-permute-start.6 = (f32[32,512]{1,0:T(8,128)S(1)}, f32[32,512]{1,0:T(8,128)S(1)}, u32[]{:S(2)}, u32[]{:S(2)}) collective-permute-start(f32[32,512]{1,0:T(8,128)S(1)} %get-tuple-element.16), channel_id=1, source_target_pairs={{0,256},{16,272},{32,288},{48,304},{64,320},{80,336},{96,352},{112... | collective-permute-start | bytes 196616 | tf_op jit(solution)/shard_map/ppermute | solution.py:172
  61.0 13.0 %collective-permute-start.7 = (f32[32,512]{1,0:T(8,128)S(1)}, f32[32,512]{1,0:T(8,128)S(1)}, u32[]{:S(2)}, u32[]{:S(2)}) collective-permute-start(f32[32,512]{1,0:T(8,128)S(1)} %get-tuple-element.17), channel_id=1, source_target_pairs={{0,320},{16,336},{32,352},{48,368},{64,384},{80,400},{96,416},{112... | collective-permute-start | bytes 196616 | tf_op jit(solution)/shard_map/ppermute | solution.py:172
  64.6 9.4 %collective-permute-start.8 = (f32[32,512]{1,0:T(8,128)S(1)}, f32[32,512]{1,0:T(8,128)S(1)}, u32[]{:S(2)}, u32[]{:S(2)}) collective-permute-start(f32[32,512]{1,0:T(8,128)S(1)} %get-tuple-element.18), channel_id=1, source_target_pairs={{0,384},{16,400},{32,416},{48,432},{64,448},{80,464},{96,480},{112... | collective-permute-start | bytes 196616 | tf_op jit(solution)/shard_map/ppermute | solution.py:172
  69.4 6.4 %collective-permute-start.9 = (f32[32,512]{1,0:T(8,128)S(1)}, f32[32,512]{1,0:T(8,128)S(1)}, u32[]{:S(2)}, u32[]{:S(2)}) collective-permute-start(f32[32,512]{1,0:T(8,128)S(1)} %get-tuple-element.19), channel_id=1, source_target_pairs={{0,448},{16,464},{32,480},{48,496},{64,0},{80,16},{96,32},{112,48}... | collective-permute-start | bytes 196616 | tf_op jit(solution)/shard_map/ppermute | solution.py:172
  76.6 21.3 %all-to-all-start.2 = ((f32[4,64,512]{2,1,0:T(8,128)}), f32[4,64,512]{2,1,0:T(8,128)S(1)}, u32[]{:S(2)}, u32[]{:S(2)}) async-start(f32[4,64,512]{2,1,0:T(8,128)} %get-tuple-element.21), calls=%async_computation.2 | async-start | bytes 1048576 | tf_op jit(solution)/shard_map/all_to_all | solution.py:185
  84.2 7.6 %collective-permute-start.10 = (f32[32,512]{1,0:T(8,128)S(1)}, f32[32,512]{1,0:T(8,128)S(1)}, u32[]{:S(2)}, u32[]{:S(2)}) collective-permute-start(f32[32,512]{1,0:T(8,128)S(1)} %get-tuple-element.20.gram0), channel_id=1, source_target_pairs={{0,16},{16,0},{32,48},{48,32},{64,80},{80,64},{96,112},{112,96},{1... | collective-permute-start | bytes 196616 | tf_op jit(solution)/shard_map/ppermute | solution.py:169
  86.1 10.6 %collective-permute-start.11 = (f32[32,512]{1,0:T(8,128)S(1)}, f32[32,512]{1,0:T(8,128)S(1)}, u32[]{:S(2)}, u32[]{:S(2)}) collective-permute-start(f32[32,512]{1,0:T(8,128)S(1)} %get-tuple-element.20.gram0), channel_id=1, source_target_pairs={{0,32},{16,48},{32,0},{48,16},{64,96},{80,112},{96,64},{112,80},{1... | collective-permute-start | bytes 196616 | tf_op jit(solution)/shard_map/ppermute | solution.py:169
  89.5 7.2 %collective-permute-start.12 = (f32[32,512]{1,0:T(8,128)S(1)}, f32[32,512]{1,0:T(8,128)S(1)}, u32[]{:S(2)}, u32[]{:S(2)}) collective-permute-start(f32[32,512]{1,0:T(8,128)S(1)} %get-tuple-element.20.gram0), channel_id=1, source_target_pairs={{0,48},{16,32},{32,16},{48,0},{64,112},{80,96},{96,80},{112,64},{1... | collective-permute-start | bytes 196616 | tf_op jit(solution)/shard_map/ppermute | solution.py:169
  99.6 40.1 %all-to-all-start.3 = ((f32[8,2,32,512]{3,2,1,0:T(8,128)}), f32[8,2,32,512]{3,2,1,0:T(8,128)S(1)}, u32[]{:S(2)}, u32[]{:S(2)}) async-start(f32[8,2,32,512]{3,2,1,0:T(8,128)} %shard_map.54), calls=%async_computation.3 | async-start | bytes 2097152 | tf_op jit(solution)/shard_map/all_to_all | solution.py:266
  105.9 17.3 %collective-permute-start.13 = (f32[4,32,512]{2,1,0:T(8,128)S(1)}, f32[4,32,512]{2,1,0:T(8,128)S(1)}, u32[]{:S(2)}, u32[]{:S(2)}) collective-permute-start(f32[4,32,512]{2,1,0:T(8,128)S(1)} %get-tuple-element.25.refs_0_), channel_id=1, source_target_pairs={{0,1},{1,2},{2,3},{3,0},{4,5},{5,6},{6,7},{7,4},{8,9},{9,10},{10,1... | collective-permute-start | bytes 786440 | tf_op jit(solution)/shard_map/ppermute | solution.py:175
  109.9 15.3 %collective-permute-start.14 = (f32[4,32,512]{2,1,0:T(8,128)S(1)}, f32[4,32,512]{2,1,0:T(8,128)S(1)}, u32[]{:S(2)}, u32[]{:S(2)}) collective-permute-start(f32[4,32,512]{2,1,0:T(8,128)S(1)} %get-tuple-element.25.refs_0_), channel_id=1, source_target_pairs={{0,2},{1,3},{2,0},{3,1},{4,6},{5,7},{6,4},{7,5},{8,10},{9,11},{10,... | collective-permute-start | bytes 786440 | tf_op jit(solution)/shard_map/ppermute | solution.py:175
  111.8 18.1 %collective-permute-start.15 = (f32[4,32,512]{2,1,0:T(8,128)S(1)}, f32[4,32,512]{2,1,0:T(8,128)S(1)}, u32[]{:S(2)}, u32[]{:S(2)}) collective-permute-start(f32[4,32,512]{2,1,0:T(8,128)S(1)} %get-tuple-element.25.refs_0_), channel_id=1, source_target_pairs={{0,3},{1,0},{2,1},{3,2},{4,7},{5,4},{6,5},{7,6},{8,11},{9,8},{10,9... | collective-permute-start | bytes 786440 | tf_op jit(solution)/shard_map/ppermute | solution.py:175
  115.3 23.5 %collective-permute-start.16 = (f32[4,32,512]{2,1,0:T(8,128)S(1)}, f32[4,32,512]{2,1,0:T(8,128)S(1)}, u32[]{:S(2)}, u32[]{:S(2)}) collective-permute-start(f32[4,32,512]{2,1,0:T(8,128)S(1)} %get-tuple-element.24.refs_2_), channel_id=1, source_target_pairs={{0,1},{1,2},{2,3},{3,0},{4,5},{5,6},{6,7},{7,4},{8,9},{9,10},{10,1... | collective-permute-start | bytes 786440 | tf_op jit(solution)/shard_map/ppermute | solution.py:175
  119.0 19.7 %collective-permute-start.17 = (f32[4,32,512]{2,1,0:T(8,128)S(1)}, f32[4,32,512]{2,1,0:T(8,128)S(1)}, u32[]{:S(2)}, u32[]{:S(2)}) collective-permute-start(f32[4,32,512]{2,1,0:T(8,128)S(1)} %get-tuple-element.24.refs_2_), channel_id=1, source_target_pairs={{0,2},{1,3},{2,0},{3,1},{4,6},{5,7},{6,4},{7,5},{8,10},{9,11},{10,... | collective-permute-start | bytes 786440 | tf_op jit(solution)/shard_map/ppermute | solution.py:175
  123.2 15.5 %collective-permute-start.18 = (f32[4,32,512]{2,1,0:T(8,128)S(1)}, f32[4,32,512]{2,1,0:T(8,128)S(1)}, u32[]{:S(2)}, u32[]{:S(2)}) collective-permute-start(f32[4,32,512]{2,1,0:T(8,128)S(1)} %get-tuple-element.24.refs_2_), channel_id=1, source_target_pairs={{0,3},{1,0},{2,1},{3,2},{4,7},{5,4},{6,5},{7,6},{8,11},{9,8},{10,9... | collective-permute-start | bytes 786440 | tf_op jit(solution)/shard_map/ppermute | solution.py:175

commit v4 on v3

v4 whole, which is shorter than its diff:
```python
import functools

import jax
import jax.numpy as jnp
from jax import lax
from jax.experimental import pallas as pl
from jax.experimental.pallas import tpu as pltpu
from jax.sharding import PartitionSpec as P

ITERS = 4
DAMP = 0.05
GROUP = 4
LANES = 128
ENTRY = 3
RETURN = 8 * ENTRY
ACROSS = 4
f32 = jnp.float32
bf16 = jnp.bfloat16

VMEM = pl.BlockSpec(memory_space=pltpu.VMEM)
ANY = pl.BlockSpec(memory_space=pl.ANY)
HBM = pl.BlockSpec(memory_space=pltpu.HBM)
SMEM = pl.BlockSpec(memory_space=pltpu.SMEM)
PARAMS = pltpu.CompilerParams(vmem_limit_bytes=40 * 2**20)


def call(kernel, out_shape, in_specs, cost, *args, scratch=(), out_specs=VMEM):
    multiple = isinstance(out_shape, (list, tuple))
    return pl.pallas_call(
        kernel,
        out_shape=out_shape,
        in_specs=in_specs,
        out_specs=[out_specs] * len(out_shape) if multiple else out_specs,
        scratch_shapes=list(scratch),
        compiler_params=PARAMS,
        cost_estimate=pl.CostEstimate(flops=cost[0], bytes_accessed=cost[1], transcendentals=0),
    )(*args)


def gram_kernel(grads_ref, out_ref):
    shards, size, _ = grads_ref.shape
    xs, zs, double, _ = out_ref.shape
    rows = double // 2
    gram = None
    total = None
    for s in range(shards):
        g = grads_ref[s]
        term = lax.dot_general(g, g, (((1,), (1,)), ((), ())), preferred_element_type=f32)
        gram = term if gram is None else gram + term
        wide = g.astype(f32)
        total = wide if total is None else total + wide
    gram = gram.reshape(zs, xs, rows, size)
    total = total.reshape(zs, xs, rows, size)
    for x in range(xs):
        out_ref[x, :, :rows, :] = gram[:, x]
        out_ref[x, :, rows:, :] = total[:, x]


def sum_kernel(parts_ref, after_ref, out_ref):
    del after_ref
    out_ref[...] = jnp.sum(parts_ref[...], axis=0)


def choose(k, options):
    value = options[0]
    for i in range(1, len(options)):
        value = jnp.where(k == i, options[i], value)
    return value


def table_kernel(me_ref, owner_ref, out_ref, count_ref, slot_ref, block_ref):
    blocks = owner_ref.shape[0]
    me = me_ref[0]
    y, q = me >> 2, me & 3
    for b in range(blocks):
        count_ref[b] = 0
    for i in range(9):
        block_ref[i] = -1
    for b in range(blocks):
        o = owner_ref[b]
        s = jnp.minimum(count_ref[o], 1)
        count_ref[o] = s + 1
        slot_ref[b] = s
        near = o ^ me
        block_ref[jnp.where(near < 4, near * 2 + s, 8)] = b

    def put(i, block, line, last=False):
        o = owner_ref[block]
        d = ((o ^ me) >> 2) & 3
        which = jnp.where(d == 0, (((o ^ q) >> 1) & 1) + 2 * ((o ^ q) & 1), 3 + d)
        if last:
            which = jnp.where((o >> 4) == (me >> 4), which, 7)
        out_ref[i * ENTRY] = which
        out_ref[i * ENTRY + 1] = slot_ref[block]
        out_ref[i * ENTRY + 2] = line

    for n in range(1, 4):
        for t in range(2):
            put((n - 1) * 2 + t, (((y & 3) ^ n) + 4 * t) * GROUP + q, t)
    put(6, me ^ 16, (me >> 4) ^ 1)
    put(7, me, me >> 4, True)
    for i in range(8):
        block = block_ref[i]
        out_ref[RETURN + 4 * i] = ((block ^ me) >> 2) & 3
        out_ref[RETURN + 4 * i + 1] = ((block ^ me) >> 4) & 1
        out_ref[RETURN + 4 * i + 2] = (block ^ me) & 1
        out_ref[RETURN + 4 * i + 3] = jnp.where(block < 0, 0, 1 + (((block ^ me) >> 1) & 1))


def columns(place, rows, size):
    first = place * rows // LANES
    return [pl.multiple_of((first + n) % (size // LANES) * LANES, LANES) for n in range(size // LANES - 1)]


def keep_kernel(place_ref, held_ref, held_z_ref, kept_ref):
    capacity, rows, size = held_ref.shape
    for n, column in enumerate(columns(place_ref[0], rows, size)):
        for i, held in enumerate((held_ref, held_z_ref)):
            for j in range(capacity):
                kept_ref[i, j, :, n * LANES : (n + 1) * LANES] = held[j, :, pl.ds(column, LANES)]


def pick(table_ref, entry, kept_ref, core_ref, near=(), far=()):
    which, slot, line = (table_ref[entry * ENTRY + i] for i in range(ENTRY))
    options = [k[i, slot] for k in (kept_ref, core_ref) for i in range(2)]
    return choose(which, options + [g[line] for g in near] + [g[...] for g in far])


def near_kernel(table_ref, kept_ref, core_ref, *outs):
    for n, out in enumerate(outs):
        for t in range(2):
            out[t] = pick(table_ref, n * 2 + t, kept_ref, core_ref)


def far_kernel(table_ref, kept_ref, core_ref, near1, near2, near3, out_ref):
    out_ref[...] = pick(table_ref, 6, kept_ref, core_ref, (near1, near2, near3))


def stat_kernel(table_ref, place_ref, sums_ref, kept_ref, core_ref, *refs):
    wide_ref, gram_ref, both_ref = refs[4:]
    rows, size = gram_ref.shape
    sums = jnp.sum(sums_ref[...], axis=0)
    gram_ref[...] = sums[:rows]
    keep = size - LANES
    for n, column in enumerate(columns(place_ref[0], rows, size)):
        both_ref[:, n * LANES : (n + 1) * LANES] = gram_ref[:, pl.ds(column, LANES)]
    both_ref[:, :keep] += pick(table_ref, 7, kept_ref, core_ref, refs[:3], refs[3:4])
    both_ref[:, keep:] = sums[rows:]
    wide_ref[...] = jnp.broadcast_to(both_ref[...][None], wide_ref.shape)


def stack_kernel(*refs):
    for m, part in enumerate(refs[:-1]):
        refs[-1][m] = part[...]


def return_kernel(table_ref, *refs):
    lines, (own_ref, core_ref) = refs[:-2], refs[-2:]
    for i in range(8):
        n, line = table_ref[RETURN + 4 * i], table_ref[RETURN + 4 * i + 1]
        out_ref = core_ref if i // 2 % 2 else own_ref
        out_ref[i // 4, i % 2] = choose(n, [g[line] for g in lines])


def pass_kernel(table_ref, own_ref, core_ref, mine_ref, send_ref):
    for k, out in enumerate((mine_ref, send_ref)):
        for j in range(2):
            other = table_ref[RETURN + 4 * (4 * k + j) + 2]
            out[j] = jnp.where(other == 0, own_ref[k, j], core_ref[k, j])


def state_kernel(table_ref, state_ref, mine_ref, got_ref, after_ref, out_ref):
    del after_ref
    for j in range(2):
        way = table_ref[RETURN + 4 * j + 3]
        gram = jnp.where(way == 1, mine_ref[j], got_ref[j])
        out_ref[j] = state_ref[j] + jnp.where(way > 0, gram, 0.0)


def split(a):
    high = a.astype(bf16)
    return high, (a - high.astype(f32)).astype(bf16)


def product(a, b):
    (a_high, a_low), (b_high, b_low) = a, b
    dot = lambda x, y: jnp.dot(x, y, preferred_element_type=f32)
    return dot(a_high, b_high) + (dot(a_high, b_low) + dot(a_low, b_high))


def copies_kernel(part_ref, after_ref, out_ref, sems):
    del after_ref
    copies = [pltpu.make_async_copy(part_ref, out_ref.at[x], sems.at[x]) for x in range(out_ref.shape[0])]
    for copy in copies:
        copy.start()
    for copy in copies:
        copy.wait()


def newton_kernel(count, place_ref, all_ref, after_ref, out_ref, end_ref, stat_ref):
    del after_ref
    end_ref[...] = jnp.zeros_like(end_ref)
    xs, zs, rows, wide = all_ref.shape
    size = stat_ref.shape[1]
    blocks = size // LANES
    place = place_ref[0]
    for z in range(zs):
        for n in range(blocks - 1):
            j = (z + n) % blocks
            part = jnp.concatenate([all_ref[x, z, :, n * LANES : (n + 1) * LANES] for x in range(xs)], axis=0)
            stat_ref[z * LANES : (z + 1) * LANES, j * LANES : (j + 1) * LANES] = part
            if n == 1:
                stat_ref[j * LANES : (j + 1) * LANES, z * LANES : (z + 1) * LANES] = part.T
    stat = stat_ref[...]
    row_ids = lax.broadcasted_iota(jnp.int32, (size, size), 0)
    col_ids = lax.broadcasted_iota(jnp.int32, (size, size), 1)
    eye = (row_ids == col_ids).astype(f32)
    thin_rows = lax.broadcasted_iota(jnp.int32, (rows, size), 0) + place * rows
    thin_cols = lax.broadcasted_iota(jnp.int32, (rows, size), 1)
    thin_eye = (thin_rows == thin_cols).astype(f32)
    norm = jnp.sqrt(jnp.sum(stat * stat))
    damped = stat + (DAMP * norm) * eye
    scale = jnp.sqrt(jnp.sum(damped * damped))
    iterate = damped / scale
    mine = stat_ref[pl.ds(pl.multiple_of(place * rows, rows), rows), :]
    mine = (mine + (DAMP * norm) * thin_eye) / scale
    thin = 1.25 * thin_eye - 0.25 * mine
    parts_of = split(iterate)
    for _ in range(ITERS - 2):
        square = product(parts_of, parts_of)
        factor2 = split(1.5625 * eye - 0.625 * iterate + 0.0625 * square)
        iterate = product(parts_of, split(product(factor2, factor2)))
        parts_of = split(iterate)
        thin = 1.25 * thin - 0.25 * product(split(thin), parts_of)
    last = product(split(thin), parts_of)
    for _ in range(4):
        last = 1.25 * last - 0.25 * product(split(last), parts_of)
    thin = (1.25 * thin - 0.25 * last) * jnp.exp(-0.25 * jnp.log(scale))
    mean = jnp.concatenate([all_ref[x, z, :, size - LANES :] for z in range(zs) for x in range(xs)], axis=0)
    mean = (mean / count).astype(bf16)
    out_ref[0] = jnp.dot(thin.astype(bf16), mean, preferred_element_type=f32).astype(bf16)


def body(grads, owner, state):
    local = grads[:, 0]
    shards, size, _ = local.shape
    held = state[0]
    capacity, rows, _ = held.shape
    reps = lax.axis_size("rep")
    blocks = owner.shape[0]
    groups = blocks // GROUP
    shape = lambda *s: jax.ShapeDtypeStruct(s, f32)

    def across(x, k):
        return lax.ppermute(x, "pre", [(i, i ^ k) for i in range(blocks)])

    zs = reps // ACROSS
    x_groups = [[z * ACROSS + x for x in range(ACROSS)] for z in range(zs)]
    z_groups = [[z * ACROSS + x for z in range(zs)] for x in range(ACROSS)]

    def exchange(x, which):
        return lax.all_to_all(x, "rep", 0, 0, tiled=True, axis_index_groups=which)

    me = lax.axis_index("pre").reshape(1).astype(jnp.int32)
    place = lax.axis_index("rep").reshape(1).astype(jnp.int32)
    table = pl.pallas_call(
        table_kernel,
        out_shape=jax.ShapeDtypeStruct((RETURN + 32,), jnp.int32),
        in_specs=[SMEM, SMEM],
        out_specs=SMEM,
        scratch_shapes=[
            pltpu.SMEM((blocks,), jnp.int32),
            pltpu.SMEM((blocks,), jnp.int32),
            pltpu.SMEM((16,), jnp.int32),
        ],
    )(me, owner)

    held_z = across(held, 2)
    sums = call(
        gram_kernel,
        shape(ACROSS, zs, 2 * rows, size),
        [VMEM],
        (2 * shards * size**3, 4 * size * size * (shards + 2)),
        local,
    )
    sums = exchange(sums, x_groups)
    kept = call(
        keep_kernel,
        shape(2, capacity, rows, size - LANES),
        [SMEM, VMEM, VMEM],
        (0, 4 * size * rows * 8),
        place,
        held,
        held_z,
    )
    core = across(kept, 1)
    near = call(
        near_kernel,
        [shape(2, rows, size - LANES)] * 3,
        [SMEM, VMEM, VMEM],
        (0, 4 * size * rows * 12),
        table,
        kept,
        core,
    )
    near = [across(sent, GROUP * (n + 1)) for n, sent in enumerate(near)]
    far = call(
        far_kernel,
        shape(rows, size - LANES),
        [SMEM] + [VMEM] * 5,
        (0, 4 * size * rows * 12),
        table,
        kept,
        core,
        *near,
    )
    sums = call(
        sum_kernel,
        shape(zs, 2 * rows, size),
        [VMEM, ANY],
        (0, 4 * size * rows * 40),
        sums,
        far,
    )
    sums = exchange(sums, z_groups)
    far = across(far, 4 * GROUP)
    both, gram = call(
        stat_kernel,
        [shape(zs, rows, 2 * size - LANES), shape(rows, size)],
        [SMEM, SMEM] + [VMEM] * 7,
        (0, 4 * size * rows * 45),
        table,
        place,
        sums,
        kept,
        core,
        *near,
        far,
        scratch=[pltpu.VMEM((rows, 2 * size - LANES), f32)],
    )
    both = exchange(both, z_groups)
    line = call(
        stack_kernel,
        shape(2, rows, size),
        [VMEM] * 2,
        (0, 4 * size * rows * 4),
        gram,
        across(gram, 4 * GROUP),
    )
    lines = [line] + [across(line, GROUP * n) for n in range(1, 4)]
    both = call(
        copies_kernel,
        shape(ACROSS, zs, rows, 2 * size - LANES),
        [VMEM, ANY],
        (0, 4 * size * rows * 40),
        both,
        lines[1],
        out_specs=HBM,
        scratch=[pltpu.SemaphoreType.DMA((ACROSS,))],
    )
    both = exchange(both, x_groups)
    own, core = call(
        return_kernel,
        [shape(2, capacity, rows, size)] * 2,
        [SMEM] + [VMEM] * 4,
        (0, 4 * size * rows * 24),
        table,
        *lines,
    )
    mine, passed = call(
        pass_kernel,
        [shape(capacity, rows, size)] * 2,
        [SMEM, VMEM, VMEM],
        (0, 4 * size * rows * 12),
        table,
        own,
        across(core, 1),
    )
    count = shards * reps
    update, end = call(
        functools.partial(newton_kernel, count),
        [jax.ShapeDtypeStruct((1, rows, size), bf16), shape(8, LANES)],
        [SMEM, VMEM, ANY],
        (2 * 20 * size**3, 8 * size * size),
        place,
        both,
        passed,
        scratch=[pltpu.VMEM((size, size), f32)],
    )
    new_state = call(
        state_kernel,
        shape(capacity, rows, size),
        [SMEM, VMEM, VMEM, VMEM, ANY],
        (0, 4 * size * rows * 8),
        table,
        held,
        mine,
        across(passed, 2),
        end,
    )
    return (new_state[None], update)


def solution(mesh):
    placed = (P("rep", "pre", None, None), P(), P("pre", None, "rep", None))
    return jax.shard_map(
        body,
        mesh=mesh,
        in_specs=placed,
        out_specs=(P("pre", None, "rep", None), P("pre", "rep", None)),
        check_vma=False,
    )
```

time: 142 us -> 126 us (0.89)
  the two profiles are of different devices: /device:TPU:14 before, /device:TPU:1 now
where the time goes in v4:
time: 126 us; the launch traced here: 125 us
  starting transfers between devices  80.1 us (64%)
  waiting for transfers between devices  22 us (17%)
  Pallas kernels  19 us (15%)
  local copies, waits for them, and re-layouts  3.21 us (3%)
    ppermute x12, starting transfers between devices, across(): return lax.ppermute(x, 'pre', [(i, i ^ k) for i in range(blocks)])  57.5 us
    all_to_all x4, starting transfers between devices, exchange(): return lax.all_to_all(x, 'rep', 0, 0, tiled=True, axis_index_groups=which)  22.6 us
    ppermute x12, waiting for transfers between devices, across(): return lax.ppermute(x, 'pre', [(i, i ^ k) for i in range(blocks)])  19.8 us
    pallas_call x12, Pallas kernels, call(): pl.pallas_call(kernel, out_shape=out_shape, in_specs=in_specs, out_specs=...  17.5 us
    unnamed x10, local copies, waits for them, and re-layouts  3.21 us
  transfers between devices with their start and end apart: 16, of which 9 were waited for; matrix products, arithmetic and copies ran while one was open for 0% of the time, Pallas kernels for 11%

profile of v4, /device:TPU:1, one launch (start us, length us, event | category | flops | bytes accessed | tf_op | source)
XLA Modules:
  0.0 125.1 jit_solution(14915424753273167871)
XLA Ops:
  0.6 0.0 copy-start.1
  0.6 1.2 copy-done.1
  1.9 0.7 shard_map.51
  2.6 0.0 copy-start
  2.6 1.3 %copy-done = f32[4,4,64,512]{3,2,1,0:T(8,128)} copy-done((f32[4,4,64,512]{3,2,1,0:T(8,128)}, f32[4,4,64,512]{3,2,1,0:T(8,128)S(1)}, u32[]{:S(2)}) %copy-start) | copy-done | bytes 2097176
  3.9 0.0 copy-start.2
  3.9 5.0 %all-to-all-start = ((f32[4,4,64,512]{3,2,1,0:T(8,128)}), f32[4,4,64,512]{3,2,1,0:T(8,128)S(1)}, u32[]{:S(2)}, u32[]{:S(2)}) async-start(f32[4,4,64,512]{3,2,1,0:T(8,128)} %copy-done), calls=%async_computation | async-start | bytes 4194304 | tf_op jit(solution)/shard_map/all_to_all | solution.py:262
  8.9 0.0 copy-done.2
  8.9 4.0 %collective-permute-start = (f32[2,32,512]{2,1,0:T(8,128)S(1)}, f32[2,32,512]{2,1,0:T(8,128)S(1)}, u32[]{:S(2)}, u32[]{:S(2)}) collective-permute-start(f32[2,32,512]{2,1,0:T(8,128)S(1)} %bitcast.6), channel_id=1, source_target_pairs={{0,32},{16,48},{32,0},{48,16},{64,96},{80,112},{96,64},{112,80},{1... | collective-permute-start | bytes 393224 | tf_op jit(solution)/shard_map/ppermute | solution.py:255
  12.9 2.3 %collective-permute-done.held_z_ref = f32[2,32,512]{2,1,0:T(8,128)S(1)} collective-permute-done((f32[2,32,512]{2,1,0:T(8,128)S(1)}, f32[2,32,512]{2,1,0:T(8,128)S(1)}, u32[]{:S(2)}, u32[]{:S(2)}) %collective-permute-start) | collective-permute-done | bytes 131104 | tf_op jit(solution)/shard_map/ppermute | solution.py:255
  15.3 8.1 %collective-permute-start.1 = (f32[2,2,32,384]{3,2,1,0:T(8,128)S(1)}, f32[2,2,32,384]{3,2,1,0:T(8,128)S(1)}, u32[]{:S(2)}, u32[]{:S(2)}) collective-permute-start(f32[2,2,32,384]{3,2,1,0:T(8,128)S(1)} %shard_map.52.kept_ref), channel_id=1, source_target_pairs={{0,16},{16,0},{32,48},{48,32},{64,80},{80,64},{96,112},{112,96},{1... | collective-permute-start | bytes 589832 | tf_op jit(solution)/shard_map/ppermute | solution.py:255
  23.4 1.4 %shard_map.50.table_ref = s32[56]{0:T(128)} custom-call(s32[1]{0:T(128)} %bitcast.me_ref, s32[32]{0:T(128)} %owner_ref.1), custom_call_target="tpu_custom_call" | custom-call | tf_op jit(solution)/shard_map/pallas_call | solution.py:266
  24.8 0.0 collective-permute-done.1.core_ref
  24.8 0.0 copy-start.3
  24.9 0.6 copy-done.3
  25.5 0.6 shard_map.53
  26.1 1.9 %collective-permute-start.2 = (f32[2,32,384]{2,1,0:T(8,128)S(1)}, f32[2,32,384]{2,1,0:T(8,128)S(1)}, u32[]{:S(2)}, u32[]{:S(2)}) collective-permute-start(f32[2,32,384]{2,1,0:T(8,128)S(1)} %get-tuple-element.13), channel_id=1, source_target_pairs={{0,64},{16,80},{32,96},{48,112},{64,0},{80,16},{96,32},{112,48},{1... | collective-permute-start | bytes 294920 | tf_op jit(solution)/shard_map/ppermute | solution.py:255
  28.0 1.9 %collective-permute-start.3 = (f32[2,32,384]{2,1,0:T(8,128)S(1)}, f32[2,32,384]{2,1,0:T(8,128)S(1)}, u32[]{:S(2)}, u32[]{:S(2)}) collective-permute-start(f32[2,32,384]{2,1,0:T(8,128)S(1)} %get-tuple-element.14), channel_id=1, source_target_pairs={{0,128},{16,144},{32,160},{48,176},{64,192},{80,208},{96,224},{112... | collective-permute-start | bytes 294920 | tf_op jit(solution)/shard_map/ppermute | solution.py:255
  30.0 0.0 copy-start.4
  30.0 5.4 %collective-permute-start.4 = (f32[2,32,384]{2,1,0:T(8,128)S(1)}, f32[2,32,384]{2,1,0:T(8,128)S(1)}, u32[]{:S(2)}, u32[]{:S(2)}) collective-permute-start(f32[2,32,384]{2,1,0:T(8,128)S(1)} %get-tuple-element.15), channel_id=1, source_target_pairs={{0,192},{16,208},{32,224},{48,240},{64,128},{80,144},{96,160},{112... | collective-permute-start | bytes 294920 | tf_op jit(solution)/shard_map/ppermute | solution.py:255
  35.4 0.0 collective-permute-done.2.near1.refs_0_
  35.4 4.0 %collective-permute-done.3.near2.refs_1_ = f32[2,32,384]{2,1,0:T(8,128)S(1)} collective-permute-done((f32[2,32,384]{2,1,0:T(8,128)S(1)}, f32[2,32,384]{2,1,0:T(8,128)S(1)}, u32[]{:S(2)}, u32[]{:S(2)}) %collective-permute-start.3) | collective-permute-done | bytes 98336 | tf_op jit(solution)/shard_map/ppermute | solution.py:255
  39.5 0.0 collective-permute-done.4.near3.refs_2_
  39.5 0.6 shard_map.54.after_ref
  40.0 0.0 all-to-all-done.parts_ref
  40.0 0.9 shard_map.55
  40.9 7.0 %all-to-all-start.1 = ((f32[4,64,512]{2,1,0:T(8,128)}), f32[4,64,512]{2,1,0:T(8,128)S(1)}, u32[]{:S(2)}, u32[]{:S(2)}) async-start(f32[4,64,512]{2,1,0:T(8,128)} %shard_map.55), calls=%async_computation.1 | async-start | bytes 1048576 | tf_op jit(solution)/shard_map/all_to_all | solution.py:262
  47.9 5.8 %collective-permute-start.5 = (f32[32,384]{1,0:T(8,128)S(1)}, f32[32,384]{1,0:T(8,128)S(1)}, u32[]{:S(2)}, u32[]{:S(2)}) collective-permute-start(f32[32,384]{1,0:T(8,128)S(1)} %shard_map.54.after_ref), channel_id=1, source_target_pairs={{0,256},{16,272},{32,288},{48,304},{64,320},{80,336},{96,352},{112... | collective-permute-start | bytes 147464 | tf_op jit(solution)/shard_map/ppermute | solution.py:255
  53.8 2.9 %collective-permute-done.5.refs_3_ = f32[32,384]{1,0:T(8,128)S(1)} collective-permute-done((f32[32,384]{1,0:T(8,128)S(1)}, f32[32,384]{1,0:T(8,128)S(1)}, u32[]{:S(2)}, u32[]{:S(2)}) %collective-permute-start.5) | collective-permute-done | bytes 49184 | tf_op jit(solution)/shard_map/ppermute | solution.py:255
  56.7 2.3 %all-to-all-done.1.sums_ref = f32[4,64,512]{2,1,0:T(8,128)S(1)} async-done(((f32[4,64,512]{2,1,0:T(8,128)}), f32[4,64,512]{2,1,0:T(8,128)S(1)}, u32[]{:S(2)}, u32[]{:S(2)}) %all-to-all-start.1) | async-done | bytes 524320 | tf_op jit(solution)/shard_map/all_to_all | solution.py:262
  58.9 0.0 copy-done.4
  58.9 1.4 %shard_map.56 = (f32[4,32,896]{2,1,0:T(8,128)}, f32[32,512]{1,0:T(8,128)S(1)}) custom-call(s32[56]{0:T(128)S(1)} %copy-done.4, s32[1]{0:T(128)} %bitcast.2.place_ref, f32[4,64,512]{2,1,0:T(8,128)S(1)} %all-to-all-done.1.sums_ref, f32[2,2,32,384]{3,2,1,0:T(8,128)S(1)} %shard_map.52.kept_ref, f32[2,2,32,384]{3,2,1,0:T(8,128)S(1)} %collective-permute-done.1.core_ref, ...), custom_call_target="tpu_custom_call" | custom-call | bytes 2949120 | tf_op jit(solution)/shard_map/pallas_call | solution.py:29
  60.3 6.1 %all-to-all-start.2 = ((f32[4,32,896]{2,1,0:T(8,128)}), f32[4,32,896]{2,1,0:T(8,128)S(1)}, u32[]{:S(2)}, u32[]{:S(2)}) async-start(f32[4,32,896]{2,1,0:T(8,128)} %get-tuple-element.21), calls=%async_computation.2 | async-start | bytes 917504 | tf_op jit(solution)/shard_map/all_to_all | solution.py:262
  66.4 6.1 %collective-permute-start.6 = (f32[32,512]{1,0:T(8,128)S(1)}, f32[32,512]{1,0:T(8,128)S(1)}, u32[]{:S(2)}, u32[]{:S(2)}) collective-permute-start(f32[32,512]{1,0:T(8,128)S(1)} %get-tuple-element.16.refs_0_), channel_id=1, source_target_pairs={{0,256},{16,272},{32,288},{48,304},{64,320},{80,336},{96,352},{112... | collective-permute-start | bytes 196616 | tf_op jit(solution)/shard_map/ppermute | solution.py:255
  72.5 2.8 %collective-permute-done.6.refs_1_ = f32[32,512]{1,0:T(8,128)S(1)} collective-permute-done((f32[32,512]{1,0:T(8,128)S(1)}, f32[32,512]{1,0:T(8,128)S(1)}, u32[]{:S(2)}, u32[]{:S(2)}) %collective-permute-start.6) | collective-permute-done | bytes 65568 | tf_op jit(solution)/shard_map/ppermute | solution.py:255
  75.3 4.3 %collective-permute-start.7 = (f32[2,32,512]{2,1,0:T(8,128)S(1)}, f32[2,32,512]{2,1,0:T(8,128)S(1)}, u32[]{:S(2)}, u32[]{:S(2)}) collective-permute-start(f32[2,32,512]{2,1,0:T(8,128)S(1)} %shard_map.57.refs_0_), channel_id=1, source_target_pairs={{0,64},{16,80},{32,96},{48,112},{64,0},{80,16},{96,32},{112,48},{1... | collective-permute-start | bytes 393224 | tf_op jit(solution)/shard_map/ppermute | solution.py:255
  79.7 2.6 %collective-permute-done.7.refs_1_.after_ref = f32[2,32,512]{2,1,0:T(8,128)S(1)} collective-permute-done((f32[2,32,512]{2,1,0:T(8,128)S(1)}, f32[2,32,512]{2,1,0:T(8,128)S(1)}, u32[]{:S(2)}, u32[]{:S(2)}) %collective-permute-start.7) | collective-permute-done | bytes 131104 | tf_op jit(solution)/shard_map/ppermute | solution.py:255
  82.3 0.0 all-to-all-done.2.part_ref
  82.3 1.3 %shard_map.60 = f32[4,4,32,896]{3,2,1,0:T(8,128)} custom-call(f32[4,32,896]{2,1,0:T(8,128)S(1)} %all-to-all-done.2.part_ref, f32[2,32,512]{2,1,0:T(8,128)S(1)} %collective-permute-done.7.refs_1_.after_ref), custom_call_target="tpu_custom_call" | custom-call | bytes 2621440 | tf_op jit(solution)/shard_map/pallas_call | solution.py:29
  83.6 4.5 %all-to-all-start.3 = ((f32[4,4,32,896]{3,2,1,0:T(8,128)}), f32[4,4,32,896]{3,2,1,0:T(8,128)S(1)}, u32[]{:S(2)}, u32[]{:S(2)}) async-start(f32[4,4,32,896]{3,2,1,0:T(8,128)} %shard_map.60), calls=%async_computation.3 | async-start | bytes 3670016 | tf_op jit(solution)/shard_map/all_to_all | solution.py:262
  88.2 3.4 %collective-permute-start.8 = (f32[2,32,512]{2,1,0:T(8,128)S(1)}, f32[2,32,512]{2,1,0:T(8,128)S(1)}, u32[]{:S(2)}, u32[]{:S(2)}) collective-permute-start(f32[2,32,512]{2,1,0:T(8,128)S(1)} %shard_map.57.refs_0_), channel_id=1, source_target_pairs={{0,128},{16,144},{32,160},{48,176},{64,192},{80,208},{96,224},{112... | collective-permute-start | bytes 393224 | tf_op jit(solution)/shard_map/ppermute | solution.py:255
  91.6 3.6 %collective-permute-start.9 = (f32[2,32,512]{2,1,0:T(8,128)S(1)}, f32[2,32,512]{2,1,0:T(8,128)S(1)}, u32[]{:S(2)}, u32[]{:S(2)}) collective-permute-start(f32[2,32,512]{2,1,0:T(8,128)S(1)} %shard_map.57.refs_0_), channel_id=1, source_target_pairs={{0,192},{16,208},{32,224},{48,240},{64,128},{80,144},{96,160},{112... | collective-permute-start | bytes 393224 | tf_op jit(solution)/shard_map/ppermute | solution.py:255
  95.2 0.9 collective-permute-done.8.refs_2_
  96.2 3.0 %collective-permute-done.9.refs_3_ = f32[2,32,512]{2,1,0:T(8,128)S(1)} collective-permute-done((f32[2,32,512]{2,1,0:T(8,128)S(1)}, f32[2,32,512]{2,1,0:T(8,128)S(1)}, u32[]{:S(2)}, u32[]{:S(2)}) %collective-permute-start.9) | collective-permute-done | bytes 131104 | tf_op jit(solution)/shard_map/ppermute | solution.py:255
  99.1 0.6 shard_map.58
  99.8 9.0 %collective-permute-start.10 = (f32[2,2,32,512]{3,2,1,0:T(8,128)S(1)}, f32[2,2,32,512]{3,2,1,0:T(8,128)S(1)}, u32[]{:S(2)}, u32[]{:S(2)}) collective-permute-start(f32[2,2,32,512]{3,2,1,0:T(8,128)S(1)} %get-tuple-element.18), channel_id=1, source_target_pairs={{0,16},{16,0},{32,48},{48,32},{64,80},{80,64},{96,112},{112,96},{1... | collective-permute-start | bytes 786440 | tf_op jit(solution)/shard_map/ppermute | solution.py:255
  108.8 1.1 collective-permute-done.10.core_ref
  110.0 0.6 shard_map.59
  110.5 3.8 %collective-permute-start.11 = (f32[2,32,512]{2,1,0:T(8,128)S(1)}, f32[2,32,512]{2,1,0:T(8,128)S(1)}, u32[]{:S(2)}, u32[]{:S(2)}) collective-permute-start(f32[2,32,512]{2,1,0:T(8,128)S(1)} %get-tuple-element.20.after_ref), channel_id=1, source_target_pairs={{0,32},{16,48},{32,0},{48,16},{64,96},{80,112},{96,64},{112,80},{1... | collective-permute-start | bytes 393224 | tf_op jit(solution)/shard_map/ppermute | solution.py:255
  114.3 0.0 all-to-all-done.3.all_ref
  114.3 9.6 %shard_map.61 = (bf16[1,32,512]{2,1,0:T(8,128)(2,1)}, f32[8,128]{1,0:T(8,128)S(1)}) custom-call(s32[1]{0:T(128)} %bitcast.2.place_ref, f32[4,4,32,896]{3,2,1,0:T(8,128)S(1)} %all-to-all-done.3.all_ref, f32[2,32,512]{2,1,0:T(8,128)S(1)} %get-tuple-element.20.after_ref), custom_call_target="tpu_custom_call" | custom-call | flops 5368709120 | bytes 2097152 | tf_op jit(solution)/shard_map/pallas_call | solution.py:29
  123.9 0.0 collective-permute-done.11.got_ref
  123.9 1.2 shard_map.62
  (2 shorter events, 0.0 us)
Async XLA Ops:
  0.6 1.2 copy-start.1
  2.6 1.3 %copy-start = (f32[4,4,64,512]{3,2,1,0:T(8,128)}, f32[4,4,64,512]{3,2,1,0:T(8,128)S(1)}, u32[]{:S(2)}) copy-start(f32[4,4,64,512]{3,2,1,0:T(8,128)S(1)} %shard_map.51) | copy-start | bytes 6291460
  3.9 5.0 %copy-start.2 = (f32[1,2,32,512]{3,2,1,0:T(8,128)S(1)}, f32[1,2,32,512]{3,2,1,0:T(8,128)}, u32[]{:S(2)}) copy-start(f32[1,2,32,512]{3,2,1,0:T(8,128)} %param.5) | copy-start | bytes 393220
  3.9 36.1 %all-to-all-start = ((f32[4,4,64,512]{3,2,1,0:T(8,128)}), f32[4,4,64,512]{3,2,1,0:T(8,128)S(1)}, u32[]{:S(2)}, u32[]{:S(2)}) async-start(f32[4,4,64,512]{3,2,1,0:T(8,128)} %copy-done), calls=%async_computation | async-start | bytes 4194304 | tf_op jit(solution)/shard_map/all_to_all | solution.py:262
  8.9 6.3 %collective-permute-start = (f32[2,32,512]{2,1,0:T(8,128)S(1)}, f32[2,32,512]{2,1,0:T(8,128)S(1)}, u32[]{:S(2)}, u32[]{:S(2)}) collective-permute-start(f32[2,32,512]{2,1,0:T(8,128)S(1)} %bitcast.6), channel_id=1, source_target_pairs={{0,32},{16,48},{32,0},{48,16},{64,96},{80,112},{96,64},{112,80},{1... | collective-permute-start | bytes 393224 | tf_op jit(solution)/shard_map/ppermute | solution.py:255
  15.3 9.5 %collective-permute-start.1 = (f32[2,2,32,384]{3,2,1,0:T(8,128)S(1)}, f32[2,2,32,384]{3,2,1,0:T(8,128)S(1)}, u32[]{:S(2)}, u32[]{:S(2)}) collective-permute-start(f32[2,2,32,384]{3,2,1,0:T(8,128)S(1)} %shard_map.52.kept_ref), channel_id=1, source_target_pairs={{0,16},{16,0},{32,48},{48,32},{64,80},{80,64},{96,112},{112,96},{1... | collective-permute-start | bytes 589832 | tf_op jit(solution)/shard_map/ppermute | solution.py:255
  24.8 0.7 copy-start.3
  26.1 9.3 %collective-permute-start.2 = (f32[2,32,384]{2,1,0:T(8,128)S(1)}, f32[2,32,384]{2,1,0:T(8,128)S(1)}, u32[]{:S(2)}, u32[]{:S(2)}) collective-permute-start(f32[2,32,384]{2,1,0:T(8,128)S(1)} %get-tuple-element.13), channel_id=1, source_target_pairs={{0,64},{16,80},{32,96},{48,112},{64,0},{80,16},{96,32},{112,48},{1... | collective-permute-start | bytes 294920 | tf_op jit(solution)/shard_map/ppermute | solution.py:255
  28.0 11.4 %collective-permute-start.3 = (f32[2,32,384]{2,1,0:T(8,128)S(1)}, f32[2,32,384]{2,1,0:T(8,128)S(1)}, u32[]{:S(2)}, u32[]{:S(2)}) collective-permute-start(f32[2,32,384]{2,1,0:T(8,128)S(1)} %get-tuple-element.14), channel_id=1, source_target_pairs={{0,128},{16,144},{32,160},{48,176},{64,192},{80,208},{96,224},{112... | collective-permute-start | bytes 294920 | tf_op jit(solution)/shard_map/ppermute | solution.py:255
  30.0 29.0 %copy-start.4 = (s32[56]{0:T(128)S(1)}, s32[56]{0:T(128)}, u32[]{:S(2)}) copy-start(s32[56]{0:T(128)} %shard_map.50.table_ref) | copy-start | bytes 676
  30.0 9.5 %collective-permute-start.4 = (f32[2,32,384]{2,1,0:T(8,128)S(1)}, f32[2,32,384]{2,1,0:T(8,128)S(1)}, u32[]{:S(2)}, u32[]{:S(2)}) collective-permute-start(f32[2,32,384]{2,1,0:T(8,128)S(1)} %get-tuple-element.15), channel_id=1, source_target_pairs={{0,192},{16,208},{32,224},{48,240},{64,128},{80,144},{96,160},{112... | collective-permute-start | bytes 294920 | tf_op jit(solution)/shard_map/ppermute | solution.py:255
  40.9 18.0 %all-to-all-start.1 = ((f32[4,64,512]{2,1,0:T(8,128)}), f32[4,64,512]{2,1,0:T(8,128)S(1)}, u32[]{:S(2)}, u32[]{:S(2)}) async-start(f32[4,64,512]{2,1,0:T(8,128)} %shard_map.55), calls=%async_computation.1 | async-start | bytes 1048576 | tf_op jit(solution)/shard_map/all_to_all | solution.py:262
  47.9 8.7 %collective-permute-start.5 = (f32[32,384]{1,0:T(8,128)S(1)}, f32[32,384]{1,0:T(8,128)S(1)}, u32[]{:S(2)}, u32[]{:S(2)}) collective-permute-start(f32[32,384]{1,0:T(8,128)S(1)} %shard_map.54.after_ref), channel_id=1, source_target_pairs={{0,256},{16,272},{32,288},{48,304},{64,320},{80,336},{96,352},{112... | collective-permute-start | bytes 147464 | tf_op jit(solution)/shard_map/ppermute | solution.py:255
  60.3 22.0 %all-to-all-start.2 = ((f32[4,32,896]{2,1,0:T(8,128)}), f32[4,32,896]{2,1,0:T(8,128)S(1)}, u32[]{:S(2)}, u32[]{:S(2)}) async-start(f32[4,32,896]{2,1,0:T(8,128)} %get-tuple-element.21), calls=%async_computation.2 | async-start | bytes 917504 | tf_op jit(solution)/shard_map/all_to_all | solution.py:262
  66.4 8.9 %collective-permute-start.6 = (f32[32,512]{1,0:T(8,128)S(1)}, f32[32,512]{1,0:T(8,128)S(1)}, u32[]{:S(2)}, u32[]{:S(2)}) collective-permute-start(f32[32,512]{1,0:T(8,128)S(1)} %get-tuple-element.16.refs_0_), channel_id=1, source_target_pairs={{0,256},{16,272},{32,288},{48,304},{64,320},{80,336},{96,352},{112... | collective-permute-start | bytes 196616 | tf_op jit(solution)/shard_map/ppermute | solution.py:255
  75.3 7.0 %collective-permute-start.7 = (f32[2,32,512]{2,1,0:T(8,128)S(1)}, f32[2,32,512]{2,1,0:T(8,128)S(1)}, u32[]{:S(2)}, u32[]{:S(2)}) collective-permute-start(f32[2,32,512]{2,1,0:T(8,128)S(1)} %shard_map.57.refs_0_), channel_id=1, source_target_pairs={{0,64},{16,80},{32,96},{48,112},{64,0},{80,16},{96,32},{112,48},{1... | collective-permute-start | bytes 393224 | tf_op jit(solution)/shard_map/ppermute | solution.py:255
  83.6 30.7 %all-to-all-start.3 = ((f32[4,4,32,896]{3,2,1,0:T(8,128)}), f32[4,4,32,896]{3,2,1,0:T(8,128)S(1)}, u32[]{:S(2)}, u32[]{:S(2)}) async-start(f32[4,4,32,896]{3,2,1,0:T(8,128)} %shard_map.60), calls=%async_computation.3 | async-start | bytes 3670016 | tf_op jit(solution)/shard_map/all_to_all | solution.py:262
  88.2 8.0 %collective-permute-start.8 = (f32[2,32,512]{2,1,0:T(8,128)S(1)}, f32[2,32,512]{2,1,0:T(8,128)S(1)}, u32[]{:S(2)}, u32[]{:S(2)}) collective-permute-start(f32[2,32,512]{2,1,0:T(8,128)S(1)} %shard_map.57.refs_0_), channel_id=1, source_target_pairs={{0,128},{16,144},{32,160},{48,176},{64,192},{80,208},{96,224},{112... | collective-permute-start | bytes 393224 | tf_op jit(solution)/shard_map/ppermute | solution.py:255
  91.6 7.5 %collective-permute-start.9 = (f32[2,32,512]{2,1,0:T(8,128)S(1)}, f32[2,32,512]{2,1,0:T(8,128)S(1)}, u32[]{:S(2)}, u32[]{:S(2)}) collective-permute-start(f32[2,32,512]{2,1,0:T(8,128)S(1)} %shard_map.57.refs_0_), channel_id=1, source_target_pairs={{0,192},{16,208},{32,224},{48,240},{64,128},{80,144},{96,160},{112... | collective-permute-start | bytes 393224 | tf_op jit(solution)/shard_map/ppermute | solution.py:255
  99.8 10.2 %collective-permute-start.10 = (f32[2,2,32,512]{3,2,1,0:T(8,128)S(1)}, f32[2,2,32,512]{3,2,1,0:T(8,128)S(1)}, u32[]{:S(2)}, u32[]{:S(2)}) collective-permute-start(f32[2,2,32,512]{3,2,1,0:T(8,128)S(1)} %get-tuple-element.18), channel_id=1, source_target_pairs={{0,16},{16,0},{32,48},{48,32},{64,80},{80,64},{96,112},{112,96},{1... | collective-permute-start | bytes 786440 | tf_op jit(solution)/shard_map/ppermute | solution.py:255
  110.5 13.4 %collective-permute-start.11 = (f32[2,32,512]{2,1,0:T(8,128)S(1)}, f32[2,32,512]{2,1,0:T(8,128)S(1)}, u32[]{:S(2)}, u32[]{:S(2)}) collective-permute-start(f32[2,32,512]{2,1,0:T(8,128)S(1)} %get-tuple-element.20.after_ref), channel_id=1, source_target_pairs={{0,32},{16,48},{32,0},{48,16},{64,96},{80,112},{96,64},{112,80},{1... | collective-permute-start | bytes 393224 | tf_op jit(solution)/shard_map/ppermute | solution.py:255

commit v5 on v4

--- a/solution.py
+++ b/solution.py
@@ -21,10 +21,9 @@
 ANY = pl.BlockSpec(memory_space=pl.ANY)
 HBM = pl.BlockSpec(memory_space=pltpu.HBM)
 SMEM = pl.BlockSpec(memory_space=pltpu.SMEM)
-PARAMS = pltpu.CompilerParams(vmem_limit_bytes=40 * 2**20)
-
-
-def call(kernel, out_shape, in_specs, cost, *args, scratch=(), out_specs=VMEM):
+
+
+def call(kernel, out_shape, in_specs, cost, *args, scratch=(), out_specs=VMEM, limit=40):
     multiple = isinstance(out_shape, (list, tuple))
     return pl.pallas_call(
         kernel,
@@ -32,28 +31,41 @@
         in_specs=in_specs,
         out_specs=[out_specs] * len(out_shape) if multiple else out_specs,
         scratch_shapes=list(scratch),
-        compiler_params=PARAMS,
+        compiler_params=pltpu.CompilerParams(vmem_limit_bytes=limit * 2**20),
         cost_estimate=pl.CostEstimate(flops=cost[0], bytes_accessed=cost[1], transcendentals=0),
     )(*args)
 
 
-def gram_kernel(grads_ref, out_ref):
+def gram_kernel(grads_hbm, out_ref, grads_ref, whole_ref, in_sems, out_sems):
     shards, size, _ = grads_ref.shape
     xs, zs, double, _ = out_ref.shape
     rows = double // 2
-    gram = None
-    total = None
-    for s in range(shards):
-        g = grads_ref[s]
-        term = lax.dot_general(g, g, (((1,), (1,)), ((), ())), preferred_element_type=f32)
-        gram = term if gram is None else gram + term
-        wide = g.astype(f32)
-        total = wide if total is None else total + wide
-    gram = gram.reshape(zs, xs, rows, size)
-    total = total.reshape(zs, xs, rows, size)
-    for x in range(xs):
-        out_ref[x, :, :rows, :] = gram[:, x]
-        out_ref[x, :, rows:, :] = total[:, x]
+    loads = [pltpu.make_async_copy(grads_hbm.at[s], grads_ref.at[s], in_sems.at[s]) for s in range(shards)]
+    for load in loads:
+        load.start()
+    for load in loads:
+        load.wait()
+    stores = []
+    half = size // 2
+    for h in range(2):
+        gram = None
+        total = None
+        for s in range(shards):
+            mine = grads_ref[s, h * half : (h + 1) * half]
+            term = lax.dot_general(mine, grads_ref[s], (((1,), (1,)), ((), ())), preferred_element_type=f32)
+            gram = term if gram is None else gram + term
+            wide = mine.astype(f32)
+            total = wide if total is None else total + wide
+        gram = gram.reshape(zs // 2, xs, rows, size)
+        total = total.reshape(zs // 2, xs, rows, size)
+        part = slice(h * zs // 2, (h + 1) * zs // 2)
+        for x in range(xs):
+            whole_ref[x, part, :rows, :] = gram[:, x]
+            whole_ref[x, part, rows:, :] = total[:, x]
+            stores.append(pltpu.make_async_copy(whole_ref.at[x, part], out_ref.at[x, part], out_sems.at[h, x]))
+            stores[-1].start()
+    for store in stores:
+        store.wait()
 
 
 def sum_kernel(parts_ref, after_ref, out_ref):
@@ -101,10 +113,9 @@
     put(7, me, me >> 4, True)
     for i in range(8):
         block = block_ref[i]
-        out_ref[RETURN + 4 * i] = ((block ^ me) >> 2) & 3
-        out_ref[RETURN + 4 * i + 1] = ((block ^ me) >> 4) & 1
-        out_ref[RETURN + 4 * i + 2] = (block ^ me) & 1
-        out_ref[RETURN + 4 * i + 3] = jnp.where(block < 0, 0, 1 + (((block ^ me) >> 1) & 1))
+        out_ref[RETURN + 3 * i] = ((block ^ me) >> 2) & 1
+        out_ref[RETURN + 3 * i + 1] = (((block ^ me) >> 4) & 1) + 2 * (((block ^ me) >> 3) & 1)
+        out_ref[RETURN + 3 * i + 2] = jnp.where(block < 0, -1, (block ^ me) & 3)
 
 
 def columns(place, rows, size):
@@ -138,43 +149,35 @@
 
 def stat_kernel(table_ref, place_ref, sums_ref, kept_ref, core_ref, *refs):
     wide_ref, gram_ref, both_ref = refs[4:]
-    rows, size = gram_ref.shape
+    _, rows, size = gram_ref.shape
     sums = jnp.sum(sums_ref[...], axis=0)
-    gram_ref[...] = sums[:rows]
+    gram_ref[0] = sums[:rows]
     keep = size - LANES
     for n, column in enumerate(columns(place_ref[0], rows, size)):
-        both_ref[:, n * LANES : (n + 1) * LANES] = gram_ref[:, pl.ds(column, LANES)]
+        both_ref[:, n * LANES : (n + 1) * LANES] = gram_ref[0, :, pl.ds(column, LANES)]
     both_ref[:, :keep] += pick(table_ref, 7, kept_ref, core_ref, refs[:3], refs[3:4])
     both_ref[:, keep:] = sums[rows:]
     wide_ref[...] = jnp.broadcast_to(both_ref[...][None], wide_ref.shape)
 
 
-def stack_kernel(*refs):
-    for m, part in enumerate(refs[:-1]):
-        refs[-1][m] = part[...]
-
-
-def return_kernel(table_ref, *refs):
-    lines, (own_ref, core_ref) = refs[:-2], refs[-2:]
+def stack_kernel(first_ref, second_ref, out_ref):
+    half = out_ref.shape[0] // 2
+    out_ref[:half] = first_ref[...]
+    out_ref[half:] = second_ref[...]
+
+
+def return_kernel(table_ref, line_ref, far_ref, *outs):
     for i in range(8):
-        n, line = table_ref[RETURN + 4 * i], table_ref[RETURN + 4 * i + 1]
-        out_ref = core_ref if i // 2 % 2 else own_ref
-        out_ref[i // 4, i % 2] = choose(n, [g[line] for g in lines])
-
-
-def pass_kernel(table_ref, own_ref, core_ref, mine_ref, send_ref):
-    for k, out in enumerate((mine_ref, send_ref)):
-        for j in range(2):
-            other = table_ref[RETURN + 4 * (4 * k + j) + 2]
-            out[j] = jnp.where(other == 0, own_ref[k, j], core_ref[k, j])
-
-
-def state_kernel(table_ref, state_ref, mine_ref, got_ref, after_ref, out_ref):
+        n, line = table_ref[RETURN + 3 * i], table_ref[RETURN + 3 * i + 1]
+        outs[i // 2][i % 2] = choose(n, [line_ref[line], far_ref[line]])
+
+
+def state_kernel(table_ref, state_ref, got0, got1, got2, got3, after_ref, out_ref):
     del after_ref
     for j in range(2):
-        way = table_ref[RETURN + 4 * j + 3]
-        gram = jnp.where(way == 1, mine_ref[j], got_ref[j])
-        out_ref[j] = state_ref[j] + jnp.where(way > 0, gram, 0.0)
+        way = table_ref[RETURN + 3 * j + 2]
+        gram = choose(way, [got0[j], got1[j], got2[j], got3[j]])
+        out_ref[j] = state_ref[j] + jnp.where(way >= 0, gram, 0.0)
 
 
 def split(a):
@@ -184,8 +187,11 @@
 
 def product(a, b):
     (a_high, a_low), (b_high, b_low) = a, b
-    dot = lambda x, y: jnp.dot(x, y, preferred_element_type=f32)
-    return dot(a_high, b_high) + (dot(a_high, b_low) + dot(a_low, b_high))
+    return jnp.dot(
+        jnp.concatenate([a_high, a_high, a_low], axis=1),
+        jnp.concatenate([b_high, b_low, b_high], axis=0),
+        preferred_element_type=f32,
+    )
 
 
 def copies_kernel(part_ref, after_ref, out_ref, sems):
@@ -195,6 +201,13 @@
         copy.start()
     for copy in copies:
         copy.wait()
+
+
+def thin_product(a, b):
+    a_high, a_low = split(a)
+    rows = a.shape[0]
+    both = jnp.dot(jnp.concatenate([a_high, a_low], axis=0), b[0], preferred_element_type=f32)
+    return both[:rows] + (both[rows:] + jnp.dot(a_high, b[1], preferred_element_type=f32))
 
 
 def newton_kernel(count, place_ref, all_ref, after_ref, out_ref, end_ref, stat_ref):
@@ -212,14 +225,13 @@
             if n == 1:
                 stat_ref[j * LANES : (j + 1) * LANES, z * LANES : (z + 1) * LANES] = part.T
     stat = stat_ref[...]
-    row_ids = lax.broadcasted_iota(jnp.int32, (size, size), 0)
-    col_ids = lax.broadcasted_iota(jnp.int32, (size, size), 1)
-    eye = (row_ids == col_ids).astype(f32)
+    diagonal = lax.broadcasted_iota(jnp.int32, (size, size), 0) == lax.broadcasted_iota(jnp.int32, (size, size), 1)
+    plus = lambda a, m: jnp.where(diagonal, m + a, m)
     thin_rows = lax.broadcasted_iota(jnp.int32, (rows, size), 0) + place * rows
     thin_cols = lax.broadcasted_iota(jnp.int32, (rows, size), 1)
     thin_eye = (thin_rows == thin_cols).astype(f32)
     norm = jnp.sqrt(jnp.sum(stat * stat))
-    damped = stat + (DAMP * norm) * eye
+    damped = plus(DAMP * norm, stat)
     scale = jnp.sqrt(jnp.sum(damped * damped))
     iterate = damped / scale
     mine = stat_ref[pl.ds(pl.multiple_of(place * rows, rows), rows), :]
@@ -228,13 +240,13 @@
     parts_of = split(iterate)
     for _ in range(ITERS - 2):
         square = product(parts_of, parts_of)
-        factor2 = split(1.5625 * eye - 0.625 * iterate + 0.0625 * square)
+        factor2 = split(plus(1.5625, 0.0625 * square - 0.625 * iterate))
         iterate = product(parts_of, split(product(factor2, factor2)))
         parts_of = split(iterate)
-        thin = 1.25 * thin - 0.25 * product(split(thin), parts_of)
-    last = product(split(thin), parts_of)
+        thin = 1.25 * thin - 0.25 * thin_product(thin, parts_of)
+    last = thin_product(thin, parts_of)
     for _ in range(4):
-        last = 1.25 * last - 0.25 * product(split(last), parts_of)
+        last = 1.25 * last - 0.25 * thin_product(last, parts_of)
     thin = (1.25 * thin - 0.25 * last) * jnp.exp(-0.25 * jnp.log(scale))
     mean = jnp.concatenate([all_ref[x, z, :, size - LANES :] for z in range(zs) for x in range(xs)], axis=0)
     mean = (mean / count).astype(bf16)
@@ -265,7 +277,7 @@
     place = lax.axis_index("rep").reshape(1).astype(jnp.int32)
     table = pl.pallas_call(
         table_kernel,
-        out_shape=jax.ShapeDtypeStruct((RETURN + 32,), jnp.int32),
+        out_shape=jax.ShapeDtypeStruct((RETURN + 24,), jnp.int32),
         in_specs=[SMEM, SMEM],
         out_specs=SMEM,
         scratch_shapes=[
@@ -279,16 +291,24 @@
     sums = call(
         gram_kernel,
         shape(ACROSS, zs, 2 * rows, size),
-        [VMEM],
+        [ANY],
         (2 * shards * size**3, 4 * size * size * (shards + 2)),
         local,
+        limit=60,
+        out_specs=ANY,
+        scratch=[
+            pltpu.VMEM(local.shape, local.dtype),
+            pltpu.VMEM((ACROSS, zs, 2 * rows, size), f32),
+            pltpu.SemaphoreType.DMA((shards,)),
+            pltpu.SemaphoreType.DMA((2, ACROSS)),
+        ],
     )
     sums = exchange(sums, x_groups)
     kept = call(
         keep_kernel,
         shape(2, capacity, rows, size - LANES),
         [SMEM, VMEM, VMEM],
-        (0, 4 * size * rows * 8),
+        (2 * 100 * size**3, 4 * size * rows * 8),
         place,
         held,
         held_z,
@@ -326,7 +346,7 @@
     far = across(far, 4 * GROUP)
     both, gram = call(
         stat_kernel,
-        [shape(zs, rows, 2 * size - LANES), shape(rows, size)],
+        [shape(zs, rows, 2 * size - LANES), shape(1, rows, size)],
         [SMEM, SMEM] + [VMEM] * 7,
         (0, 4 * size * rows * 45),
         table,
@@ -339,42 +359,37 @@
         scratch=[pltpu.VMEM((rows, 2 * size - LANES), f32)],
     )
     both = exchange(both, z_groups)
-    line = call(
-        stack_kernel,
-        shape(2, rows, size),
-        [VMEM] * 2,
-        (0, 4 * size * rows * 4),
-        gram,
-        across(gram, 4 * GROUP),
-    )
-    lines = [line] + [across(line, GROUP * n) for n in range(1, 4)]
+    line = gram
+    lines = []
+    for bit in (4, 2):
+        line = call(
+            stack_kernel,
+            shape(2 * line.shape[0], rows, size),
+            [VMEM] * 2,
+            (0, 4 * size * rows * 8),
+            line,
+            across(line, GROUP * bit),
+        )
+        lines.append(line)
     both = call(
         copies_kernel,
         shape(ACROSS, zs, rows, 2 * size - LANES),
         [VMEM, ANY],
         (0, 4 * size * rows * 40),
         both,
-        lines[1],
+        lines[0],
         out_specs=HBM,
         scratch=[pltpu.SemaphoreType.DMA((ACROSS,))],
     )
     both = exchange(both, x_groups)
-    own, core = call(
+    own, *sent = call(
         return_kernel,
-        [shape(2, capacity, rows, size)] * 2,
-        [SMEM] + [VMEM] * 4,
+        [shape(capacity, rows, size)] * 4,
+        [SMEM] + [VMEM] * 2,
         (0, 4 * size * rows * 24),
         table,
-        *lines,
-    )
-    mine, passed = call(
-        pass_kernel,
-        [shape(capacity, rows, size)] * 2,
-        [SMEM, VMEM, VMEM],
-        (0, 4 * size * rows * 12),
-        table,
-        own,
-        across(core, 1),
+        line,
+        across(line, GROUP),
     )
     count = shards * reps
     update, end = call(
@@ -384,18 +399,18 @@
         (2 * 20 * size**3, 8 * size * size),
         place,
         both,
-        passed,
+        own,
         scratch=[pltpu.VMEM((size, size), f32)],
     )
     new_state = call(
         state_kernel,
         shape(capacity, rows, size),
-        [SMEM, VMEM, VMEM, VMEM, ANY],
+        [SMEM] + [VMEM] * 5 + [ANY],
         (0, 4 * size * rows * 8),
         table,
         held,
-        mine,
-        across(passed, 2),
+        own,
+        *[across(rows_sent, k + 1) for k, rows_sent in enumerate(sent)],
         end,
     )
     return (new_state[None], update)

time: 126 us -> 124 us (0.984)
  starting transfers between devices: 80.1 us -> 76.5 us
  waiting for transfers between devices: 22 us -> 24.1 us
  local copies, waits for them, and re-layouts: 3.21 us -> 1.32 us
    all_to_all x4, waiting for transfers between devices: 2.28 us -> 8.43 us  [exchange(): return lax.all_to_all(x, 'rep', 0, 0, tiled=True, axis_index_groups=which)]
    ppermute x12, starting transfers between devices: 57.5 us -> 53 us  [across(): return lax.ppermute(x, 'pre', [(i, i ^ k) for i in range(blocks)])]
    ppermute x12, waiting for transfers between devices: 19.8 us -> 15.7 us  [across(): return lax.ppermute(x, 'pre', [(i, i ^ k) for i in range(blocks)])]
    unnamed x10 -> x8, local copies, waits for them, and re-layouts: 3.21 us -> 1.32 us
  transfers between devices with their start and end apart: 16 -> 16, of which waited for: 9 -> 9; matrix products, arithmetic and copies ran while one was open for 0% -> 0% of each run, Pallas kernels for 11% -> 12%
where the time goes in v5:
time: 124 us; the launch traced here: 123 us
  starting transfers between devices  76.5 us (62%)
  waiting for transfers between devices  24.1 us (19%)
  Pallas kernels  20 us (16%)
  local copies, waits for them, and re-layouts  1.32 us (1%)
    ppermute x12, starting transfers between devices, across(): return lax.ppermute(x, 'pre', [(i, i ^ k) for i in range(blocks)])  53 us
    all_to_all x4, starting transfers between devices, exchange(): return lax.all_to_all(x, 'rep', 0, 0, tiled=True, axis_index_groups=which)  23.5 us
    pallas_call x12, Pallas kernels, call(): pl.pallas_call(kernel, out_shape=out_shape, in_specs=in_specs, out_specs=...  18.6 us
    ppermute x12, waiting for transfers between devices, across(): return lax.ppermute(x, 'pre', [(i, i ^ k) for i in range(blocks)])  15.7 us
    all_to_all x4, waiting for transfers between devices, exchange(): return lax.all_to_all(x, 'rep', 0, 0, tiled=True, axis_index_groups=which)  8.43 us
  transfers between devices with their start and end apart: 16, of which 9 were waited for; matrix products, arithmetic and copies ran while one was open for 0% of the time, Pallas kernels for 12%

profile of v5, /device:TPU:1, one launch (start us, length us, event | category | flops | bytes accessed | tf_op | source)
XLA Modules:
  0.0 122.8 jit_solution(10631203795634574755)
XLA Ops:
  0.6 4.8 %collective-permute-start = (f32[2,32,512]{2,1,0:T(8,128)}, f32[2,32,512]{2,1,0:T(8,128)S(1)}, u32[]{:S(2)}, u32[]{:S(2)}) collective-permute-start(f32[2,32,512]{2,1,0:T(8,128)} %bitcast.5), channel_id=1, source_target_pairs={{0,32},{16,48},{32,0},{48,16},{64,96},{80,112},{96,64},{112,80},{1... | collective-permute-start | bytes 393224 | tf_op jit(solution)/shard_map/ppermute | solution.py:267
  5.5 3.1 %shard_map.51 = f32[4,4,64,512]{3,2,1,0:T(8,128)} custom-call(bf16[2,512,512]{2,1,0:T(8,128)(2,1)} %bitcast.8), custom_call_target="tpu_custom_call" | custom-call | flops 536870912 | bytes 4194304 | tf_op jit(solution)/shard_map/pallas_call | solution.py:28
  8.5 0.0 copy-start
  8.6 4.2 %all-to-all-start = ((f32[4,4,64,512]{3,2,1,0:T(8,128)}), f32[4,4,64,512]{3,2,1,0:T(8,128)S(1)}, u32[]{:S(2)}, u32[]{:S(2)}) async-start(f32[4,4,64,512]{3,2,1,0:T(8,128)} %shard_map.51), calls=%async_computation | async-start | bytes 4194304 | tf_op jit(solution)/shard_map/all_to_all | solution.py:274
  12.7 0.0 collective-permute-done.held_z_ref
  12.7 0.0 copy-done
  12.8 5.5 %collective-permute-start.1 = (f32[2,2,32,384]{3,2,1,0:T(8,128)S(1)}, f32[2,2,32,384]{3,2,1,0:T(8,128)S(1)}, u32[]{:S(2)}, u32[]{:S(2)}) collective-permute-start(f32[2,2,32,384]{3,2,1,0:T(8,128)S(1)} %shard_map.52.kept_ref), channel_id=1, source_target_pairs={{0,16},{16,0},{32,48},{48,32},{64,80},{80,64},{96,112},{112,96},{1... | collective-permute-start | bytes 589832 | tf_op jit(solution)/shard_map/ppermute | solution.py:267
  18.3 1.4 %shard_map.50.table_ref = s32[48]{0:T(128)} custom-call(s32[1]{0:T(128)} %bitcast.me_ref, s32[32]{0:T(128)} %owner_ref.1), custom_call_target="tpu_custom_call" | custom-call | tf_op jit(solution)/shard_map/pallas_call | solution.py:278
  19.7 0.0 collective-permute-done.1.core_ref
  19.7 0.0 copy-start.1
  19.8 0.6 copy-done.1
  20.4 0.6 shard_map.53
  21.0 1.9 %collective-permute-start.2 = (f32[2,32,384]{2,1,0:T(8,128)S(1)}, f32[2,32,384]{2,1,0:T(8,128)S(1)}, u32[]{:S(2)}, u32[]{:S(2)}) collective-permute-start(f32[2,32,384]{2,1,0:T(8,128)S(1)} %get-tuple-element.13), channel_id=1, source_target_pairs={{0,64},{16,80},{32,96},{48,112},{64,0},{80,16},{96,32},{112,48},{1... | collective-permute-start | bytes 294920 | tf_op jit(solution)/shard_map/ppermute | solution.py:267
  22.9 3.2 %collective-permute-start.3 = (f32[2,32,384]{2,1,0:T(8,128)S(1)}, f32[2,32,384]{2,1,0:T(8,128)S(1)}, u32[]{:S(2)}, u32[]{:S(2)}) collective-permute-start(f32[2,32,384]{2,1,0:T(8,128)S(1)} %get-tuple-element.14), channel_id=1, source_target_pairs={{0,128},{16,144},{32,160},{48,176},{64,192},{80,208},{96,224},{112... | collective-permute-start | bytes 294920 | tf_op jit(solution)/shard_map/ppermute | solution.py:267
  26.1 0.0 copy-start.3
  26.1 4.2 %collective-permute-start.4 = (f32[2,32,384]{2,1,0:T(8,128)S(1)}, f32[2,32,384]{2,1,0:T(8,128)S(1)}, u32[]{:S(2)}, u32[]{:S(2)}) collective-permute-start(f32[2,32,384]{2,1,0:T(8,128)S(1)} %get-tuple-element.15), channel_id=1, source_target_pairs={{0,192},{16,208},{32,224},{48,240},{64,128},{80,144},{96,160},{112... | collective-permute-start | bytes 294920 | tf_op jit(solution)/shard_map/ppermute | solution.py:267
  30.3 0.0 collective-permute-done.2.near1.refs_0_
  30.3 1.9 %collective-permute-done.3.near2.refs_1_ = f32[2,32,384]{2,1,0:T(8,128)S(1)} collective-permute-done((f32[2,32,384]{2,1,0:T(8,128)S(1)}, f32[2,32,384]{2,1,0:T(8,128)S(1)}, u32[]{:S(2)}, u32[]{:S(2)}) %collective-permute-start.3) | collective-permute-done | bytes 98336 | tf_op jit(solution)/shard_map/ppermute | solution.py:267
  32.2 1.4 %collective-permute-done.4.near3.refs_2_ = f32[2,32,384]{2,1,0:T(8,128)S(1)} collective-permute-done((f32[2,32,384]{2,1,0:T(8,128)S(1)}, f32[2,32,384]{2,1,0:T(8,128)S(1)}, u32[]{:S(2)}, u32[]{:S(2)}) %collective-permute-start.4) | collective-permute-done | bytes 98336 | tf_op jit(solution)/shard_map/ppermute | solution.py:267
  33.7 0.0 copy-start.2
  33.7 0.7 copy-done.2
  34.3 0.6 shard_map.54.after_ref
  34.9 0.7 all-to-all-done.parts_ref
  35.5 0.9 shard_map.55
  36.5 11.4 %all-to-all-start.1 = ((f32[4,64,512]{2,1,0:T(8,128)}), f32[4,64,512]{2,1,0:T(8,128)S(1)}, u32[]{:S(2)}, u32[]{:S(2)}) async-start(f32[4,64,512]{2,1,0:T(8,128)} %shard_map.55), calls=%async_computation.1 | async-start | bytes 1048576 | tf_op jit(solution)/shard_map/all_to_all | solution.py:274
  47.9 7.4 %collective-permute-start.5 = (f32[32,384]{1,0:T(8,128)S(1)}, f32[32,384]{1,0:T(8,128)S(1)}, u32[]{:S(2)}, u32[]{:S(2)}) collective-permute-start(f32[32,384]{1,0:T(8,128)S(1)} %shard_map.54.after_ref), channel_id=1, source_target_pairs={{0,256},{16,272},{32,288},{48,304},{64,320},{80,336},{96,352},{112... | collective-permute-start | bytes 147464 | tf_op jit(solution)/shard_map/ppermute | solution.py:267
  55.3 1.5 %collective-permute-done.5.refs_3_ = f32[32,384]{1,0:T(8,128)S(1)} collective-permute-done((f32[32,384]{1,0:T(8,128)S(1)}, f32[32,384]{1,0:T(8,128)S(1)}, u32[]{:S(2)}, u32[]{:S(2)}) %collective-permute-start.5) | collective-permute-done | bytes 49184 | tf_op jit(solution)/shard_map/ppermute | solution.py:267
  56.8 6.0 %all-to-all-done.1.sums_ref = f32[4,64,512]{2,1,0:T(8,128)S(1)} async-done(((f32[4,64,512]{2,1,0:T(8,128)}), f32[4,64,512]{2,1,0:T(8,128)S(1)}, u32[]{:S(2)}, u32[]{:S(2)}) %all-to-all-start.1) | async-done | bytes 524320 | tf_op jit(solution)/shard_map/all_to_all | solution.py:274
  62.9 0.0 copy-done.3
  62.9 1.4 %shard_map.56 = (f32[4,32,896]{2,1,0:T(8,128)}, f32[1,32,512]{2,1,0:T(8,128)S(1)}) custom-call(s32[48]{0:T(128)S(1)} %copy-done.3, s32[1]{0:T(128)} %bitcast.2.place_ref, f32[4,64,512]{2,1,0:T(8,128)S(1)} %all-to-all-done.1.sums_ref, f32[2,2,32,384]{3,2,1,0:T(8,128)S(1)} %shard_map.52.kept_ref, f32[2,2,32,384]{3,2,1,0:T(8,128)S(1)} %collective-permute-done.1.core_ref, ...), custom_call_target="tpu_custom_call" | custom-call | bytes 2949120 | tf_op jit(solution)/shard_map/pallas_call | solution.py:28
  64.2 4.3 %all-to-all-start.2 = ((f32[4,32,896]{2,1,0:T(8,128)}), f32[4,32,896]{2,1,0:T(8,128)S(1)}, u32[]{:S(2)}, u32[]{:S(2)}) async-start(f32[4,32,896]{2,1,0:T(8,128)} %get-tuple-element.21), calls=%async_computation.2 | async-start | bytes 917504 | tf_op jit(solution)/shard_map/all_to_all | solution.py:274
  68.6 7.4 %collective-permute-start.6 = (f32[1,32,512]{2,1,0:T(8,128)S(1)}, f32[1,32,512]{2,1,0:T(8,128)S(1)}, u32[]{:S(2)}, u32[]{:S(2)}) collective-permute-start(f32[1,32,512]{2,1,0:T(8,128)S(1)} %get-tuple-element.16.first_ref), channel_id=1, source_target_pairs={{0,256},{16,272},{32,288},{48,304},{64,320},{80,336},{96,352},{112... | collective-permute-start | bytes 196616 | tf_op jit(solution)/shard_map/ppermute | solution.py:267
  76.0 1.7 %collective-permute-done.6.second_ref = f32[1,32,512]{2,1,0:T(8,128)S(1)} collective-permute-done((f32[1,32,512]{2,1,0:T(8,128)S(1)}, f32[1,32,512]{2,1,0:T(8,128)S(1)}, u32[]{:S(2)}, u32[]{:S(2)}) %collective-permute-start.6) | collective-permute-done | bytes 65568 | tf_op jit(solution)/shard_map/ppermute | solution.py:267
  77.7 1.8 %all-to-all-done.2.part_ref = f32[4,32,896]{2,1,0:T(8,128)S(1)} async-done(((f32[4,32,896]{2,1,0:T(8,128)}), f32[4,32,896]{2,1,0:T(8,128)S(1)}, u32[]{:S(2)}, u32[]{:S(2)}) %all-to-all-start.2) | async-done | bytes 458784 | tf_op jit(solution)/shard_map/all_to_all | solution.py:274
  79.5 1.3 %shard_map.60 = f32[4,4,32,896]{3,2,1,0:T(8,128)} custom-call(f32[4,32,896]{2,1,0:T(8,128)S(1)} %all-to-all-done.2.part_ref, f32[2,32,512]{2,1,0:T(8,128)S(1)} %shard_map.57.first_ref.after_ref), custom_call_target="tpu_custom_call" | custom-call | bytes 2621440 | tf_op jit(solution)/shard_map/pallas_call | solution.py:28
  80.8 3.6 %all-to-all-start.3 = ((f32[4,4,32,896]{3,2,1,0:T(8,128)}), f32[4,4,32,896]{3,2,1,0:T(8,128)S(1)}, u32[]{:S(2)}, u32[]{:S(2)}) async-start(f32[4,4,32,896]{3,2,1,0:T(8,128)} %shard_map.60), calls=%async_computation.3 | async-start | bytes 3670016 | tf_op jit(solution)/shard_map/all_to_all | solution.py:274
  84.4 4.3 %collective-permute-start.7 = (f32[2,32,512]{2,1,0:T(8,128)S(1)}, f32[2,32,512]{2,1,0:T(8,128)S(1)}, u32[]{:S(2)}, u32[]{:S(2)}) collective-permute-start(f32[2,32,512]{2,1,0:T(8,128)S(1)} %shard_map.57.first_ref.after_ref), channel_id=1, source_target_pairs={{0,128},{16,144},{32,160},{48,176},{64,192},{80,208},{96,224},{112... | collective-permute-start | bytes 393224 | tf_op jit(solution)/shard_map/ppermute | solution.py:267
  88.7 4.0 %collective-permute-done.7.second_ref = f32[2,32,512]{2,1,0:T(8,128)S(1)} collective-permute-done((f32[2,32,512]{2,1,0:T(8,128)S(1)}, f32[2,32,512]{2,1,0:T(8,128)S(1)}, u32[]{:S(2)}, u32[]{:S(2)}) %collective-permute-start.7) | collective-permute-done | bytes 131104 | tf_op jit(solution)/shard_map/ppermute | solution.py:267
  92.8 2.3 %collective-permute-start.8 = (f32[4,32,512]{2,1,0:T(8,128)S(1)}, f32[4,32,512]{2,1,0:T(8,128)S(1)}, u32[]{:S(2)}, u32[]{:S(2)}) collective-permute-start(f32[4,32,512]{2,1,0:T(8,128)S(1)} %shard_map.58.line_ref), channel_id=1, source_target_pairs={{0,64},{16,80},{32,96},{48,112},{64,0},{80,16},{96,32},{112,48},{1... | collective-permute-start | bytes 786440 | tf_op jit(solution)/shard_map/ppermute | solution.py:267
  95.1 5.1 %collective-permute-done.8.far_ref = f32[4,32,512]{2,1,0:T(8,128)S(1)} collective-permute-done((f32[4,32,512]{2,1,0:T(8,128)S(1)}, f32[4,32,512]{2,1,0:T(8,128)S(1)}, u32[]{:S(2)}, u32[]{:S(2)}) %collective-permute-start.8) | collective-permute-done | bytes 262176 | tf_op jit(solution)/shard_map/ppermute | solution.py:267
  100.2 0.6 shard_map.59
  100.8 6.4 %collective-permute-start.9 = (f32[2,32,512]{2,1,0:T(8,128)S(1)}, f32[2,32,512]{2,1,0:T(8,128)S(1)}, u32[]{:S(2)}, u32[]{:S(2)}) collective-permute-start(f32[2,32,512]{2,1,0:T(8,128)S(1)} %get-tuple-element.18), channel_id=1, source_target_pairs={{0,16},{16,0},{32,48},{48,32},{64,80},{80,64},{96,112},{112,96},{1... | collective-permute-start | bytes 393224 | tf_op jit(solution)/shard_map/ppermute | solution.py:267
  107.2 2.7 %collective-permute-start.10 = (f32[2,32,512]{2,1,0:T(8,128)S(1)}, f32[2,32,512]{2,1,0:T(8,128)S(1)}, u32[]{:S(2)}, u32[]{:S(2)}) collective-permute-start(f32[2,32,512]{2,1,0:T(8,128)S(1)} %get-tuple-element.19), channel_id=1, source_target_pairs={{0,32},{16,48},{32,0},{48,16},{64,96},{80,112},{96,64},{112,80},{1... | collective-permute-start | bytes 393224 | tf_op jit(solution)/shard_map/ppermute | solution.py:267
  109.9 2.8 %collective-permute-start.11 = (f32[2,32,512]{2,1,0:T(8,128)S(1)}, f32[2,32,512]{2,1,0:T(8,128)S(1)}, u32[]{:S(2)}, u32[]{:S(2)}) collective-permute-start(f32[2,32,512]{2,1,0:T(8,128)S(1)} %get-tuple-element.20), channel_id=1, source_target_pairs={{0,48},{16,32},{32,16},{48,0},{64,112},{80,96},{96,80},{112,64},{1... | collective-permute-start | bytes 393224 | tf_op jit(solution)/shard_map/ppermute | solution.py:267
  112.7 0.0 all-to-all-done.3.all_ref
  112.7 8.9 %shard_map.61 = (bf16[1,32,512]{2,1,0:T(8,128)(2,1)}, f32[8,128]{1,0:T(8,128)S(1)}) custom-call(s32[1]{0:T(128)} %bitcast.2.place_ref, f32[4,4,32,896]{3,2,1,0:T(8,128)S(1)} %all-to-all-done.3.all_ref, f32[2,32,512]{2,1,0:T(8,128)S(1)} %get-tuple-element.17.after_ref.got0), custom_call_target="tpu_custom_call" | custom-call | flops 5368709120 | bytes 2097152 | tf_op jit(solution)/shard_map/pallas_call | solution.py:28
  121.6 0.0 collective-permute-done.9.got1
  121.6 0.0 collective-permute-done.10.got2
  121.6 0.0 collective-permute-done.11.got3
  121.6 1.2 %shard_map.62 = f32[2,32,512]{2,1,0:T(8,128)} custom-call(s32[48]{0:T(128)S(1)} %copy-done.3, f32[2,32,512]{2,1,0:T(8,128)S(1)} %bitcast.7, f32[2,32,512]{2,1,0:T(8,128)S(1)} %get-tuple-element.17.after_ref.got0, f32[2,32,512]{2,1,0:T(8,128)S(1)} %collective-permute-done.9.got1, f32[2,32,512]{2,1,0:T(8,128)S(1)} %collective-permute-done.10.got2, ...), custom_call_target="tpu_custom_call" | custom-call | bytes 524288 | tf_op jit(solution)/shard_map/pallas_call | solution.py:28
  (3 shorter events, 0.1 us)
Async XLA Ops:
  0.6 12.1 %collective-permute-start = (f32[2,32,512]{2,1,0:T(8,128)}, f32[2,32,512]{2,1,0:T(8,128)S(1)}, u32[]{:S(2)}, u32[]{:S(2)}) collective-permute-start(f32[2,32,512]{2,1,0:T(8,128)} %bitcast.5), channel_id=1, source_target_pairs={{0,32},{16,48},{32,0},{48,16},{64,96},{80,112},{96,64},{112,80},{1... | collective-permute-start | bytes 393224 | tf_op jit(solution)/shard_map/ppermute | solution.py:267
  8.5 4.2 %copy-start = (f32[1,2,32,512]{3,2,1,0:T(8,128)S(1)}, f32[1,2,32,512]{3,2,1,0:T(8,128)}, u32[]{:S(2)}) copy-start(f32[1,2,32,512]{3,2,1,0:T(8,128)} %param.5) | copy-start | bytes 393220
  8.6 27.0 %all-to-all-start = ((f32[4,4,64,512]{3,2,1,0:T(8,128)}), f32[4,4,64,512]{3,2,1,0:T(8,128)S(1)}, u32[]{:S(2)}, u32[]{:S(2)}) async-start(f32[4,4,64,512]{3,2,1,0:T(8,128)} %shard_map.51), calls=%async_computation | async-start | bytes 4194304 | tf_op jit(solution)/shard_map/all_to_all | solution.py:274
  12.8 7.0 %collective-permute-start.1 = (f32[2,2,32,384]{3,2,1,0:T(8,128)S(1)}, f32[2,2,32,384]{3,2,1,0:T(8,128)S(1)}, u32[]{:S(2)}, u32[]{:S(2)}) collective-permute-start(f32[2,2,32,384]{3,2,1,0:T(8,128)S(1)} %shard_map.52.kept_ref), channel_id=1, source_target_pairs={{0,16},{16,0},{32,48},{48,32},{64,80},{80,64},{96,112},{112,96},{1... | collective-permute-start | bytes 589832 | tf_op jit(solution)/shard_map/ppermute | solution.py:267
  19.7 0.7 copy-start.1
  21.0 9.3 %collective-permute-start.2 = (f32[2,32,384]{2,1,0:T(8,128)S(1)}, f32[2,32,384]{2,1,0:T(8,128)S(1)}, u32[]{:S(2)}, u32[]{:S(2)}) collective-permute-start(f32[2,32,384]{2,1,0:T(8,128)S(1)} %get-tuple-element.13), channel_id=1, source_target_pairs={{0,64},{16,80},{32,96},{48,112},{64,0},{80,16},{96,32},{112,48},{1... | collective-permute-start | bytes 294920 | tf_op jit(solution)/shard_map/ppermute | solution.py:267
  22.9 9.3 %collective-permute-start.3 = (f32[2,32,384]{2,1,0:T(8,128)S(1)}, f32[2,32,384]{2,1,0:T(8,128)S(1)}, u32[]{:S(2)}, u32[]{:S(2)}) collective-permute-start(f32[2,32,384]{2,1,0:T(8,128)S(1)} %get-tuple-element.14), channel_id=1, source_target_pairs={{0,128},{16,144},{32,160},{48,176},{64,192},{80,208},{96,224},{112... | collective-permute-start | bytes 294920 | tf_op jit(solution)/shard_map/ppermute | solution.py:267
  26.1 36.8 %copy-start.3 = (s32[48]{0:T(128)S(1)}, s32[48]{0:T(128)}, u32[]{:S(2)}) copy-start(s32[48]{0:T(128)} %shard_map.50.table_ref) | copy-start | bytes 580
  26.1 7.6 %collective-permute-start.4 = (f32[2,32,384]{2,1,0:T(8,128)S(1)}, f32[2,32,384]{2,1,0:T(8,128)S(1)}, u32[]{:S(2)}, u32[]{:S(2)}) collective-permute-start(f32[2,32,384]{2,1,0:T(8,128)S(1)} %get-tuple-element.15), channel_id=1, source_target_pairs={{0,192},{16,208},{32,224},{48,240},{64,128},{80,144},{96,160},{112... | collective-permute-start | bytes 294920 | tf_op jit(solution)/shard_map/ppermute | solution.py:267
  33.7 0.7 copy-start.2
  36.5 26.4 %all-to-all-start.1 = ((f32[4,64,512]{2,1,0:T(8,128)}), f32[4,64,512]{2,1,0:T(8,128)S(1)}, u32[]{:S(2)}, u32[]{:S(2)}) async-start(f32[4,64,512]{2,1,0:T(8,128)} %shard_map.55), calls=%async_computation.1 | async-start | bytes 1048576 | tf_op jit(solution)/shard_map/all_to_all | solution.py:274
  47.9 9.0 %collective-permute-start.5 = (f32[32,384]{1,0:T(8,128)S(1)}, f32[32,384]{1,0:T(8,128)S(1)}, u32[]{:S(2)}, u32[]{:S(2)}) collective-permute-start(f32[32,384]{1,0:T(8,128)S(1)} %shard_map.54.after_ref), channel_id=1, source_target_pairs={{0,256},{16,272},{32,288},{48,304},{64,320},{80,336},{96,352},{112... | collective-permute-start | bytes 147464 | tf_op jit(solution)/shard_map/ppermute | solution.py:267
  64.2 15.2 %all-to-all-start.2 = ((f32[4,32,896]{2,1,0:T(8,128)}), f32[4,32,896]{2,1,0:T(8,128)S(1)}, u32[]{:S(2)}, u32[]{:S(2)}) async-start(f32[4,32,896]{2,1,0:T(8,128)} %get-tuple-element.21), calls=%async_computation.2 | async-start | bytes 917504 | tf_op jit(solution)/shard_map/all_to_all | solution.py:274
  68.6 9.2 %collective-permute-start.6 = (f32[1,32,512]{2,1,0:T(8,128)S(1)}, f32[1,32,512]{2,1,0:T(8,128)S(1)}, u32[]{:S(2)}, u32[]{:S(2)}) collective-permute-start(f32[1,32,512]{2,1,0:T(8,128)S(1)} %get-tuple-element.16.first_ref), channel_id=1, source_target_pairs={{0,256},{16,272},{32,288},{48,304},{64,320},{80,336},{96,352},{112... | collective-permute-start | bytes 196616 | tf_op jit(solution)/shard_map/ppermute | solution.py:267
  80.8 31.9 %all-to-all-start.3 = ((f32[4,4,32,896]{3,2,1,0:T(8,128)}), f32[4,4,32,896]{3,2,1,0:T(8,128)S(1)}, u32[]{:S(2)}, u32[]{:S(2)}) async-start(f32[4,4,32,896]{3,2,1,0:T(8,128)} %shard_map.60), calls=%async_computation.3 | async-start | bytes 3670016 | tf_op jit(solution)/shard_map/all_to_all | solution.py:274
  84.4 8.4 %collective-permute-start.7 = (f32[2,32,512]{2,1,0:T(8,128)S(1)}, f32[2,32,512]{2,1,0:T(8,128)S(1)}, u32[]{:S(2)}, u32[]{:S(2)}) collective-permute-start(f32[2,32,512]{2,1,0:T(8,128)S(1)} %shard_map.57.first_ref.after_ref), channel_id=1, source_target_pairs={{0,128},{16,144},{32,160},{48,176},{64,192},{80,208},{96,224},{112... | collective-permute-start | bytes 393224 | tf_op jit(solution)/shard_map/ppermute | solution.py:267
  92.8 7.4 %collective-permute-start.8 = (f32[4,32,512]{2,1,0:T(8,128)S(1)}, f32[4,32,512]{2,1,0:T(8,128)S(1)}, u32[]{:S(2)}, u32[]{:S(2)}) collective-permute-start(f32[4,32,512]{2,1,0:T(8,128)S(1)} %shard_map.58.line_ref), channel_id=1, source_target_pairs={{0,64},{16,80},{32,96},{48,112},{64,0},{80,16},{96,32},{112,48},{1... | collective-permute-start | bytes 786440 | tf_op jit(solution)/shard_map/ppermute | solution.py:267
  100.8 20.8 %collective-permute-start.9 = (f32[2,32,512]{2,1,0:T(8,128)S(1)}, f32[2,32,512]{2,1,0:T(8,128)S(1)}, u32[]{:S(2)}, u32[]{:S(2)}) collective-permute-start(f32[2,32,512]{2,1,0:T(8,128)S(1)} %get-tuple-element.18), channel_id=1, source_target_pairs={{0,16},{16,0},{32,48},{48,32},{64,80},{80,64},{96,112},{112,96},{1... | collective-permute-start | bytes 393224 | tf_op jit(solution)/shard_map/ppermute | solution.py:267
  107.2 14.4 %collective-permute-start.10 = (f32[2,32,512]{2,1,0:T(8,128)S(1)}, f32[2,32,512]{2,1,0:T(8,128)S(1)}, u32[]{:S(2)}, u32[]{:S(2)}) collective-permute-start(f32[2,32,512]{2,1,0:T(8,128)S(1)} %get-tuple-element.19), channel_id=1, source_target_pairs={{0,32},{16,48},{32,0},{48,16},{64,96},{80,112},{96,64},{112,80},{1... | collective-permute-start | bytes 393224 | tf_op jit(solution)/shard_map/ppermute | solution.py:267
  109.9 11.7 %collective-permute-start.11 = (f32[2,32,512]{2,1,0:T(8,128)S(1)}, f32[2,32,512]{2,1,0:T(8,128)S(1)}, u32[]{:S(2)}, u32[]{:S(2)}) collective-permute-start(f32[2,32,512]{2,1,0:T(8,128)S(1)} %get-tuple-element.20), channel_id=1, source_target_pairs={{0,48},{16,32},{32,16},{48,0},{64,112},{80,96},{96,80},{112,64},{1... | collective-permute-start | bytes 393224 | tf_op jit(solution)/shard_map/ppermute | solution.py:267

commit v6 on v5

--- a/solution.py
+++ b/solution.py
@@ -187,11 +187,12 @@
 
 def product(a, b):
     (a_high, a_low), (b_high, b_low) = a, b
-    return jnp.dot(
-        jnp.concatenate([a_high, a_high, a_low], axis=1),
-        jnp.concatenate([b_high, b_low, b_high], axis=0),
-        preferred_element_type=f32,
-    )
+    half = a_high.shape[0] // 2
+    left = jnp.concatenate([a_high, a_high, a_low], axis=1)
+    right = jnp.concatenate([b_high, b_low, b_high], axis=0)
+    top = jnp.dot(left[:half], right, preferred_element_type=f32)
+    corner = jnp.dot(left[half:], right[:, half:], preferred_element_type=f32)
+    return jnp.concatenate([top, jnp.concatenate([top[:, half:].T, corner], axis=1)], axis=0)
 
 
 def copies_kernel(part_ref, after_ref, out_ref, sems):
@@ -366,7 +367,7 @@
             stack_kernel,
             shape(2 * line.shape[0], rows, size),
             [VMEM] * 2,
-            (0, 4 * size * rows * 8),
+            (2 * (60 if bit == 2 else 0) * size**3, 4 * size * rows * 8),
             line,
             across(line, GROUP * bit),
         )

time: 124 us -> 121 us (0.976)
  starting transfers between devices: 76.5 us -> 74.7 us
    ppermute x12, starting transfers between devices: 53 us -> 51.2 us  [across(): return lax.ppermute(x, 'pre', [(i, i ^ k) for i in range(blocks)])]
    ppermute x12, waiting for transfers between devices: 15.7 us -> 14.3 us  [across(): return lax.ppermute(x, 'pre', [(i, i ^ k) for i in range(blocks)])]
  transfers between devices with their start and end apart: 16 -> 16, of which waited for: 9 -> 9; matrix products, arithmetic and copies ran while one was open for 0% -> 0% of each run, Pallas kernels for 12% -> 13%
where the time goes in v6:
time: 121 us; the launch traced here: 120 us
  starting transfers between devices  74.7 us (62%)
  waiting for transfers between devices  23.5 us (19%)
  Pallas kernels  19.4 us (16%)
  local copies, waits for them, and re-layouts  1.32 us (1%)
    ppermute x12, starting transfers between devices, across(): return lax.ppermute(x, 'pre', [(i, i ^ k) for i in range(blocks)])  51.2 us
    all_to_all x4, starting transfers between devices, exchange(): return lax.all_to_all(x, 'rep', 0, 0, tiled=True, axis_index_groups=which)  23.5 us
    pallas_call x12, Pallas kernels, call(): pl.pallas_call(kernel, out_shape=out_shape, in_specs=in_specs, out_specs=...  18 us
    ppermute x12, waiting for transfers between devices, across(): return lax.ppermute(x, 'pre', [(i, i ^ k) for i in range(blocks)])  14.3 us
    all_to_all x4, waiting for transfers between devices, exchange(): return lax.all_to_all(x, 'rep', 0, 0, tiled=True, axis_index_groups=which)  9.24 us
  transfers between devices with their start and end apart: 16, of which 9 were waited for; matrix products, arithmetic and copies ran while one was open for 0% of the time, Pallas kernels for 13%

profile of v6, /device:TPU:1, one launch (start us, length us, event | category | flops | bytes accessed | tf_op | source)
XLA Modules:
  0.0 119.8 jit_solution(13046439103032829132)
XLA Ops:
  0.6 4.8 %collective-permute-start = (f32[2,32,512]{2,1,0:T(8,128)}, f32[2,32,512]{2,1,0:T(8,128)S(1)}, u32[]{:S(2)}, u32[]{:S(2)}) collective-permute-start(f32[2,32,512]{2,1,0:T(8,128)} %bitcast.5), channel_id=1, source_target_pairs={{0,32},{16,48},{32,0},{48,16},{64,96},{80,112},{96,64},{112,80},{1... | collective-permute-start | bytes 393224 | tf_op jit(solution)/shard_map/ppermute | solution.py:268
  5.5 3.1 %shard_map.51 = f32[4,4,64,512]{3,2,1,0:T(8,128)} custom-call(bf16[2,512,512]{2,1,0:T(8,128)(2,1)} %bitcast.8), custom_call_target="tpu_custom_call" | custom-call | flops 536870912 | bytes 4194304 | tf_op jit(solution)/shard_map/pallas_call | solution.py:28
  8.5 0.0 copy-start
  8.6 4.2 %all-to-all-start = ((f32[4,4,64,512]{3,2,1,0:T(8,128)}), f32[4,4,64,512]{3,2,1,0:T(8,128)S(1)}, u32[]{:S(2)}, u32[]{:S(2)}) async-start(f32[4,4,64,512]{3,2,1,0:T(8,128)} %shard_map.51), calls=%async_computation | async-start | bytes 4194304 | tf_op jit(solution)/shard_map/all_to_all | solution.py:275
  12.7 0.0 collective-permute-done.held_z_ref
  12.7 0.0 copy-done
  12.8 5.5 %collective-permute-start.1 = (f32[2,2,32,384]{3,2,1,0:T(8,128)S(1)}, f32[2,2,32,384]{3,2,1,0:T(8,128)S(1)}, u32[]{:S(2)}, u32[]{:S(2)}) collective-permute-start(f32[2,2,32,384]{3,2,1,0:T(8,128)S(1)} %shard_map.52.kept_ref), channel_id=1, source_target_pairs={{0,16},{16,0},{32,48},{48,32},{64,80},{80,64},{96,112},{112,96},{1... | collective-permute-start | bytes 589832 | tf_op jit(solution)/shard_map/ppermute | solution.py:268
  18.3 1.4 %shard_map.50.table_ref = s32[48]{0:T(128)} custom-call(s32[1]{0:T(128)} %bitcast.me_ref, s32[32]{0:T(128)} %owner_ref.1), custom_call_target="tpu_custom_call" | custom-call | tf_op jit(solution)/shard_map/pallas_call | solution.py:279
  19.7 0.0 collective-permute-done.1.core_ref
  19.7 0.0 copy-start.1
  19.8 0.6 copy-done.1
  20.4 0.6 shard_map.53
  21.0 1.9 %collective-permute-start.2 = (f32[2,32,384]{2,1,0:T(8,128)S(1)}, f32[2,32,384]{2,1,0:T(8,128)S(1)}, u32[]{:S(2)}, u32[]{:S(2)}) collective-permute-start(f32[2,32,384]{2,1,0:T(8,128)S(1)} %get-tuple-element.13), channel_id=1, source_target_pairs={{0,64},{16,80},{32,96},{48,112},{64,0},{80,16},{96,32},{112,48},{1... | collective-permute-start | bytes 294920 | tf_op jit(solution)/shard_map/ppermute | solution.py:268
  22.9 3.2 %collective-permute-start.3 = (f32[2,32,384]{2,1,0:T(8,128)S(1)}, f32[2,32,384]{2,1,0:T(8,128)S(1)}, u32[]{:S(2)}, u32[]{:S(2)}) collective-permute-start(f32[2,32,384]{2,1,0:T(8,128)S(1)} %get-tuple-element.14), channel_id=1, source_target_pairs={{0,128},{16,144},{32,160},{48,176},{64,192},{80,208},{96,224},{112... | collective-permute-start | bytes 294920 | tf_op jit(solution)/shard_map/ppermute | solution.py:268
  26.1 0.0 copy-start.3
  26.1 4.2 %collective-permute-start.4 = (f32[2,32,384]{2,1,0:T(8,128)S(1)}, f32[2,32,384]{2,1,0:T(8,128)S(1)}, u32[]{:S(2)}, u32[]{:S(2)}) collective-permute-start(f32[2,32,384]{2,1,0:T(8,128)S(1)} %get-tuple-element.15), channel_id=1, source_target_pairs={{0,192},{16,208},{32,224},{48,240},{64,128},{80,144},{96,160},{112... | collective-permute-start | bytes 294920 | tf_op jit(solution)/shard_map/ppermute | solution.py:268
  30.3 0.0 collective-permute-done.2.near1.refs_0_
  30.3 1.9 %collective-permute-done.3.near2.refs_1_ = f32[2,32,384]{2,1,0:T(8,128)S(1)} collective-permute-done((f32[2,32,384]{2,1,0:T(8,128)S(1)}, f32[2,32,384]{2,1,0:T(8,128)S(1)}, u32[]{:S(2)}, u32[]{:S(2)}) %collective-permute-start.3) | collective-permute-done | bytes 98336 | tf_op jit(solution)/shard_map/ppermute | solution.py:268
  32.2 1.4 %collective-permute-done.4.near3.refs_2_ = f32[2,32,384]{2,1,0:T(8,128)S(1)} collective-permute-done((f32[2,32,384]{2,1,0:T(8,128)S(1)}, f32[2,32,384]{2,1,0:T(8,128)S(1)}, u32[]{:S(2)}, u32[]{:S(2)}) %collective-permute-start.4) | collective-permute-done | bytes 98336 | tf_op jit(solution)/shard_map/ppermute | solution.py:268
  33.7 0.0 copy-start.2
  33.7 0.7 copy-done.2
  34.3 0.6 shard_map.54.after_ref
  34.9 0.7 all-to-all-done.parts_ref
  35.5 0.9 shard_map.55
  36.5 11.4 %all-to-all-start.1 = ((f32[4,64,512]{2,1,0:T(8,128)}), f32[4,64,512]{2,1,0:T(8,128)S(1)}, u32[]{:S(2)}, u32[]{:S(2)}) async-start(f32[4,64,512]{2,1,0:T(8,128)} %shard_map.55), calls=%async_computation.1 | async-start | bytes 1048576 | tf_op jit(solution)/shard_map/all_to_all | solution.py:275
  47.9 7.4 %collective-permute-start.5 = (f32[32,384]{1,0:T(8,128)S(1)}, f32[32,384]{1,0:T(8,128)S(1)}, u32[]{:S(2)}, u32[]{:S(2)}) collective-permute-start(f32[32,384]{1,0:T(8,128)S(1)} %shard_map.54.after_ref), channel_id=1, source_target_pairs={{0,256},{16,272},{32,288},{48,304},{64,320},{80,336},{96,352},{112... | collective-permute-start | bytes 147464 | tf_op jit(solution)/shard_map/ppermute | solution.py:268
  55.3 1.5 %collective-permute-done.5.refs_3_ = f32[32,384]{1,0:T(8,128)S(1)} collective-permute-done((f32[32,384]{1,0:T(8,128)S(1)}, f32[32,384]{1,0:T(8,128)S(1)}, u32[]{:S(2)}, u32[]{:S(2)}) %collective-permute-start.5) | collective-permute-done | bytes 49184 | tf_op jit(solution)/shard_map/ppermute | solution.py:268
  56.8 6.0 %all-to-all-done.1.sums_ref = f32[4,64,512]{2,1,0:T(8,128)S(1)} async-done(((f32[4,64,512]{2,1,0:T(8,128)}), f32[4,64,512]{2,1,0:T(8,128)S(1)}, u32[]{:S(2)}, u32[]{:S(2)}) %all-to-all-start.1) | async-done | bytes 524320 | tf_op jit(solution)/shard_map/all_to_all | solution.py:275
  62.9 0.0 copy-done.3
  62.9 1.4 %shard_map.56 = (f32[4,32,896]{2,1,0:T(8,128)}, f32[1,32,512]{2,1,0:T(8,128)S(1)}) custom-call(s32[48]{0:T(128)S(1)} %copy-done.3, s32[1]{0:T(128)} %bitcast.2.place_ref, f32[4,64,512]{2,1,0:T(8,128)S(1)} %all-to-all-done.1.sums_ref, f32[2,2,32,384]{3,2,1,0:T(8,128)S(1)} %shard_map.52.kept_ref, f32[2,2,32,384]{3,2,1,0:T(8,128)S(1)} %collective-permute-done.1.core_ref, ...), custom_call_target="tpu_custom_call" | custom-call | bytes 2949120 | tf_op jit(solution)/shard_map/pallas_call | solution.py:28
  64.2 4.3 %all-to-all-start.2 = ((f32[4,32,896]{2,1,0:T(8,128)}), f32[4,32,896]{2,1,0:T(8,128)S(1)}, u32[]{:S(2)}, u32[]{:S(2)}) async-start(f32[4,32,896]{2,1,0:T(8,128)} %get-tuple-element.21), calls=%async_computation.2 | async-start | bytes 917504 | tf_op jit(solution)/shard_map/all_to_all | solution.py:275
  68.6 7.4 %collective-permute-start.6 = (f32[1,32,512]{2,1,0:T(8,128)S(1)}, f32[1,32,512]{2,1,0:T(8,128)S(1)}, u32[]{:S(2)}, u32[]{:S(2)}) collective-permute-start(f32[1,32,512]{2,1,0:T(8,128)S(1)} %get-tuple-element.16.first_ref), channel_id=1, source_target_pairs={{0,256},{16,272},{32,288},{48,304},{64,320},{80,336},{96,352},{112... | collective-permute-start | bytes 196616 | tf_op jit(solution)/shard_map/ppermute | solution.py:268
  76.0 1.7 %collective-permute-done.6.second_ref = f32[1,32,512]{2,1,0:T(8,128)S(1)} collective-permute-done((f32[1,32,512]{2,1,0:T(8,128)S(1)}, f32[1,32,512]{2,1,0:T(8,128)S(1)}, u32[]{:S(2)}, u32[]{:S(2)}) %collective-permute-start.6) | collective-permute-done | bytes 65568 | tf_op jit(solution)/shard_map/ppermute | solution.py:268
  77.7 5.6 %collective-permute-start.7 = (f32[2,32,512]{2,1,0:T(8,128)S(1)}, f32[2,32,512]{2,1,0:T(8,128)S(1)}, u32[]{:S(2)}, u32[]{:S(2)}) collective-permute-start(f32[2,32,512]{2,1,0:T(8,128)S(1)} %shard_map.57.first_ref.after_ref), channel_id=1, source_target_pairs={{0,128},{16,144},{32,160},{48,176},{64,192},{80,208},{96,224},{112... | collective-permute-start | bytes 393224 | tf_op jit(solution)/shard_map/ppermute | solution.py:268
  83.4 0.0 all-to-all-done.2.part_ref
  83.4 1.3 %shard_map.60 = f32[4,4,32,896]{3,2,1,0:T(8,128)} custom-call(f32[4,32,896]{2,1,0:T(8,128)S(1)} %all-to-all-done.2.part_ref, f32[2,32,512]{2,1,0:T(8,128)S(1)} %shard_map.57.first_ref.after_ref), custom_call_target="tpu_custom_call" | custom-call | bytes 2621440 | tf_op jit(solution)/shard_map/pallas_call | solution.py:28
  84.7 3.6 %all-to-all-start.3 = ((f32[4,4,32,896]{3,2,1,0:T(8,128)}), f32[4,4,32,896]{3,2,1,0:T(8,128)S(1)}, u32[]{:S(2)}, u32[]{:S(2)}) async-start(f32[4,4,32,896]{3,2,1,0:T(8,128)} %shard_map.60), calls=%async_computation.3 | async-start | bytes 3670016 | tf_op jit(solution)/shard_map/all_to_all | solution.py:275
  88.3 0.9 collective-permute-done.7.second_ref
  89.2 1.9 %collective-permute-start.8 = (f32[4,32,512]{2,1,0:T(8,128)S(1)}, f32[4,32,512]{2,1,0:T(8,128)S(1)}, u32[]{:S(2)}, u32[]{:S(2)}) collective-permute-start(f32[4,32,512]{2,1,0:T(8,128)S(1)} %shard_map.58.line_ref), channel_id=1, source_target_pairs={{0,64},{16,80},{32,96},{48,112},{64,0},{80,16},{96,32},{112,48},{1... | collective-permute-start | bytes 786440 | tf_op jit(solution)/shard_map/ppermute | solution.py:268
  91.1 6.8 %collective-permute-done.8.far_ref = f32[4,32,512]{2,1,0:T(8,128)S(1)} collective-permute-done((f32[4,32,512]{2,1,0:T(8,128)S(1)}, f32[4,32,512]{2,1,0:T(8,128)S(1)}, u32[]{:S(2)}, u32[]{:S(2)}) %collective-permute-start.8) | collective-permute-done | bytes 262176 | tf_op jit(solution)/shard_map/ppermute | solution.py:268
  97.9 0.6 shard_map.59
  98.6 3.8 %collective-permute-start.9 = (f32[2,32,512]{2,1,0:T(8,128)S(1)}, f32[2,32,512]{2,1,0:T(8,128)S(1)}, u32[]{:S(2)}, u32[]{:S(2)}) collective-permute-start(f32[2,32,512]{2,1,0:T(8,128)S(1)} %get-tuple-element.18), channel_id=1, source_target_pairs={{0,16},{16,0},{32,48},{48,32},{64,80},{80,64},{96,112},{112,96},{1... | collective-permute-start | bytes 393224 | tf_op jit(solution)/shard_map/ppermute | solution.py:268
  102.3 1.9 %collective-permute-start.10 = (f32[2,32,512]{2,1,0:T(8,128)S(1)}, f32[2,32,512]{2,1,0:T(8,128)S(1)}, u32[]{:S(2)}, u32[]{:S(2)}) collective-permute-start(f32[2,32,512]{2,1,0:T(8,128)S(1)} %get-tuple-element.19), channel_id=1, source_target_pairs={{0,32},{16,48},{32,0},{48,16},{64,96},{80,112},{96,64},{112,80},{1... | collective-permute-start | bytes 393224 | tf_op jit(solution)/shard_map/ppermute | solution.py:268
  104.2 3.5 %collective-permute-start.11 = (f32[2,32,512]{2,1,0:T(8,128)S(1)}, f32[2,32,512]{2,1,0:T(8,128)S(1)}, u32[]{:S(2)}, u32[]{:S(2)}) collective-permute-start(f32[2,32,512]{2,1,0:T(8,128)S(1)} %get-tuple-element.20), channel_id=1, source_target_pairs={{0,48},{16,32},{32,16},{48,0},{64,112},{80,96},{96,80},{112,64},{1... | collective-permute-start | bytes 393224 | tf_op jit(solution)/shard_map/ppermute | solution.py:268
  107.8 2.6 %all-to-all-done.3.all_ref = f32[4,4,32,896]{3,2,1,0:T(8,128)S(1)} async-done(((f32[4,4,32,896]{3,2,1,0:T(8,128)}), f32[4,4,32,896]{3,2,1,0:T(8,128)S(1)}, u32[]{:S(2)}, u32[]{:S(2)}) %all-to-all-start.3) | async-done | bytes 1835040 | tf_op jit(solution)/shard_map/all_to_all | solution.py:275
  110.3 8.3 %shard_map.61 = (bf16[1,32,512]{2,1,0:T(8,128)(2,1)}, f32[8,128]{1,0:T(8,128)S(1)}) custom-call(s32[1]{0:T(128)} %bitcast.2.place_ref, f32[4,4,32,896]{3,2,1,0:T(8,128)S(1)} %all-to-all-done.3.all_ref, f32[2,32,512]{2,1,0:T(8,128)S(1)} %get-tuple-element.17.after_ref.got0), custom_call_target="tpu_custom_call" | custom-call | flops 5368709120 | bytes 2097152 | tf_op jit(solution)/shard_map/pallas_call | solution.py:28
  118.6 0.0 collective-permute-done.9.got1
  118.6 0.0 collective-permute-done.10.got2
  118.6 0.0 collective-permute-done.11.got3
  118.6 1.2 %shard_map.62 = f32[2,32,512]{2,1,0:T(8,128)} custom-call(s32[48]{0:T(128)S(1)} %copy-done.3, f32[2,32,512]{2,1,0:T(8,128)S(1)} %bitcast.7, f32[2,32,512]{2,1,0:T(8,128)S(1)} %get-tuple-element.17.after_ref.got0, f32[2,32,512]{2,1,0:T(8,128)S(1)} %collective-permute-done.9.got1, f32[2,32,512]{2,1,0:T(8,128)S(1)} %collective-permute-done.10.got2, ...), custom_call_target="tpu_custom_call" | custom-call | bytes 524288 | tf_op jit(solution)/shard_map/pallas_call | solution.py:28
  (3 shorter events, 0.1 us)
Async XLA Ops:
  0.6 12.1 %collective-permute-start = (f32[2,32,512]{2,1,0:T(8,128)}, f32[2,32,512]{2,1,0:T(8,128)S(1)}, u32[]{:S(2)}, u32[]{:S(2)}) collective-permute-start(f32[2,32,512]{2,1,0:T(8,128)} %bitcast.5), channel_id=1, source_target_pairs={{0,32},{16,48},{32,0},{48,16},{64,96},{80,112},{96,64},{112,80},{1... | collective-permute-start | bytes 393224 | tf_op jit(solution)/shard_map/ppermute | solution.py:268
  8.5 4.2 %copy-start = (f32[1,2,32,512]{3,2,1,0:T(8,128)S(1)}, f32[1,2,32,512]{3,2,1,0:T(8,128)}, u32[]{:S(2)}) copy-start(f32[1,2,32,512]{3,2,1,0:T(8,128)} %param.5) | copy-start | bytes 393220
  8.6 27.0 %all-to-all-start = ((f32[4,4,64,512]{3,2,1,0:T(8,128)}), f32[4,4,64,512]{3,2,1,0:T(8,128)S(1)}, u32[]{:S(2)}, u32[]{:S(2)}) async-start(f32[4,4,64,512]{3,2,1,0:T(8,128)} %shard_map.51), calls=%async_computation | async-start | bytes 4194304 | tf_op jit(solution)/shard_map/all_to_all | solution.py:275
  12.8 7.0 %collective-permute-start.1 = (f32[2,2,32,384]{3,2,1,0:T(8,128)S(1)}, f32[2,2,32,384]{3,2,1,0:T(8,128)S(1)}, u32[]{:S(2)}, u32[]{:S(2)}) collective-permute-start(f32[2,2,32,384]{3,2,1,0:T(8,128)S(1)} %shard_map.52.kept_ref), channel_id=1, source_target_pairs={{0,16},{16,0},{32,48},{48,32},{64,80},{80,64},{96,112},{112,96},{1... | collective-permute-start | bytes 589832 | tf_op jit(solution)/shard_map/ppermute | solution.py:268
  19.7 0.7 copy-start.1
  21.0 9.3 %collective-permute-start.2 = (f32[2,32,384]{2,1,0:T(8,128)S(1)}, f32[2,32,384]{2,1,0:T(8,128)S(1)}, u32[]{:S(2)}, u32[]{:S(2)}) collective-permute-start(f32[2,32,384]{2,1,0:T(8,128)S(1)} %get-tuple-element.13), channel_id=1, source_target_pairs={{0,64},{16,80},{32,96},{48,112},{64,0},{80,16},{96,32},{112,48},{1... | collective-permute-start | bytes 294920 | tf_op jit(solution)/shard_map/ppermute | solution.py:268
  22.9 9.3 %collective-permute-start.3 = (f32[2,32,384]{2,1,0:T(8,128)S(1)}, f32[2,32,384]{2,1,0:T(8,128)S(1)}, u32[]{:S(2)}, u32[]{:S(2)}) collective-permute-start(f32[2,32,384]{2,1,0:T(8,128)S(1)} %get-tuple-element.14), channel_id=1, source_target_pairs={{0,128},{16,144},{32,160},{48,176},{64,192},{80,208},{96,224},{112... | collective-permute-start | bytes 294920 | tf_op jit(solution)/shard_map/ppermute | solution.py:268
  26.1 36.8 %copy-start.3 = (s32[48]{0:T(128)S(1)}, s32[48]{0:T(128)}, u32[]{:S(2)}) copy-start(s32[48]{0:T(128)} %shard_map.50.table_ref) | copy-start | bytes 580
  26.1 7.6 %collective-permute-start.4 = (f32[2,32,384]{2,1,0:T(8,128)S(1)}, f32[2,32,384]{2,1,0:T(8,128)S(1)}, u32[]{:S(2)}, u32[]{:S(2)}) collective-permute-start(f32[2,32,384]{2,1,0:T(8,128)S(1)} %get-tuple-element.15), channel_id=1, source_target_pairs={{0,192},{16,208},{32,224},{48,240},{64,128},{80,144},{96,160},{112... | collective-permute-start | bytes 294920 | tf_op jit(solution)/shard_map/ppermute | solution.py:268
  33.7 0.7 copy-start.2
  36.5 26.4 %all-to-all-start.1 = ((f32[4,64,512]{2,1,0:T(8,128)}), f32[4,64,512]{2,1,0:T(8,128)S(1)}, u32[]{:S(2)}, u32[]{:S(2)}) async-start(f32[4,64,512]{2,1,0:T(8,128)} %shard_map.55), calls=%async_computation.1 | async-start | bytes 1048576 | tf_op jit(solution)/shard_map/all_to_all | solution.py:275
  47.9 9.0 %collective-permute-start.5 = (f32[32,384]{1,0:T(8,128)S(1)}, f32[32,384]{1,0:T(8,128)S(1)}, u32[]{:S(2)}, u32[]{:S(2)}) collective-permute-start(f32[32,384]{1,0:T(8,128)S(1)} %shard_map.54.after_ref), channel_id=1, source_target_pairs={{0,256},{16,272},{32,288},{48,304},{64,320},{80,336},{96,352},{112... | collective-permute-start | bytes 147464 | tf_op jit(solution)/shard_map/ppermute | solution.py:268
  64.2 19.1 %all-to-all-start.2 = ((f32[4,32,896]{2,1,0:T(8,128)}), f32[4,32,896]{2,1,0:T(8,128)S(1)}, u32[]{:S(2)}, u32[]{:S(2)}) async-start(f32[4,32,896]{2,1,0:T(8,128)} %get-tuple-element.21), calls=%async_computation.2 | async-start | bytes 917504 | tf_op jit(solution)/shard_map/all_to_all | solution.py:275
  68.6 9.2 %collective-permute-start.6 = (f32[1,32,512]{2,1,0:T(8,128)S(1)}, f32[1,32,512]{2,1,0:T(8,128)S(1)}, u32[]{:S(2)}, u32[]{:S(2)}) collective-permute-start(f32[1,32,512]{2,1,0:T(8,128)S(1)} %get-tuple-element.16.first_ref), channel_id=1, source_target_pairs={{0,256},{16,272},{32,288},{48,304},{64,320},{80,336},{96,352},{112... | collective-permute-start | bytes 196616 | tf_op jit(solution)/shard_map/ppermute | solution.py:268
  77.7 11.4 %collective-permute-start.7 = (f32[2,32,512]{2,1,0:T(8,128)S(1)}, f32[2,32,512]{2,1,0:T(8,128)S(1)}, u32[]{:S(2)}, u32[]{:S(2)}) collective-permute-start(f32[2,32,512]{2,1,0:T(8,128)S(1)} %shard_map.57.first_ref.after_ref), channel_id=1, source_target_pairs={{0,128},{16,144},{32,160},{48,176},{64,192},{80,208},{96,224},{112... | collective-permute-start | bytes 393224 | tf_op jit(solution)/shard_map/ppermute | solution.py:268
  84.7 25.7 %all-to-all-start.3 = ((f32[4,4,32,896]{3,2,1,0:T(8,128)}), f32[4,4,32,896]{3,2,1,0:T(8,128)S(1)}, u32[]{:S(2)}, u32[]{:S(2)}) async-start(f32[4,4,32,896]{3,2,1,0:T(8,128)} %shard_map.60), calls=%async_computation.3 | async-start | bytes 3670016 | tf_op jit(solution)/shard_map/all_to_all | solution.py:275
  89.2 8.8 %collective-permute-start.8 = (f32[4,32,512]{2,1,0:T(8,128)S(1)}, f32[4,32,512]{2,1,0:T(8,128)S(1)}, u32[]{:S(2)}, u32[]{:S(2)}) collective-permute-start(f32[4,32,512]{2,1,0:T(8,128)S(1)} %shard_map.58.line_ref), channel_id=1, source_target_pairs={{0,64},{16,80},{32,96},{48,112},{64,0},{80,16},{96,32},{112,48},{1... | collective-permute-start | bytes 786440 | tf_op jit(solution)/shard_map/ppermute | solution.py:268
  98.6 20.0 %collective-permute-start.9 = (f32[2,32,512]{2,1,0:T(8,128)S(1)}, f32[2,32,512]{2,1,0:T(8,128)S(1)}, u32[]{:S(2)}, u32[]{:S(2)}) collective-permute-start(f32[2,32,512]{2,1,0:T(8,128)S(1)} %get-tuple-element.18), channel_id=1, source_target_pairs={{0,16},{16,0},{32,48},{48,32},{64,80},{80,64},{96,112},{112,96},{1... | collective-permute-start | bytes 393224 | tf_op jit(solution)/shard_map/ppermute | solution.py:268
  102.3 16.3 %collective-permute-start.10 = (f32[2,32,512]{2,1,0:T(8,128)S(1)}, f32[2,32,512]{2,1,0:T(8,128)S(1)}, u32[]{:S(2)}, u32[]{:S(2)}) collective-permute-start(f32[2,32,512]{2,1,0:T(8,128)S(1)} %get-tuple-element.19), channel_id=1, source_target_pairs={{0,32},{16,48},{32,0},{48,16},{64,96},{80,112},{96,64},{112,80},{1... | collective-permute-start | bytes 393224 | tf_op jit(solution)/shard_map/ppermute | solution.py:268
  104.2 14.4 %collective-permute-start.11 = (f32[2,32,512]{2,1,0:T(8,128)S(1)}, f32[2,32,512]{2,1,0:T(8,128)S(1)}, u32[]{:S(2)}, u32[]{:S(2)}) collective-permute-start(f32[2,32,512]{2,1,0:T(8,128)S(1)} %get-tuple-element.20), channel_id=1, source_target_pairs={{0,48},{16,32},{32,16},{48,0},{64,112},{80,96},{96,80},{112,64},{1... | collective-permute-start | bytes 393224 | tf_op jit(solution)/shard_map/ppermute | solution.py:268

commit v7 on v6

--- a/solution.py
+++ b/solution.py
@@ -147,16 +147,29 @@
     out_ref[...] = pick(table_ref, 6, kept_ref, core_ref, (near1, near2, near3))
 
 
+def packed_rows(rows, size):
+    return 2 * rows + rows // 2 + size // LANES * rows
+
+
 def stat_kernel(table_ref, place_ref, sums_ref, kept_ref, core_ref, *refs):
-    wide_ref, gram_ref, both_ref = refs[4:]
+    wide_ref, gram_ref, stat_ref, both_ref = refs[4:]
     _, rows, size = gram_ref.shape
     sums = jnp.sum(sums_ref[...], axis=0)
     gram_ref[0] = sums[:rows]
-    keep = size - LANES
     for n, column in enumerate(columns(place_ref[0], rows, size)):
-        both_ref[:, n * LANES : (n + 1) * LANES] = gram_ref[0, :, pl.ds(column, LANES)]
-    both_ref[:, :keep] += pick(table_ref, 7, kept_ref, core_ref, refs[:3], refs[3:4])
-    both_ref[:, keep:] = sums[rows:]
+        stat_ref[:, n * LANES : (n + 1) * LANES] = gram_ref[0, :, pl.ds(column, LANES)]
+    stat = stat_ref[...] + pick(table_ref, 7, kept_ref, core_ref, refs[:3], refs[3:4])
+    both_ref[:rows] = stat[:, :LANES]
+    both_ref[rows : 2 * rows] = stat[:, LANES : 2 * LANES]
+    x, z = place_ref[0] % ACROSS, place_ref[0] // ACROSS
+    third = [stat[:, 2 * LANES + s * rows : 2 * LANES + (s + 1) * rows] for s in range(LANES // rows)]
+    odd = (x + z // 2) % 2
+    half = jnp.where(odd == 0, jnp.concatenate(third[::2], axis=1), jnp.concatenate(third[1::2], axis=1))
+    half = jnp.concatenate([half[: rows // 2], half[rows // 2 :]], axis=1)
+    start = 2 * rows + rows // 2
+    both_ref[2 * rows : start] = half
+    for m in range(size // LANES):
+        both_ref[start + m * rows : start + (m + 1) * rows] = sums[rows:, m * LANES : (m + 1) * LANES]
     wide_ref[...] = jnp.broadcast_to(both_ref[...][None], wide_ref.shape)
 
 
@@ -214,17 +227,31 @@
 def newton_kernel(count, place_ref, all_ref, after_ref, out_ref, end_ref, stat_ref):
     del after_ref
     end_ref[...] = jnp.zeros_like(end_ref)
-    xs, zs, rows, wide = all_ref.shape
+    xs, zs, _, _ = all_ref.shape
     size = stat_ref.shape[1]
-    blocks = size // LANES
+    rows = size // (xs * zs)
+    start = 2 * rows + rows // 2
     place = place_ref[0]
+    block = lambda i: slice(i % zs * LANES, (i % zs + 1) * LANES)
+    third = []
     for z in range(zs):
-        for n in range(blocks - 1):
-            j = (z + n) % blocks
-            part = jnp.concatenate([all_ref[x, z, :, n * LANES : (n + 1) * LANES] for x in range(xs)], axis=0)
-            stat_ref[z * LANES : (z + 1) * LANES, j * LANES : (j + 1) * LANES] = part
+        for n in range(2):
+            part = jnp.concatenate([all_ref[x, z, n * rows : (n + 1) * rows] for x in range(xs)], axis=0)
+            stat_ref[block(z), block(z + n)] = part
             if n == 1:
-                stat_ref[j * LANES : (j + 1) * LANES, z * LANES : (z + 1) * LANES] = part.T
+                stat_ref[block(z + n), block(z)] = part.T
+        strips = []
+        for x in range(xs):
+            half = all_ref[x, z, 2 * rows : start]
+            half = jnp.concatenate([half[:, : LANES // 2], half[:, LANES // 2 :]], axis=0)
+            blank = jnp.zeros((rows, rows), f32)
+            pieces = [half[:, :rows], blank, half[:, rows:], blank]
+            strips.append(jnp.concatenate(pieces if (x + z // 2) % 2 == 0 else pieces[1:2] + pieces[:1] + pieces[3:] + pieces[2:3], axis=1))
+        third.append(jnp.concatenate(strips, axis=0))
+    for z in range(zs // 2):
+        part = third[z] + third[z + 2].T
+        stat_ref[block(z), block(z + 2)] = part
+        stat_ref[block(z + 2), block(z)] = part.T
     stat = stat_ref[...]
     diagonal = lax.broadcasted_iota(jnp.int32, (size, size), 0) == lax.broadcasted_iota(jnp.int32, (size, size), 1)
     plus = lambda a, m: jnp.where(diagonal, m + a, m)
@@ -249,8 +276,13 @@
     for _ in range(4):
         last = 1.25 * last - 0.25 * thin_product(last, parts_of)
     thin = (1.25 * thin - 0.25 * last) * jnp.exp(-0.25 * jnp.log(scale))
-    mean = jnp.concatenate([all_ref[x, z, :, size - LANES :] for z in range(zs) for x in range(xs)], axis=0)
-    mean = (mean / count).astype(bf16)
+    mean = [
+        jnp.concatenate(
+            [all_ref[x, z, start + m * rows : start + (m + 1) * rows] for z in range(zs) for x in range(xs)], axis=0
+        )
+        for m in range(size // LANES)
+    ]
+    mean = (jnp.concatenate(mean, axis=1) / count).astype(bf16)
     out_ref[0] = jnp.dot(thin.astype(bf16), mean, preferred_element_type=f32).astype(bf16)
 
 
@@ -347,7 +379,7 @@
     far = across(far, 4 * GROUP)
     both, gram = call(
         stat_kernel,
-        [shape(zs, rows, 2 * size - LANES), shape(1, rows, size)],
+        [shape(zs, packed_rows(rows, size), LANES), shape(1, rows, size)],
         [SMEM, SMEM] + [VMEM] * 7,
         (0, 4 * size * rows * 45),
         table,
@@ -357,7 +389,10 @@
         core,
         *near,
         far,
-        scratch=[pltpu.VMEM((rows, 2 * size - LANES), f32)],
+        scratch=[
+            pltpu.VMEM((rows, size - LANES), f32),
+            pltpu.VMEM((packed_rows(rows, size), LANES), f32),
+        ],
     )
     both = exchange(both, z_groups)
     line = gram
@@ -374,7 +409,7 @@
         lines.append(line)
     both = call(
         copies_kernel,
-        shape(ACROSS, zs, rows, 2 * size - LANES),
+        shape(ACROSS, zs, packed_rows(rows, size), LANES),
         [VMEM, ANY],
         (0, 4 * size * rows * 40),
         both,

time: 121 us -> 120 us (level)
  waiting for transfers between devices: 23.5 us -> 22.1 us
    all_to_all x4, waiting for transfers between devices: 9.24 us -> 7.79 us  [exchange(): return lax.all_to_all(x, 'rep', 0, 0, tiled=True, axis_index_groups=which)]
  transfers between devices with their start and end apart: 16 -> 16, of which waited for: 9 -> 9; matrix products, arithmetic and copies ran while one was open for 0% -> 0% of each run, Pallas kernels for 13% -> 14%
where the time goes in v7:
time: 120 us; the launch traced here: 119 us
  starting transfers between devices  74.7 us (62%)
  waiting for transfers between devices  22.1 us (18%)
  Pallas kernels  19.8 us (16%)
  local copies, waits for them, and re-layouts  1.32 us (1%)
    ppermute x12, starting transfers between devices, across(): return lax.ppermute(x, 'pre', [(i, i ^ k) for i in range(blocks)])  51.2 us
    all_to_all x4, starting transfers between devices, exchange(): return lax.all_to_all(x, 'rep', 0, 0, tiled=True, axis_index_groups=which)  23.5 us
    pallas_call x12, Pallas kernels, call(): pl.pallas_call(kernel, out_shape=out_shape, in_specs=in_specs, out_specs=...  18.4 us
    ppermute x12, waiting for transfers between devices, across(): return lax.ppermute(x, 'pre', [(i, i ^ k) for i in range(blocks)])  14.3 us
    all_to_all x4, waiting for transfers between devices, exchange(): return lax.all_to_all(x, 'rep', 0, 0, tiled=True, axis_index_groups=which)  7.79 us
  transfers between devices with their start and end apart: 16, of which 9 were waited for; matrix products, arithmetic and copies ran while one was open for 0% of the time, Pallas kernels for 14%

profile of v7, /device:TPU:1, one launch (start us, length us, event | category | flops | bytes accessed | tf_op | source)
XLA Modules:
  0.0 118.8 jit_solution(8246787880400397280)
XLA Ops:
  0.6 4.8 %collective-permute-start = (f32[2,32,512]{2,1,0:T(8,128)}, f32[2,32,512]{2,1,0:T(8,128)S(1)}, u32[]{:S(2)}, u32[]{:S(2)}) collective-permute-start(f32[2,32,512]{2,1,0:T(8,128)} %bitcast.5), channel_id=1, source_target_pairs={{0,32},{16,48},{32,0},{48,16},{64,96},{80,112},{96,64},{112,80},{1... | collective-permute-start | bytes 393224 | tf_op jit(solution)/shard_map/ppermute | solution.py:300
  5.5 3.1 %shard_map.51 = f32[4,4,64,512]{3,2,1,0:T(8,128)} custom-call(bf16[2,512,512]{2,1,0:T(8,128)(2,1)} %bitcast.8), custom_call_target="tpu_custom_call" | custom-call | flops 536870912 | bytes 4194304 | tf_op jit(solution)/shard_map/pallas_call | solution.py:28
  8.5 0.0 copy-start
  8.6 4.2 %all-to-all-start = ((f32[4,4,64,512]{3,2,1,0:T(8,128)}), f32[4,4,64,512]{3,2,1,0:T(8,128)S(1)}, u32[]{:S(2)}, u32[]{:S(2)}) async-start(f32[4,4,64,512]{3,2,1,0:T(8,128)} %shard_map.51), calls=%async_computation | async-start | bytes 4194304 | tf_op jit(solution)/shard_map/all_to_all | solution.py:307
  12.7 0.0 collective-permute-done.held_z_ref
  12.7 0.0 copy-done
  12.8 5.5 %collective-permute-start.1 = (f32[2,2,32,384]{3,2,1,0:T(8,128)S(1)}, f32[2,2,32,384]{3,2,1,0:T(8,128)S(1)}, u32[]{:S(2)}, u32[]{:S(2)}) collective-permute-start(f32[2,2,32,384]{3,2,1,0:T(8,128)S(1)} %shard_map.52.kept_ref), channel_id=1, source_target_pairs={{0,16},{16,0},{32,48},{48,32},{64,80},{80,64},{96,112},{112,96},{1... | collective-permute-start | bytes 589832 | tf_op jit(solution)/shard_map/ppermute | solution.py:300
  18.3 1.4 %shard_map.50.table_ref = s32[48]{0:T(128)} custom-call(s32[1]{0:T(128)} %bitcast.me_ref, s32[32]{0:T(128)} %owner_ref.1), custom_call_target="tpu_custom_call" | custom-call | tf_op jit(solution)/shard_map/pallas_call | solution.py:311
  19.7 0.0 collective-permute-done.1.core_ref
  19.7 0.0 copy-start.1
  19.8 0.6 copy-done.1
  20.4 0.6 shard_map.53
  21.0 1.9 %collective-permute-start.2 = (f32[2,32,384]{2,1,0:T(8,128)S(1)}, f32[2,32,384]{2,1,0:T(8,128)S(1)}, u32[]{:S(2)}, u32[]{:S(2)}) collective-permute-start(f32[2,32,384]{2,1,0:T(8,128)S(1)} %get-tuple-element.13), channel_id=1, source_target_pairs={{0,64},{16,80},{32,96},{48,112},{64,0},{80,16},{96,32},{112,48},{1... | collective-permute-start | bytes 294920 | tf_op jit(solution)/shard_map/ppermute | solution.py:300
  22.9 3.2 %collective-permute-start.3 = (f32[2,32,384]{2,1,0:T(8,128)S(1)}, f32[2,32,384]{2,1,0:T(8,128)S(1)}, u32[]{:S(2)}, u32[]{:S(2)}) collective-permute-start(f32[2,32,384]{2,1,0:T(8,128)S(1)} %get-tuple-element.14), channel_id=1, source_target_pairs={{0,128},{16,144},{32,160},{48,176},{64,192},{80,208},{96,224},{112... | collective-permute-start | bytes 294920 | tf_op jit(solution)/shard_map/ppermute | solution.py:300
  26.1 0.0 copy-start.3
  26.1 4.2 %collective-permute-start.4 = (f32[2,32,384]{2,1,0:T(8,128)S(1)}, f32[2,32,384]{2,1,0:T(8,128)S(1)}, u32[]{:S(2)}, u32[]{:S(2)}) collective-permute-start(f32[2,32,384]{2,1,0:T(8,128)S(1)} %get-tuple-element.15), channel_id=1, source_target_pairs={{0,192},{16,208},{32,224},{48,240},{64,128},{80,144},{96,160},{112... | collective-permute-start | bytes 294920 | tf_op jit(solution)/shard_map/ppermute | solution.py:300
  30.3 0.0 collective-permute-done.2.near1.refs_0_
  30.3 1.9 %collective-permute-done.3.near2.refs_1_ = f32[2,32,384]{2,1,0:T(8,128)S(1)} collective-permute-done((f32[2,32,384]{2,1,0:T(8,128)S(1)}, f32[2,32,384]{2,1,0:T(8,128)S(1)}, u32[]{:S(2)}, u32[]{:S(2)}) %collective-permute-start.3) | collective-permute-done | bytes 98336 | tf_op jit(solution)/shard_map/ppermute | solution.py:300
  32.2 1.4 %collective-permute-done.4.near3.refs_2_ = f32[2,32,384]{2,1,0:T(8,128)S(1)} collective-permute-done((f32[2,32,384]{2,1,0:T(8,128)S(1)}, f32[2,32,384]{2,1,0:T(8,128)S(1)}, u32[]{:S(2)}, u32[]{:S(2)}) %collective-permute-start.4) | collective-permute-done | bytes 98336 | tf_op jit(solution)/shard_map/ppermute | solution.py:300
  33.7 0.0 copy-start.2
  33.7 0.7 copy-done.2
  34.3 0.6 shard_map.54.after_ref
  34.9 0.7 all-to-all-done.parts_ref
  35.5 0.9 shard_map.55
  36.5 11.4 %all-to-all-start.1 = ((f32[4,64,512]{2,1,0:T(8,128)}), f32[4,64,512]{2,1,0:T(8,128)S(1)}, u32[]{:S(2)}, u32[]{:S(2)}) async-start(f32[4,64,512]{2,1,0:T(8,128)} %shard_map.55), calls=%async_computation.1 | async-start | bytes 1048576 | tf_op jit(solution)/shard_map/all_to_all | solution.py:307
  47.9 7.4 %collective-permute-start.5 = (f32[32,384]{1,0:T(8,128)S(1)}, f32[32,384]{1,0:T(8,128)S(1)}, u32[]{:S(2)}, u32[]{:S(2)}) collective-permute-start(f32[32,384]{1,0:T(8,128)S(1)} %shard_map.54.after_ref), channel_id=1, source_target_pairs={{0,256},{16,272},{32,288},{48,304},{64,320},{80,336},{96,352},{112... | collective-permute-start | bytes 147464 | tf_op jit(solution)/shard_map/ppermute | solution.py:300
  55.3 1.5 %collective-permute-done.5.refs_3_ = f32[32,384]{1,0:T(8,128)S(1)} collective-permute-done((f32[32,384]{1,0:T(8,128)S(1)}, f32[32,384]{1,0:T(8,128)S(1)}, u32[]{:S(2)}, u32[]{:S(2)}) %collective-permute-start.5) | collective-permute-done | bytes 49184 | tf_op jit(solution)/shard_map/ppermute | solution.py:300
  56.8 6.0 %all-to-all-done.1.sums_ref = f32[4,64,512]{2,1,0:T(8,128)S(1)} async-done(((f32[4,64,512]{2,1,0:T(8,128)}), f32[4,64,512]{2,1,0:T(8,128)S(1)}, u32[]{:S(2)}, u32[]{:S(2)}) %all-to-all-start.1) | async-done | bytes 524320 | tf_op jit(solution)/shard_map/all_to_all | solution.py:307
  62.9 0.0 copy-done.3
  62.9 1.5 %shard_map.56 = (f32[4,208,128]{2,1,0:T(8,128)}, f32[1,32,512]{2,1,0:T(8,128)S(1)}) custom-call(s32[48]{0:T(128)S(1)} %copy-done.3, s32[1]{0:T(128)} %bitcast.2.place_ref, f32[4,64,512]{2,1,0:T(8,128)S(1)} %all-to-all-done.1.sums_ref, f32[2,2,32,384]{3,2,1,0:T(8,128)S(1)} %shard_map.52.kept_ref, f32[2,2,32,384]{3,2,1,0:T(8,128)S(1)} %collective-permute-done.1.core_ref, ...), custom_call_target="tpu_custom_call" | custom-call | bytes 2949120 | tf_op jit(solution)/shard_map/pallas_call | solution.py:28
  64.3 4.3 %all-to-all-start.2 = ((f32[4,208,128]{2,1,0:T(8,128)}), f32[4,208,128]{2,1,0:T(8,128)S(1)}, u32[]{:S(2)}, u32[]{:S(2)}) async-start(f32[4,208,128]{2,1,0:T(8,128)} %get-tuple-element.21), calls=%async_computation.2 | async-start | bytes 851968 | tf_op jit(solution)/shard_map/all_to_all | solution.py:307
  68.6 7.4 %collective-permute-start.6 = (f32[1,32,512]{2,1,0:T(8,128)S(1)}, f32[1,32,512]{2,1,0:T(8,128)S(1)}, u32[]{:S(2)}, u32[]{:S(2)}) collective-permute-start(f32[1,32,512]{2,1,0:T(8,128)S(1)} %get-tuple-element.16.first_ref), channel_id=1, source_target_pairs={{0,256},{16,272},{32,288},{48,304},{64,320},{80,336},{96,352},{112... | collective-permute-start | bytes 196616 | tf_op jit(solution)/shard_map/ppermute | solution.py:300
  76.1 1.7 %collective-permute-done.6.second_ref = f32[1,32,512]{2,1,0:T(8,128)S(1)} collective-permute-done((f32[1,32,512]{2,1,0:T(8,128)S(1)}, f32[1,32,512]{2,1,0:T(8,128)S(1)}, u32[]{:S(2)}, u32[]{:S(2)}) %collective-permute-start.6) | collective-permute-done | bytes 65568 | tf_op jit(solution)/shard_map/ppermute | solution.py:300
  77.8 5.6 %collective-permute-start.7 = (f32[2,32,512]{2,1,0:T(8,128)S(1)}, f32[2,32,512]{2,1,0:T(8,128)S(1)}, u32[]{:S(2)}, u32[]{:S(2)}) collective-permute-start(f32[2,32,512]{2,1,0:T(8,128)S(1)} %shard_map.57.first_ref.after_ref), channel_id=1, source_target_pairs={{0,128},{16,144},{32,160},{48,176},{64,192},{80,208},{96,224},{112... | collective-permute-start | bytes 393224 | tf_op jit(solution)/shard_map/ppermute | solution.py:300
  83.5 0.0 all-to-all-done.2.part_ref
  83.5 1.3 %shard_map.60 = f32[4,4,208,128]{3,2,1,0:T(8,128)} custom-call(f32[4,208,128]{2,1,0:T(8,128)S(1)} %all-to-all-done.2.part_ref, f32[2,32,512]{2,1,0:T(8,128)S(1)} %shard_map.57.first_ref.after_ref), custom_call_target="tpu_custom_call" | custom-call | bytes 2621440 | tf_op jit(solution)/shard_map/pallas_call | solution.py:28
  84.7 3.6 %all-to-all-start.3 = ((f32[4,4,208,128]{3,2,1,0:T(8,128)}), f32[4,4,208,128]{3,2,1,0:T(8,128)S(1)}, u32[]{:S(2)}, u32[]{:S(2)}) async-start(f32[4,4,208,128]{3,2,1,0:T(8,128)} %shard_map.60), calls=%async_computation.3 | async-start | bytes 3407872 | tf_op jit(solution)/shard_map/all_to_all | solution.py:307
  88.3 0.9 collective-permute-done.7.second_ref
  89.3 1.9 %collective-permute-start.8 = (f32[4,32,512]{2,1,0:T(8,128)S(1)}, f32[4,32,512]{2,1,0:T(8,128)S(1)}, u32[]{:S(2)}, u32[]{:S(2)}) collective-permute-start(f32[4,32,512]{2,1,0:T(8,128)S(1)} %shard_map.58.line_ref), channel_id=1, source_target_pairs={{0,64},{16,80},{32,96},{48,112},{64,0},{80,16},{96,32},{112,48},{1... | collective-permute-start | bytes 786440 | tf_op jit(solution)/shard_map/ppermute | solution.py:300
  91.2 6.8 %collective-permute-done.8.far_ref = f32[4,32,512]{2,1,0:T(8,128)S(1)} collective-permute-done((f32[4,32,512]{2,1,0:T(8,128)S(1)}, f32[4,32,512]{2,1,0:T(8,128)S(1)}, u32[]{:S(2)}, u32[]{:S(2)}) %collective-permute-start.8) | collective-permute-done | bytes 262176 | tf_op jit(solution)/shard_map/ppermute | solution.py:300
  98.0 0.6 shard_map.59
  98.6 3.8 %collective-permute-start.9 = (f32[2,32,512]{2,1,0:T(8,128)S(1)}, f32[2,32,512]{2,1,0:T(8,128)S(1)}, u32[]{:S(2)}, u32[]{:S(2)}) collective-permute-start(f32[2,32,512]{2,1,0:T(8,128)S(1)} %get-tuple-element.18), channel_id=1, source_target_pairs={{0,16},{16,0},{32,48},{48,32},{64,80},{80,64},{96,112},{112,96},{1... | collective-permute-start | bytes 393224 | tf_op jit(solution)/shard_map/ppermute | solution.py:300
  102.4 1.9 %collective-permute-start.10 = (f32[2,32,512]{2,1,0:T(8,128)S(1)}, f32[2,32,512]{2,1,0:T(8,128)S(1)}, u32[]{:S(2)}, u32[]{:S(2)}) collective-permute-start(f32[2,32,512]{2,1,0:T(8,128)S(1)} %get-tuple-element.19), channel_id=1, source_target_pairs={{0,32},{16,48},{32,0},{48,16},{64,96},{80,112},{96,64},{112,80},{1... | collective-permute-start | bytes 393224 | tf_op jit(solution)/shard_map/ppermute | solution.py:300
  104.3 3.5 %collective-permute-start.11 = (f32[2,32,512]{2,1,0:T(8,128)S(1)}, f32[2,32,512]{2,1,0:T(8,128)S(1)}, u32[]{:S(2)}, u32[]{:S(2)}) collective-permute-start(f32[2,32,512]{2,1,0:T(8,128)S(1)} %get-tuple-element.20), channel_id=1, source_target_pairs={{0,48},{16,32},{32,16},{48,0},{64,112},{80,96},{96,80},{112,64},{1... | collective-permute-start | bytes 393224 | tf_op jit(solution)/shard_map/ppermute | solution.py:300
  107.9 1.1 all-to-all-done.3.all_ref
  109.0 8.6 %shard_map.61 = (bf16[1,32,512]{2,1,0:T(8,128)(2,1)}, f32[8,128]{1,0:T(8,128)S(1)}) custom-call(s32[1]{0:T(128)} %bitcast.2.place_ref, f32[4,4,208,128]{3,2,1,0:T(8,128)S(1)} %all-to-all-done.3.all_ref, f32[2,32,512]{2,1,0:T(8,128)S(1)} %get-tuple-element.17.after_ref.got0), custom_call_target="tpu_custom_call" | custom-call | flops 5368709120 | bytes 2097152 | tf_op jit(solution)/shard_map/pallas_call | solution.py:28
  117.6 0.0 collective-permute-done.9.got1
  117.6 0.0 collective-permute-done.10.got2
  117.6 0.0 collective-permute-done.11.got3
  117.6 1.2 %shard_map.62 = f32[2,32,512]{2,1,0:T(8,128)} custom-call(s32[48]{0:T(128)S(1)} %copy-done.3, f32[2,32,512]{2,1,0:T(8,128)S(1)} %bitcast.7, f32[2,32,512]{2,1,0:T(8,128)S(1)} %get-tuple-element.17.after_ref.got0, f32[2,32,512]{2,1,0:T(8,128)S(1)} %collective-permute-done.9.got1, f32[2,32,512]{2,1,0:T(8,128)S(1)} %collective-permute-done.10.got2, ...), custom_call_target="tpu_custom_call" | custom-call | bytes 524288 | tf_op jit(solution)/shard_map/pallas_call | solution.py:28
  (3 shorter events, 0.1 us)
Async XLA Ops:
  0.6 12.1 %collective-permute-start = (f32[2,32,512]{2,1,0:T(8,128)}, f32[2,32,512]{2,1,0:T(8,128)S(1)}, u32[]{:S(2)}, u32[]{:S(2)}) collective-permute-start(f32[2,32,512]{2,1,0:T(8,128)} %bitcast.5), channel_id=1, source_target_pairs={{0,32},{16,48},{32,0},{48,16},{64,96},{80,112},{96,64},{112,80},{1... | collective-permute-start | bytes 393224 | tf_op jit(solution)/shard_map/ppermute | solution.py:300
  8.5 4.2 %copy-start = (f32[1,2,32,512]{3,2,1,0:T(8,128)S(1)}, f32[1,2,32,512]{3,2,1,0:T(8,128)}, u32[]{:S(2)}) copy-start(f32[1,2,32,512]{3,2,1,0:T(8,128)} %param.5) | copy-start | bytes 393220
  8.6 27.0 %all-to-all-start = ((f32[4,4,64,512]{3,2,1,0:T(8,128)}), f32[4,4,64,512]{3,2,1,0:T(8,128)S(1)}, u32[]{:S(2)}, u32[]{:S(2)}) async-start(f32[4,4,64,512]{3,2,1,0:T(8,128)} %shard_map.51), calls=%async_computation | async-start | bytes 4194304 | tf_op jit(solution)/shard_map/all_to_all | solution.py:307
  12.8 7.0 %collective-permute-start.1 = (f32[2,2,32,384]{3,2,1,0:T(8,128)S(1)}, f32[2,2,32,384]{3,2,1,0:T(8,128)S(1)}, u32[]{:S(2)}, u32[]{:S(2)}) collective-permute-start(f32[2,2,32,384]{3,2,1,0:T(8,128)S(1)} %shard_map.52.kept_ref), channel_id=1, source_target_pairs={{0,16},{16,0},{32,48},{48,32},{64,80},{80,64},{96,112},{112,96},{1... | collective-permute-start | bytes 589832 | tf_op jit(solution)/shard_map/ppermute | solution.py:300
  19.7 0.7 copy-start.1
  21.0 9.3 %collective-permute-start.2 = (f32[2,32,384]{2,1,0:T(8,128)S(1)}, f32[2,32,384]{2,1,0:T(8,128)S(1)}, u32[]{:S(2)}, u32[]{:S(2)}) collective-permute-start(f32[2,32,384]{2,1,0:T(8,128)S(1)} %get-tuple-element.13), channel_id=1, source_target_pairs={{0,64},{16,80},{32,96},{48,112},{64,0},{80,16},{96,32},{112,48},{1... | collective-permute-start | bytes 294920 | tf_op jit(solution)/shard_map/ppermute | solution.py:300
  22.9 9.3 %collective-permute-start.3 = (f32[2,32,384]{2,1,0:T(8,128)S(1)}, f32[2,32,384]{2,1,0:T(8,128)S(1)}, u32[]{:S(2)}, u32[]{:S(2)}) collective-permute-start(f32[2,32,384]{2,1,0:T(8,128)S(1)} %get-tuple-element.14), channel_id=1, source_target_pairs={{0,128},{16,144},{32,160},{48,176},{64,192},{80,208},{96,224},{112... | collective-permute-start | bytes 294920 | tf_op jit(solution)/shard_map/ppermute | solution.py:300
  26.1 36.8 %copy-start.3 = (s32[48]{0:T(128)S(1)}, s32[48]{0:T(128)}, u32[]{:S(2)}) copy-start(s32[48]{0:T(128)} %shard_map.50.table_ref) | copy-start | bytes 580
  26.1 7.6 %collective-permute-start.4 = (f32[2,32,384]{2,1,0:T(8,128)S(1)}, f32[2,32,384]{2,1,0:T(8,128)S(1)}, u32[]{:S(2)}, u32[]{:S(2)}) collective-permute-start(f32[2,32,384]{2,1,0:T(8,128)S(1)} %get-tuple-element.15), channel_id=1, source_target_pairs={{0,192},{16,208},{32,224},{48,240},{64,128},{80,144},{96,160},{112... | collective-permute-start | bytes 294920 | tf_op jit(solution)/shard_map/ppermute | solution.py:300
  33.7 0.7 copy-start.2
  36.5 26.4 %all-to-all-start.1 = ((f32[4,64,512]{2,1,0:T(8,128)}), f32[4,64,512]{2,1,0:T(8,128)S(1)}, u32[]{:S(2)}, u32[]{:S(2)}) async-start(f32[4,64,512]{2,1,0:T(8,128)} %shard_map.55), calls=%async_computation.1 | async-start | bytes 1048576 | tf_op jit(solution)/shard_map/all_to_all | solution.py:307
  47.9 9.0 %collective-permute-start.5 = (f32[32,384]{1,0:T(8,128)S(1)}, f32[32,384]{1,0:T(8,128)S(1)}, u32[]{:S(2)}, u32[]{:S(2)}) collective-permute-start(f32[32,384]{1,0:T(8,128)S(1)} %shard_map.54.after_ref), channel_id=1, source_target_pairs={{0,256},{16,272},{32,288},{48,304},{64,320},{80,336},{96,352},{112... | collective-permute-start | bytes 147464 | tf_op jit(solution)/shard_map/ppermute | solution.py:300
  64.3 19.1 %all-to-all-start.2 = ((f32[4,208,128]{2,1,0:T(8,128)}), f32[4,208,128]{2,1,0:T(8,128)S(1)}, u32[]{:S(2)}, u32[]{:S(2)}) async-start(f32[4,208,128]{2,1,0:T(8,128)} %get-tuple-element.21), calls=%async_computation.2 | async-start | bytes 851968 | tf_op jit(solution)/shard_map/all_to_all | solution.py:307
  68.6 9.2 %collective-permute-start.6 = (f32[1,32,512]{2,1,0:T(8,128)S(1)}, f32[1,32,512]{2,1,0:T(8,128)S(1)}, u32[]{:S(2)}, u32[]{:S(2)}) collective-permute-start(f32[1,32,512]{2,1,0:T(8,128)S(1)} %get-tuple-element.16.first_ref), channel_id=1, source_target_pairs={{0,256},{16,272},{32,288},{48,304},{64,320},{80,336},{96,352},{112... | collective-permute-start | bytes 196616 | tf_op jit(solution)/shard_map/ppermute | solution.py:300
  77.8 11.4 %collective-permute-start.7 = (f32[2,32,512]{2,1,0:T(8,128)S(1)}, f32[2,32,512]{2,1,0:T(8,128)S(1)}, u32[]{:S(2)}, u32[]{:S(2)}) collective-permute-start(f32[2,32,512]{2,1,0:T(8,128)S(1)} %shard_map.57.first_ref.after_ref), channel_id=1, source_target_pairs={{0,128},{16,144},{32,160},{48,176},{64,192},{80,208},{96,224},{112... | collective-permute-start | bytes 393224 | tf_op jit(solution)/shard_map/ppermute | solution.py:300
  84.7 24.2 %all-to-all-start.3 = ((f32[4,4,208,128]{3,2,1,0:T(8,128)}), f32[4,4,208,128]{3,2,1,0:T(8,128)S(1)}, u32[]{:S(2)}, u32[]{:S(2)}) async-start(f32[4,4,208,128]{3,2,1,0:T(8,128)} %shard_map.60), calls=%async_computation.3 | async-start | bytes 3407872 | tf_op jit(solution)/shard_map/all_to_all | solution.py:307
  89.3 8.8 %collective-permute-start.8 = (f32[4,32,512]{2,1,0:T(8,128)S(1)}, f32[4,32,512]{2,1,0:T(8,128)S(1)}, u32[]{:S(2)}, u32[]{:S(2)}) collective-permute-start(f32[4,32,512]{2,1,0:T(8,128)S(1)} %shard_map.58.line_ref), channel_id=1, source_target_pairs={{0,64},{16,80},{32,96},{48,112},{64,0},{80,16},{96,32},{112,48},{1... | collective-permute-start | bytes 786440 | tf_op jit(solution)/shard_map/ppermute | solution.py:300
  98.6 18.9 %collective-permute-start.9 = (f32[2,32,512]{2,1,0:T(8,128)S(1)}, f32[2,32,512]{2,1,0:T(8,128)S(1)}, u32[]{:S(2)}, u32[]{:S(2)}) collective-permute-start(f32[2,32,512]{2,1,0:T(8,128)S(1)} %get-tuple-element.18), channel_id=1, source_target_pairs={{0,16},{16,0},{32,48},{48,32},{64,80},{80,64},{96,112},{112,96},{1... | collective-permute-start | bytes 393224 | tf_op jit(solution)/shard_map/ppermute | solution.py:300
  102.4 15.2 %collective-permute-start.10 = (f32[2,32,512]{2,1,0:T(8,128)S(1)}, f32[2,32,512]{2,1,0:T(8,128)S(1)}, u32[]{:S(2)}, u32[]{:S(2)}) collective-permute-start(f32[2,32,512]{2,1,0:T(8,128)S(1)} %get-tuple-element.19), channel_id=1, source_target_pairs={{0,32},{16,48},{32,0},{48,16},{64,96},{80,112},{96,64},{112,80},{1... | collective-permute-start | bytes 393224 | tf_op jit(solution)/shard_map/ppermute | solution.py:300
  104.3 13.3 %collective-permute-start.11 = (f32[2,32,512]{2,1,0:T(8,128)S(1)}, f32[2,32,512]{2,1,0:T(8,128)S(1)}, u32[]{:S(2)}, u32[]{:S(2)}) collective-permute-start(f32[2,32,512]{2,1,0:T(8,128)S(1)} %get-tuple-element.20), channel_id=1, source_target_pairs={{0,48},{16,32},{32,16},{48,0},{64,112},{80,96},{96,80},{112,64},{1... | collective-permute-start | bytes 393224 | tf_op jit(solution)/shard_map/ppermute | solution.py:300

commit v8 on v7

--- a/solution.py
+++ b/solution.py
@@ -258,12 +258,14 @@
     thin_rows = lax.broadcasted_iota(jnp.int32, (rows, size), 0) + place * rows
     thin_cols = lax.broadcasted_iota(jnp.int32, (rows, size), 1)
     thin_eye = (thin_rows == thin_cols).astype(f32)
-    norm = jnp.sqrt(jnp.sum(stat * stat))
-    damped = plus(DAMP * norm, stat)
-    scale = jnp.sqrt(jnp.sum(damped * damped))
-    iterate = damped / scale
+    squares = jnp.sum(stat * stat)
+    trace = jnp.sum(jnp.where(diagonal, stat, 0.0))
+    norm = jnp.sqrt(squares)
+    damp = DAMP * norm
+    scale = jnp.sqrt(squares + 2.0 * damp * trace + size * damp * damp)
+    iterate = plus(damp, stat) * (1.0 / scale)
     mine = stat_ref[pl.ds(pl.multiple_of(place * rows, rows), rows), :]
-    mine = (mine + (DAMP * norm) * thin_eye) / scale
+    mine = (mine + damp * thin_eye) * (1.0 / scale)
     thin = 1.25 * thin_eye - 0.25 * mine
     parts_of = split(iterate)
     for _ in range(ITERS - 2):
@@ -282,7 +284,7 @@
         )
         for m in range(size // LANES)
     ]
-    mean = (jnp.concatenate(mean, axis=1) / count).astype(bf16)
+    mean = (jnp.concatenate(mean, axis=1) * (1.0 / count)).astype(bf16)
     out_ref[0] = jnp.dot(thin.astype(bf16), mean, preferred_element_type=f32).astype(bf16)
 
 

time: 120 us -> 119 us (level)
  transfers between devices with their start and end apart: 16 -> 16, of which waited for: 9 -> 9; matrix products, arithmetic and copies ran while one was open for 0% -> 0% of each run, Pallas kernels for 14% -> 13%
where the time goes in v8:
time: 119 us; the launch traced here: 118 us
  starting transfers between devices  74.7 us (63%)
  waiting for transfers between devices  22.1 us (19%)
  Pallas kernels  19.5 us (16%)
  local copies, waits for them, and re-layouts  1.32 us (1%)
    ppermute x12, starting transfers between devices, across(): return lax.ppermute(x, 'pre', [(i, i ^ k) for i in range(blocks)])  51.2 us
    all_to_all x4, starting transfers between devices, exchange(): return lax.all_to_all(x, 'rep', 0, 0, tiled=True, axis_index_groups=which)  23.5 us
    pallas_call x12, Pallas kernels, call(): pl.pallas_call(kernel, out_shape=out_shape, in_specs=in_specs, out_specs=...  18 us
    ppermute x12, waiting for transfers between devices, across(): return lax.ppermute(x, 'pre', [(i, i ^ k) for i in range(blocks)])  14.3 us
    all_to_all x4, waiting for transfers between devices, exchange(): return lax.all_to_all(x, 'rep', 0, 0, tiled=True, axis_index_groups=which)  7.79 us
  transfers between devices with their start and end apart: 16, of which 9 were waited for; matrix products, arithmetic and copies ran while one was open for 0% of the time, Pallas kernels for 13%

profile of v8, /device:TPU:1, one launch (start us, length us, event | category | flops | bytes accessed | tf_op | source)
XLA Modules:
  0.0 118.5 jit_solution(11102416901348598810)
XLA Ops:
  0.6 4.8 %collective-permute-start = (f32[2,32,512]{2,1,0:T(8,128)}, f32[2,32,512]{2,1,0:T(8,128)S(1)}, u32[]{:S(2)}, u32[]{:S(2)}) collective-permute-start(f32[2,32,512]{2,1,0:T(8,128)} %bitcast.5), channel_id=1, source_target_pairs={{0,32},{16,48},{32,0},{48,16},{64,96},{80,112},{96,64},{112,80},{1... | collective-permute-start | bytes 393224 | tf_op jit(solution)/shard_map/ppermute | solution.py:302
  5.5 3.1 %shard_map.51 = f32[4,4,64,512]{3,2,1,0:T(8,128)} custom-call(bf16[2,512,512]{2,1,0:T(8,128)(2,1)} %bitcast.8), custom_call_target="tpu_custom_call" | custom-call | flops 536870912 | bytes 4194304 | tf_op jit(solution)/shard_map/pallas_call | solution.py:28
  8.5 0.0 copy-start
  8.6 4.2 %all-to-all-start = ((f32[4,4,64,512]{3,2,1,0:T(8,128)}), f32[4,4,64,512]{3,2,1,0:T(8,128)S(1)}, u32[]{:S(2)}, u32[]{:S(2)}) async-start(f32[4,4,64,512]{3,2,1,0:T(8,128)} %shard_map.51), calls=%async_computation | async-start | bytes 4194304 | tf_op jit(solution)/shard_map/all_to_all | solution.py:309
  12.7 0.0 collective-permute-done.held_z_ref
  12.7 0.0 copy-done
  12.8 5.5 %collective-permute-start.1 = (f32[2,2,32,384]{3,2,1,0:T(8,128)S(1)}, f32[2,2,32,384]{3,2,1,0:T(8,128)S(1)}, u32[]{:S(2)}, u32[]{:S(2)}) collective-permute-start(f32[2,2,32,384]{3,2,1,0:T(8,128)S(1)} %shard_map.52.kept_ref), channel_id=1, source_target_pairs={{0,16},{16,0},{32,48},{48,32},{64,80},{80,64},{96,112},{112,96},{1... | collective-permute-start | bytes 589832 | tf_op jit(solution)/shard_map/ppermute | solution.py:302
  18.3 1.4 %shard_map.50.table_ref = s32[48]{0:T(128)} custom-call(s32[1]{0:T(128)} %bitcast.me_ref, s32[32]{0:T(128)} %owner_ref.1), custom_call_target="tpu_custom_call" | custom-call | tf_op jit(solution)/shard_map/pallas_call | solution.py:313
  19.7 0.0 collective-permute-done.1.core_ref
  19.7 0.0 copy-start.1
  19.8 0.6 copy-done.1
  20.4 0.6 shard_map.53
  21.0 1.9 %collective-permute-start.2 = (f32[2,32,384]{2,1,0:T(8,128)S(1)}, f32[2,32,384]{2,1,0:T(8,128)S(1)}, u32[]{:S(2)}, u32[]{:S(2)}) collective-permute-start(f32[2,32,384]{2,1,0:T(8,128)S(1)} %get-tuple-element.13), channel_id=1, source_target_pairs={{0,64},{16,80},{32,96},{48,112},{64,0},{80,16},{96,32},{112,48},{1... | collective-permute-start | bytes 294920 | tf_op jit(solution)/shard_map/ppermute | solution.py:302
  22.9 3.2 %collective-permute-start.3 = (f32[2,32,384]{2,1,0:T(8,128)S(1)}, f32[2,32,384]{2,1,0:T(8,128)S(1)}, u32[]{:S(2)}, u32[]{:S(2)}) collective-permute-start(f32[2,32,384]{2,1,0:T(8,128)S(1)} %get-tuple-element.14), channel_id=1, source_target_pairs={{0,128},{16,144},{32,160},{48,176},{64,192},{80,208},{96,224},{112... | collective-permute-start | bytes 294920 | tf_op jit(solution)/shard_map/ppermute | solution.py:302
  26.1 0.0 copy-start.3
  26.1 4.2 %collective-permute-start.4 = (f32[2,32,384]{2,1,0:T(8,128)S(1)}, f32[2,32,384]{2,1,0:T(8,128)S(1)}, u32[]{:S(2)}, u32[]{:S(2)}) collective-permute-start(f32[2,32,384]{2,1,0:T(8,128)S(1)} %get-tuple-element.15), channel_id=1, source_target_pairs={{0,192},{16,208},{32,224},{48,240},{64,128},{80,144},{96,160},{112... | collective-permute-start | bytes 294920 | tf_op jit(solution)/shard_map/ppermute | solution.py:302
  30.3 0.0 collective-permute-done.2.near1.refs_0_
  30.3 1.9 %collective-permute-done.3.near2.refs_1_ = f32[2,32,384]{2,1,0:T(8,128)S(1)} collective-permute-done((f32[2,32,384]{2,1,0:T(8,128)S(1)}, f32[2,32,384]{2,1,0:T(8,128)S(1)}, u32[]{:S(2)}, u32[]{:S(2)}) %collective-permute-start.3) | collective-permute-done | bytes 98336 | tf_op jit(solution)/shard_map/ppermute | solution.py:302
  32.2 1.4 %collective-permute-done.4.near3.refs_2_ = f32[2,32,384]{2,1,0:T(8,128)S(1)} collective-permute-done((f32[2,32,384]{2,1,0:T(8,128)S(1)}, f32[2,32,384]{2,1,0:T(8,128)S(1)}, u32[]{:S(2)}, u32[]{:S(2)}) %collective-permute-start.4) | collective-permute-done | bytes 98336 | tf_op jit(solution)/shard_map/ppermute | solution.py:302
  33.7 0.0 copy-start.2
  33.7 0.7 copy-done.2
  34.3 0.6 shard_map.54.after_ref
  34.9 0.7 all-to-all-done.parts_ref
  35.5 0.9 shard_map.55
  36.5 11.4 %all-to-all-start.1 = ((f32[4,64,512]{2,1,0:T(8,128)}), f32[4,64,512]{2,1,0:T(8,128)S(1)}, u32[]{:S(2)}, u32[]{:S(2)}) async-start(f32[4,64,512]{2,1,0:T(8,128)} %shard_map.55), calls=%async_computation.1 | async-start | bytes 1048576 | tf_op jit(solution)/shard_map/all_to_all | solution.py:309
  47.9 7.4 %collective-permute-start.5 = (f32[32,384]{1,0:T(8,128)S(1)}, f32[32,384]{1,0:T(8,128)S(1)}, u32[]{:S(2)}, u32[]{:S(2)}) collective-permute-start(f32[32,384]{1,0:T(8,128)S(1)} %shard_map.54.after_ref), channel_id=1, source_target_pairs={{0,256},{16,272},{32,288},{48,304},{64,320},{80,336},{96,352},{112... | collective-permute-start | bytes 147464 | tf_op jit(solution)/shard_map/ppermute | solution.py:302
  55.3 1.5 %collective-permute-done.5.refs_3_ = f32[32,384]{1,0:T(8,128)S(1)} collective-permute-done((f32[32,384]{1,0:T(8,128)S(1)}, f32[32,384]{1,0:T(8,128)S(1)}, u32[]{:S(2)}, u32[]{:S(2)}) %collective-permute-start.5) | collective-permute-done | bytes 49184 | tf_op jit(solution)/shard_map/ppermute | solution.py:302
  56.8 6.0 %all-to-all-done.1.sums_ref = f32[4,64,512]{2,1,0:T(8,128)S(1)} async-done(((f32[4,64,512]{2,1,0:T(8,128)}), f32[4,64,512]{2,1,0:T(8,128)S(1)}, u32[]{:S(2)}, u32[]{:S(2)}) %all-to-all-start.1) | async-done | bytes 524320 | tf_op jit(solution)/shard_map/all_to_all | solution.py:309
  62.9 0.0 copy-done.3
  62.9 1.5 %shard_map.56 = (f32[4,208,128]{2,1,0:T(8,128)}, f32[1,32,512]{2,1,0:T(8,128)S(1)}) custom-call(s32[48]{0:T(128)S(1)} %copy-done.3, s32[1]{0:T(128)} %bitcast.2.place_ref, f32[4,64,512]{2,1,0:T(8,128)S(1)} %all-to-all-done.1.sums_ref, f32[2,2,32,384]{3,2,1,0:T(8,128)S(1)} %shard_map.52.kept_ref, f32[2,2,32,384]{3,2,1,0:T(8,128)S(1)} %collective-permute-done.1.core_ref, ...), custom_call_target="tpu_custom_call" | custom-call | bytes 2949120 | tf_op jit(solution)/shard_map/pallas_call | solution.py:28
  64.3 4.3 %all-to-all-start.2 = ((f32[4,208,128]{2,1,0:T(8,128)}), f32[4,208,128]{2,1,0:T(8,128)S(1)}, u32[]{:S(2)}, u32[]{:S(2)}) async-start(f32[4,208,128]{2,1,0:T(8,128)} %get-tuple-element.21), calls=%async_computation.2 | async-start | bytes 851968 | tf_op jit(solution)/shard_map/all_to_all | solution.py:309
  68.6 7.4 %collective-permute-start.6 = (f32[1,32,512]{2,1,0:T(8,128)S(1)}, f32[1,32,512]{2,1,0:T(8,128)S(1)}, u32[]{:S(2)}, u32[]{:S(2)}) collective-permute-start(f32[1,32,512]{2,1,0:T(8,128)S(1)} %get-tuple-element.16.first_ref), channel_id=1, source_target_pairs={{0,256},{16,272},{32,288},{48,304},{64,320},{80,336},{96,352},{112... | collective-permute-start | bytes 196616 | tf_op jit(solution)/shard_map/ppermute | solution.py:302
  76.1 1.7 %collective-permute-done.6.second_ref = f32[1,32,512]{2,1,0:T(8,128)S(1)} collective-permute-done((f32[1,32,512]{2,1,0:T(8,128)S(1)}, f32[1,32,512]{2,1,0:T(8,128)S(1)}, u32[]{:S(2)}, u32[]{:S(2)}) %collective-permute-start.6) | collective-permute-done | bytes 65568 | tf_op jit(solution)/shard_map/ppermute | solution.py:302
  77.8 5.6 %collective-permute-start.7 = (f32[2,32,512]{2,1,0:T(8,128)S(1)}, f32[2,32,512]{2,1,0:T(8,128)S(1)}, u32[]{:S(2)}, u32[]{:S(2)}) collective-permute-start(f32[2,32,512]{2,1,0:T(8,128)S(1)} %shard_map.57.first_ref.after_ref), channel_id=1, source_target_pairs={{0,128},{16,144},{32,160},{48,176},{64,192},{80,208},{96,224},{112... | collective-permute-start | bytes 393224 | tf_op jit(solution)/shard_map/ppermute | solution.py:302
  83.5 0.0 all-to-all-done.2.part_ref
  83.5 1.3 %shard_map.60 = f32[4,4,208,128]{3,2,1,0:T(8,128)} custom-call(f32[4,208,128]{2,1,0:T(8,128)S(1)} %all-to-all-done.2.part_ref, f32[2,32,512]{2,1,0:T(8,128)S(1)} %shard_map.57.first_ref.after_ref), custom_call_target="tpu_custom_call" | custom-call | bytes 2621440 | tf_op jit(solution)/shard_map/pallas_call | solution.py:28
  84.7 3.6 %all-to-all-start.3 = ((f32[4,4,208,128]{3,2,1,0:T(8,128)}), f32[4,4,208,128]{3,2,1,0:T(8,128)S(1)}, u32[]{:S(2)}, u32[]{:S(2)}) async-start(f32[4,4,208,128]{3,2,1,0:T(8,128)} %shard_map.60), calls=%async_computation.3 | async-start | bytes 3407872 | tf_op jit(solution)/shard_map/all_to_all | solution.py:309
  88.3 0.9 collective-permute-done.7.second_ref
  89.3 1.9 %collective-permute-start.8 = (f32[4,32,512]{2,1,0:T(8,128)S(1)}, f32[4,32,512]{2,1,0:T(8,128)S(1)}, u32[]{:S(2)}, u32[]{:S(2)}) collective-permute-start(f32[4,32,512]{2,1,0:T(8,128)S(1)} %shard_map.58.line_ref), channel_id=1, source_target_pairs={{0,64},{16,80},{32,96},{48,112},{64,0},{80,16},{96,32},{112,48},{1... | collective-permute-start | bytes 786440 | tf_op jit(solution)/shard_map/ppermute | solution.py:302
  91.2 6.8 %collective-permute-done.8.far_ref = f32[4,32,512]{2,1,0:T(8,128)S(1)} collective-permute-done((f32[4,32,512]{2,1,0:T(8,128)S(1)}, f32[4,32,512]{2,1,0:T(8,128)S(1)}, u32[]{:S(2)}, u32[]{:S(2)}) %collective-permute-start.8) | collective-permute-done | bytes 262176 | tf_op jit(solution)/shard_map/ppermute | solution.py:302
  98.0 0.6 shard_map.59
  98.6 3.8 %collective-permute-start.9 = (f32[2,32,512]{2,1,0:T(8,128)S(1)}, f32[2,32,512]{2,1,0:T(8,128)S(1)}, u32[]{:S(2)}, u32[]{:S(2)}) collective-permute-start(f32[2,32,512]{2,1,0:T(8,128)S(1)} %get-tuple-element.18), channel_id=1, source_target_pairs={{0,16},{16,0},{32,48},{48,32},{64,80},{80,64},{96,112},{112,96},{1... | collective-permute-start | bytes 393224 | tf_op jit(solution)/shard_map/ppermute | solution.py:302
  102.4 1.9 %collective-permute-start.10 = (f32[2,32,512]{2,1,0:T(8,128)S(1)}, f32[2,32,512]{2,1,0:T(8,128)S(1)}, u32[]{:S(2)}, u32[]{:S(2)}) collective-permute-start(f32[2,32,512]{2,1,0:T(8,128)S(1)} %get-tuple-element.19), channel_id=1, source_target_pairs={{0,32},{16,48},{32,0},{48,16},{64,96},{80,112},{96,64},{112,80},{1... | collective-permute-start | bytes 393224 | tf_op jit(solution)/shard_map/ppermute | solution.py:302
  104.3 3.5 %collective-permute-start.11 = (f32[2,32,512]{2,1,0:T(8,128)S(1)}, f32[2,32,512]{2,1,0:T(8,128)S(1)}, u32[]{:S(2)}, u32[]{:S(2)}) collective-permute-start(f32[2,32,512]{2,1,0:T(8,128)S(1)} %get-tuple-element.20), channel_id=1, source_target_pairs={{0,48},{16,32},{32,16},{48,0},{64,112},{80,96},{96,80},{112,64},{1... | collective-permute-start | bytes 393224 | tf_op jit(solution)/shard_map/ppermute | solution.py:302
  107.9 1.1 all-to-all-done.3.all_ref
  109.0 8.3 %shard_map.61 = (bf16[1,32,512]{2,1,0:T(8,128)(2,1)}, f32[8,128]{1,0:T(8,128)S(1)}) custom-call(s32[1]{0:T(128)} %bitcast.2.place_ref, f32[4,4,208,128]{3,2,1,0:T(8,128)S(1)} %all-to-all-done.3.all_ref, f32[2,32,512]{2,1,0:T(8,128)S(1)} %get-tuple-element.17.after_ref.got0), custom_call_target="tpu_custom_call" | custom-call | flops 5368709120 | bytes 2097152 | tf_op jit(solution)/shard_map/pallas_call | solution.py:28
  117.2 0.0 collective-permute-done.9.got1
  117.3 0.0 collective-permute-done.10.got2
  117.3 0.0 collective-permute-done.11.got3
  117.3 1.2 %shard_map.62 = f32[2,32,512]{2,1,0:T(8,128)} custom-call(s32[48]{0:T(128)S(1)} %copy-done.3, f32[2,32,512]{2,1,0:T(8,128)S(1)} %bitcast.7, f32[2,32,512]{2,1,0:T(8,128)S(1)} %get-tuple-element.17.after_ref.got0, f32[2,32,512]{2,1,0:T(8,128)S(1)} %collective-permute-done.9.got1, f32[2,32,512]{2,1,0:T(8,128)S(1)} %collective-permute-done.10.got2, ...), custom_call_target="tpu_custom_call" | custom-call | bytes 524288 | tf_op jit(solution)/shard_map/pallas_call | solution.py:28
  (3 shorter events, 0.1 us)
Async XLA Ops:
  0.6 12.1 %collective-permute-start = (f32[2,32,512]{2,1,0:T(8,128)}, f32[2,32,512]{2,1,0:T(8,128)S(1)}, u32[]{:S(2)}, u32[]{:S(2)}) collective-permute-start(f32[2,32,512]{2,1,0:T(8,128)} %bitcast.5), channel_id=1, source_target_pairs={{0,32},{16,48},{32,0},{48,16},{64,96},{80,112},{96,64},{112,80},{1... | collective-permute-start | bytes 393224 | tf_op jit(solution)/shard_map/ppermute | solution.py:302
  8.5 4.2 %copy-start = (f32[1,2,32,512]{3,2,1,0:T(8,128)S(1)}, f32[1,2,32,512]{3,2,1,0:T(8,128)}, u32[]{:S(2)}) copy-start(f32[1,2,32,512]{3,2,1,0:T(8,128)} %param.5) | copy-start | bytes 393220
  8.6 27.0 %all-to-all-start = ((f32[4,4,64,512]{3,2,1,0:T(8,128)}), f32[4,4,64,512]{3,2,1,0:T(8,128)S(1)}, u32[]{:S(2)}, u32[]{:S(2)}) async-start(f32[4,4,64,512]{3,2,1,0:T(8,128)} %shard_map.51), calls=%async_computation | async-start | bytes 4194304 | tf_op jit(solution)/shard_map/all_to_all | solution.py:309
  12.8 7.0 %collective-permute-start.1 = (f32[2,2,32,384]{3,2,1,0:T(8,128)S(1)}, f32[2,2,32,384]{3,2,1,0:T(8,128)S(1)}, u32[]{:S(2)}, u32[]{:S(2)}) collective-permute-start(f32[2,2,32,384]{3,2,1,0:T(8,128)S(1)} %shard_map.52.kept_ref), channel_id=1, source_target_pairs={{0,16},{16,0},{32,48},{48,32},{64,80},{80,64},{96,112},{112,96},{1... | collective-permute-start | bytes 589832 | tf_op jit(solution)/shard_map/ppermute | solution.py:302
  19.7 0.7 copy-start.1
  21.0 9.3 %collective-permute-start.2 = (f32[2,32,384]{2,1,0:T(8,128)S(1)}, f32[2,32,384]{2,1,0:T(8,128)S(1)}, u32[]{:S(2)}, u32[]{:S(2)}) collective-permute-start(f32[2,32,384]{2,1,0:T(8,128)S(1)} %get-tuple-element.13), channel_id=1, source_target_pairs={{0,64},{16,80},{32,96},{48,112},{64,0},{80,16},{96,32},{112,48},{1... | collective-permute-start | bytes 294920 | tf_op jit(solution)/shard_map/ppermute | solution.py:302
  22.9 9.3 %collective-permute-start.3 = (f32[2,32,384]{2,1,0:T(8,128)S(1)}, f32[2,32,384]{2,1,0:T(8,128)S(1)}, u32[]{:S(2)}, u32[]{:S(2)}) collective-permute-start(f32[2,32,384]{2,1,0:T(8,128)S(1)} %get-tuple-element.14), channel_id=1, source_target_pairs={{0,128},{16,144},{32,160},{48,176},{64,192},{80,208},{96,224},{112... | collective-permute-start | bytes 294920 | tf_op jit(solution)/shard_map/ppermute | solution.py:302
  26.1 36.8 %copy-start.3 = (s32[48]{0:T(128)S(1)}, s32[48]{0:T(128)}, u32[]{:S(2)}) copy-start(s32[48]{0:T(128)} %shard_map.50.table_ref) | copy-start | bytes 580
  26.1 7.6 %collective-permute-start.4 = (f32[2,32,384]{2,1,0:T(8,128)S(1)}, f32[2,32,384]{2,1,0:T(8,128)S(1)}, u32[]{:S(2)}, u32[]{:S(2)}) collective-permute-start(f32[2,32,384]{2,1,0:T(8,128)S(1)} %get-tuple-element.15), channel_id=1, source_target_pairs={{0,192},{16,208},{32,224},{48,240},{64,128},{80,144},{96,160},{112... | collective-permute-start | bytes 294920 | tf_op jit(solution)/shard_map/ppermute | solution.py:302
  33.7 0.7 copy-start.2
  36.5 26.4 %all-to-all-start.1 = ((f32[4,64,512]{2,1,0:T(8,128)}), f32[4,64,512]{2,1,0:T(8,128)S(1)}, u32[]{:S(2)}, u32[]{:S(2)}) async-start(f32[4,64,512]{2,1,0:T(8,128)} %shard_map.55), calls=%async_computation.1 | async-start | bytes 1048576 | tf_op jit(solution)/shard_map/all_to_all | solution.py:309
  47.9 9.0 %collective-permute-start.5 = (f32[32,384]{1,0:T(8,128)S(1)}, f32[32,384]{1,0:T(8,128)S(1)}, u32[]{:S(2)}, u32[]{:S(2)}) collective-permute-start(f32[32,384]{1,0:T(8,128)S(1)} %shard_map.54.after_ref), channel_id=1, source_target_pairs={{0,256},{16,272},{32,288},{48,304},{64,320},{80,336},{96,352},{112... | collective-permute-start | bytes 147464 | tf_op jit(solution)/shard_map/ppermute | solution.py:302
  64.3 19.1 %all-to-all-start.2 = ((f32[4,208,128]{2,1,0:T(8,128)}), f32[4,208,128]{2,1,0:T(8,128)S(1)}, u32[]{:S(2)}, u32[]{:S(2)}) async-start(f32[4,208,128]{2,1,0:T(8,128)} %get-tuple-element.21), calls=%async_computation.2 | async-start | bytes 851968 | tf_op jit(solution)/shard_map/all_to_all | solution.py:309
  68.6 9.2 %collective-permute-start.6 = (f32[1,32,512]{2,1,0:T(8,128)S(1)}, f32[1,32,512]{2,1,0:T(8,128)S(1)}, u32[]{:S(2)}, u32[]{:S(2)}) collective-permute-start(f32[1,32,512]{2,1,0:T(8,128)S(1)} %get-tuple-element.16.first_ref), channel_id=1, source_target_pairs={{0,256},{16,272},{32,288},{48,304},{64,320},{80,336},{96,352},{112... | collective-permute-start | bytes 196616 | tf_op jit(solution)/shard_map/ppermute | solution.py:302
  77.8 11.4 %collective-permute-start.7 = (f32[2,32,512]{2,1,0:T(8,128)S(1)}, f32[2,32,512]{2,1,0:T(8,128)S(1)}, u32[]{:S(2)}, u32[]{:S(2)}) collective-permute-start(f32[2,32,512]{2,1,0:T(8,128)S(1)} %shard_map.57.first_ref.after_ref), channel_id=1, source_target_pairs={{0,128},{16,144},{32,160},{48,176},{64,192},{80,208},{96,224},{112... | collective-permute-start | bytes 393224 | tf_op jit(solution)/shard_map/ppermute | solution.py:302
  84.7 24.2 %all-to-all-start.3 = ((f32[4,4,208,128]{3,2,1,0:T(8,128)}), f32[4,4,208,128]{3,2,1,0:T(8,128)S(1)}, u32[]{:S(2)}, u32[]{:S(2)}) async-start(f32[4,4,208,128]{3,2,1,0:T(8,128)} %shard_map.60), calls=%async_computation.3 | async-start | bytes 3407872 | tf_op jit(solution)/shard_map/all_to_all | solution.py:309
  89.3 8.8 %collective-permute-start.8 = (f32[4,32,512]{2,1,0:T(8,128)S(1)}, f32[4,32,512]{2,1,0:T(8,128)S(1)}, u32[]{:S(2)}, u32[]{:S(2)}) collective-permute-start(f32[4,32,512]{2,1,0:T(8,128)S(1)} %shard_map.58.line_ref), channel_id=1, source_target_pairs={{0,64},{16,80},{32,96},{48,112},{64,0},{80,16},{96,32},{112,48},{1... | collective-permute-start | bytes 786440 | tf_op jit(solution)/shard_map/ppermute | solution.py:302
  98.6 18.6 %collective-permute-start.9 = (f32[2,32,512]{2,1,0:T(8,128)S(1)}, f32[2,32,512]{2,1,0:T(8,128)S(1)}, u32[]{:S(2)}, u32[]{:S(2)}) collective-permute-start(f32[2,32,512]{2,1,0:T(8,128)S(1)} %get-tuple-element.18), channel_id=1, source_target_pairs={{0,16},{16,0},{32,48},{48,32},{64,80},{80,64},{96,112},{112,96},{1... | collective-permute-start | bytes 393224 | tf_op jit(solution)/shard_map/ppermute | solution.py:302
  102.4 14.8 %collective-permute-start.10 = (f32[2,32,512]{2,1,0:T(8,128)S(1)}, f32[2,32,512]{2,1,0:T(8,128)S(1)}, u32[]{:S(2)}, u32[]{:S(2)}) collective-permute-start(f32[2,32,512]{2,1,0:T(8,128)S(1)} %get-tuple-element.19), channel_id=1, source_target_pairs={{0,32},{16,48},{32,0},{48,16},{64,96},{80,112},{96,64},{112,80},{1... | collective-permute-start | bytes 393224 | tf_op jit(solution)/shard_map/ppermute | solution.py:302
  104.3 12.9 %collective-permute-start.11 = (f32[2,32,512]{2,1,0:T(8,128)S(1)}, f32[2,32,512]{2,1,0:T(8,128)S(1)}, u32[]{:S(2)}, u32[]{:S(2)}) collective-permute-start(f32[2,32,512]{2,1,0:T(8,128)S(1)} %get-tuple-element.20), channel_id=1, source_target_pairs={{0,48},{16,32},{32,16},{48,0},{64,112},{80,96},{96,80},{112,64},{1... | collective-permute-start | bytes 393224 | tf_op jit(solution)/shard_map/ppermute | solution.py:302

commit v9 on v8

--- a/solution.py
+++ b/solution.py
@@ -36,15 +36,10 @@
     )(*args)
 
 
-def gram_kernel(grads_hbm, out_ref, grads_ref, whole_ref, in_sems, out_sems):
+def gram_kernel(grads_ref, out_ref, whole_ref, out_sems):
     shards, size, _ = grads_ref.shape
     xs, zs, double, _ = out_ref.shape
     rows = double // 2
-    loads = [pltpu.make_async_copy(grads_hbm.at[s], grads_ref.at[s], in_sems.at[s]) for s in range(shards)]
-    for load in loads:
-        load.start()
-    for load in loads:
-        load.wait()
     stores = []
     half = size // 2
     for h in range(2):
@@ -326,15 +321,13 @@
     sums = call(
         gram_kernel,
         shape(ACROSS, zs, 2 * rows, size),
-        [ANY],
+        [VMEM],
         (2 * shards * size**3, 4 * size * size * (shards + 2)),
         local,
-        limit=60,
+        limit=62,
         out_specs=ANY,
         scratch=[
-            pltpu.VMEM(local.shape, local.dtype),
             pltpu.VMEM((ACROSS, zs, 2 * rows, size), f32),
-            pltpu.SemaphoreType.DMA((shards,)),
             pltpu.SemaphoreType.DMA((2, ACROSS)),
         ],
     )

time: 119 us -> 119 us (level)
  no operation moved by 1% of the time
where the time goes in v9:
time: 119 us; the launch traced here: 118 us
  starting transfers between devices  74.7 us (63%)
  waiting for transfers between devices  22.1 us (19%)
  Pallas kernels  19.5 us (16%)
  local copies, waits for them, and re-layouts  1.32 us (1%)
    ppermute x12, starting transfers between devices, across(): return lax.ppermute(x, 'pre', [(i, i ^ k) for i in range(blocks)])  51.2 us
    all_to_all x4, starting transfers between devices, exchange(): return lax.all_to_all(x, 'rep', 0, 0, tiled=True, axis_index_groups=which)  23.4 us
    pallas_call x12, Pallas kernels, call(): pl.pallas_call(kernel, out_shape=out_shape, in_specs=in_specs, out_specs=...  18 us
    ppermute x12, waiting for transfers between devices, across(): return lax.ppermute(x, 'pre', [(i, i ^ k) for i in range(blocks)])  14.4 us
    all_to_all x4, waiting for transfers between devices, exchange(): return lax.all_to_all(x, 'rep', 0, 0, tiled=True, axis_index_groups=which)  7.72 us
  transfers between devices with their start and end apart: 16, of which 9 were waited for; matrix products, arithmetic and copies ran while one was open for 0% of the time, Pallas kernels for 13%

profile of v9, /device:TPU:1, one launch (start us, length us, event | category | flops | bytes accessed | tf_op | source)
XLA Modules:
  0.0 118.5 jit_solution(12151615379543078530)
XLA Ops:
  0.6 4.8 %collective-permute-start = (f32[2,32,512]{2,1,0:T(8,128)}, f32[2,32,512]{2,1,0:T(8,128)S(1)}, u32[]{:S(2)}, u32[]{:S(2)}) collective-permute-start(f32[2,32,512]{2,1,0:T(8,128)} %bitcast.5), channel_id=1, source_target_pairs={{0,32},{16,48},{32,0},{48,16},{64,96},{80,112},{96,64},{112,80},{1... | collective-permute-start | bytes 393224 | tf_op jit(solution)/shard_map/ppermute | solution.py:297
  5.5 3.1 %shard_map.51 = f32[4,4,64,512]{3,2,1,0:T(8,128)} custom-call(bf16[2,512,512]{2,1,0:T(8,128)(2,1)} %bitcast.8), custom_call_target="tpu_custom_call" | custom-call | flops 536870912 | bytes 4194304 | tf_op jit(solution)/shard_map/pallas_call | solution.py:28
  8.6 0.0 copy-start
  8.6 4.2 %all-to-all-start = ((f32[4,4,64,512]{3,2,1,0:T(8,128)}), f32[4,4,64,512]{3,2,1,0:T(8,128)S(1)}, u32[]{:S(2)}, u32[]{:S(2)}) async-start(f32[4,4,64,512]{3,2,1,0:T(8,128)} %shard_map.51), calls=%async_computation | async-start | bytes 4194304 | tf_op jit(solution)/shard_map/all_to_all | solution.py:304
  12.7 0.0 collective-permute-done.held_z_ref
  12.7 0.0 copy-done
  12.8 5.5 %collective-permute-start.1 = (f32[2,2,32,384]{3,2,1,0:T(8,128)S(1)}, f32[2,2,32,384]{3,2,1,0:T(8,128)S(1)}, u32[]{:S(2)}, u32[]{:S(2)}) collective-permute-start(f32[2,2,32,384]{3,2,1,0:T(8,128)S(1)} %shard_map.52.kept_ref), channel_id=1, source_target_pairs={{0,16},{16,0},{32,48},{48,32},{64,80},{80,64},{96,112},{112,96},{1... | collective-permute-start | bytes 589832 | tf_op jit(solution)/shard_map/ppermute | solution.py:297
  18.3 1.4 %shard_map.50.table_ref = s32[48]{0:T(128)} custom-call(s32[1]{0:T(128)} %bitcast.me_ref, s32[32]{0:T(128)} %owner_ref.1), custom_call_target="tpu_custom_call" | custom-call | tf_op jit(solution)/shard_map/pallas_call | solution.py:308
  19.7 0.0 collective-permute-done.1.core_ref
  19.8 0.0 copy-start.1
  19.8 0.6 copy-done.1
  20.4 0.6 shard_map.53
  21.0 1.9 %collective-permute-start.2 = (f32[2,32,384]{2,1,0:T(8,128)S(1)}, f32[2,32,384]{2,1,0:T(8,128)S(1)}, u32[]{:S(2)}, u32[]{:S(2)}) collective-permute-start(f32[2,32,384]{2,1,0:T(8,128)S(1)} %get-tuple-element.13), channel_id=1, source_target_pairs={{0,64},{16,80},{32,96},{48,112},{64,0},{80,16},{96,32},{112,48},{1... | collective-permute-start | bytes 294920 | tf_op jit(solution)/shard_map/ppermute | solution.py:297
  22.9 3.2 %collective-permute-start.3 = (f32[2,32,384]{2,1,0:T(8,128)S(1)}, f32[2,32,384]{2,1,0:T(8,128)S(1)}, u32[]{:S(2)}, u32[]{:S(2)}) collective-permute-start(f32[2,32,384]{2,1,0:T(8,128)S(1)} %get-tuple-element.14), channel_id=1, source_target_pairs={{0,128},{16,144},{32,160},{48,176},{64,192},{80,208},{96,224},{112... | collective-permute-start | bytes 294920 | tf_op jit(solution)/shard_map/ppermute | solution.py:297
  26.1 0.0 copy-start.3
  26.1 4.2 %collective-permute-start.4 = (f32[2,32,384]{2,1,0:T(8,128)S(1)}, f32[2,32,384]{2,1,0:T(8,128)S(1)}, u32[]{:S(2)}, u32[]{:S(2)}) collective-permute-start(f32[2,32,384]{2,1,0:T(8,128)S(1)} %get-tuple-element.15), channel_id=1, source_target_pairs={{0,192},{16,208},{32,224},{48,240},{64,128},{80,144},{96,160},{112... | collective-permute-start | bytes 294920 | tf_op jit(solution)/shard_map/ppermute | solution.py:297
  30.3 0.0 collective-permute-done.2.near1.refs_0_
  30.3 1.9 %collective-permute-done.3.near2.refs_1_ = f32[2,32,384]{2,1,0:T(8,128)S(1)} collective-permute-done((f32[2,32,384]{2,1,0:T(8,128)S(1)}, f32[2,32,384]{2,1,0:T(8,128)S(1)}, u32[]{:S(2)}, u32[]{:S(2)}) %collective-permute-start.3) | collective-permute-done | bytes 98336 | tf_op jit(solution)/shard_map/ppermute | solution.py:297
  32.3 1.4 %collective-permute-done.4.near3.refs_2_ = f32[2,32,384]{2,1,0:T(8,128)S(1)} collective-permute-done((f32[2,32,384]{2,1,0:T(8,128)S(1)}, f32[2,32,384]{2,1,0:T(8,128)S(1)}, u32[]{:S(2)}, u32[]{:S(2)}) %collective-permute-start.4) | collective-permute-done | bytes 98336 | tf_op jit(solution)/shard_map/ppermute | solution.py:297
  33.7 0.0 copy-start.2
  33.7 0.7 copy-done.2
  34.3 0.6 shard_map.54.after_ref
  34.9 0.7 all-to-all-done.parts_ref
  35.6 0.9 shard_map.55
  36.5 11.4 %all-to-all-start.1 = ((f32[4,64,512]{2,1,0:T(8,128)}), f32[4,64,512]{2,1,0:T(8,128)S(1)}, u32[]{:S(2)}, u32[]{:S(2)}) async-start(f32[4,64,512]{2,1,0:T(8,128)} %shard_map.55), calls=%async_computation.1 | async-start | bytes 1048576 | tf_op jit(solution)/shard_map/all_to_all | solution.py:304
  47.9 7.5 %collective-permute-start.5 = (f32[32,384]{1,0:T(8,128)S(1)}, f32[32,384]{1,0:T(8,128)S(1)}, u32[]{:S(2)}, u32[]{:S(2)}) collective-permute-start(f32[32,384]{1,0:T(8,128)S(1)} %shard_map.54.after_ref), channel_id=1, source_target_pairs={{0,256},{16,272},{32,288},{48,304},{64,320},{80,336},{96,352},{112... | collective-permute-start | bytes 147464 | tf_op jit(solution)/shard_map/ppermute | solution.py:297
  55.3 1.5 %collective-permute-done.5.refs_3_ = f32[32,384]{1,0:T(8,128)S(1)} collective-permute-done((f32[32,384]{1,0:T(8,128)S(1)}, f32[32,384]{1,0:T(8,128)S(1)}, u32[]{:S(2)}, u32[]{:S(2)}) %collective-permute-start.5) | collective-permute-done | bytes 49184 | tf_op jit(solution)/shard_map/ppermute | solution.py:297
  56.8 6.0 %all-to-all-done.1.sums_ref = f32[4,64,512]{2,1,0:T(8,128)S(1)} async-done(((f32[4,64,512]{2,1,0:T(8,128)}), f32[4,64,512]{2,1,0:T(8,128)S(1)}, u32[]{:S(2)}, u32[]{:S(2)}) %all-to-all-start.1) | async-done | bytes 524320 | tf_op jit(solution)/shard_map/all_to_all | solution.py:304
  62.9 0.0 copy-done.3
  62.9 1.5 %shard_map.56 = (f32[4,208,128]{2,1,0:T(8,128)}, f32[1,32,512]{2,1,0:T(8,128)S(1)}) custom-call(s32[48]{0:T(128)S(1)} %copy-done.3, s32[1]{0:T(128)} %bitcast.2.place_ref, f32[4,64,512]{2,1,0:T(8,128)S(1)} %all-to-all-done.1.sums_ref, f32[2,2,32,384]{3,2,1,0:T(8,128)S(1)} %shard_map.52.kept_ref, f32[2,2,32,384]{3,2,1,0:T(8,128)S(1)} %collective-permute-done.1.core_ref, ...), custom_call_target="tpu_custom_call" | custom-call | bytes 2949120 | tf_op jit(solution)/shard_map/pallas_call | solution.py:28
  64.3 4.3 %all-to-all-start.2 = ((f32[4,208,128]{2,1,0:T(8,128)}), f32[4,208,128]{2,1,0:T(8,128)S(1)}, u32[]{:S(2)}, u32[]{:S(2)}) async-start(f32[4,208,128]{2,1,0:T(8,128)} %get-tuple-element.21), calls=%async_computation.2 | async-start | bytes 851968 | tf_op jit(solution)/shard_map/all_to_all | solution.py:304
  68.6 7.4 %collective-permute-start.6 = (f32[1,32,512]{2,1,0:T(8,128)S(1)}, f32[1,32,512]{2,1,0:T(8,128)S(1)}, u32[]{:S(2)}, u32[]{:S(2)}) collective-permute-start(f32[1,32,512]{2,1,0:T(8,128)S(1)} %get-tuple-element.16.first_ref), channel_id=1, source_target_pairs={{0,256},{16,272},{32,288},{48,304},{64,320},{80,336},{96,352},{112... | collective-permute-start | bytes 196616 | tf_op jit(solution)/shard_map/ppermute | solution.py:297
  76.1 1.7 %collective-permute-done.6.second_ref = f32[1,32,512]{2,1,0:T(8,128)S(1)} collective-permute-done((f32[1,32,512]{2,1,0:T(8,128)S(1)}, f32[1,32,512]{2,1,0:T(8,128)S(1)}, u32[]{:S(2)}, u32[]{:S(2)}) %collective-permute-start.6) | collective-permute-done | bytes 65568 | tf_op jit(solution)/shard_map/ppermute | solution.py:297
  77.8 5.6 %collective-permute-start.7 = (f32[2,32,512]{2,1,0:T(8,128)S(1)}, f32[2,32,512]{2,1,0:T(8,128)S(1)}, u32[]{:S(2)}, u32[]{:S(2)}) collective-permute-start(f32[2,32,512]{2,1,0:T(8,128)S(1)} %shard_map.57.first_ref.after_ref), channel_id=1, source_target_pairs={{0,128},{16,144},{32,160},{48,176},{64,192},{80,208},{96,224},{112... | collective-permute-start | bytes 393224 | tf_op jit(solution)/shard_map/ppermute | solution.py:297
  83.4 0.0 all-to-all-done.2.part_ref
  83.5 1.3 %shard_map.60 = f32[4,4,208,128]{3,2,1,0:T(8,128)} custom-call(f32[4,208,128]{2,1,0:T(8,128)S(1)} %all-to-all-done.2.part_ref, f32[2,32,512]{2,1,0:T(8,128)S(1)} %shard_map.57.first_ref.after_ref), custom_call_target="tpu_custom_call" | custom-call | bytes 2621440 | tf_op jit(solution)/shard_map/pallas_call | solution.py:28
  84.7 3.6 %all-to-all-start.3 = ((f32[4,4,208,128]{3,2,1,0:T(8,128)}), f32[4,4,208,128]{3,2,1,0:T(8,128)S(1)}, u32[]{:S(2)}, u32[]{:S(2)}) async-start(f32[4,4,208,128]{3,2,1,0:T(8,128)} %shard_map.60), calls=%async_computation.3 | async-start | bytes 3407872 | tf_op jit(solution)/shard_map/all_to_all | solution.py:304
  88.3 1.0 collective-permute-done.7.second_ref
  89.3 1.9 %collective-permute-start.8 = (f32[4,32,512]{2,1,0:T(8,128)S(1)}, f32[4,32,512]{2,1,0:T(8,128)S(1)}, u32[]{:S(2)}, u32[]{:S(2)}) collective-permute-start(f32[4,32,512]{2,1,0:T(8,128)S(1)} %shard_map.58.line_ref), channel_id=1, source_target_pairs={{0,64},{16,80},{32,96},{48,112},{64,0},{80,16},{96,32},{112,48},{1... | collective-permute-start | bytes 786440 | tf_op jit(solution)/shard_map/ppermute | solution.py:297
  91.2 6.9 %collective-permute-done.8.far_ref = f32[4,32,512]{2,1,0:T(8,128)S(1)} collective-permute-done((f32[4,32,512]{2,1,0:T(8,128)S(1)}, f32[4,32,512]{2,1,0:T(8,128)S(1)}, u32[]{:S(2)}, u32[]{:S(2)}) %collective-permute-start.8) | collective-permute-done | bytes 262176 | tf_op jit(solution)/shard_map/ppermute | solution.py:297
  98.1 0.6 shard_map.59
  98.7 3.7 %collective-permute-start.9 = (f32[2,32,512]{2,1,0:T(8,128)S(1)}, f32[2,32,512]{2,1,0:T(8,128)S(1)}, u32[]{:S(2)}, u32[]{:S(2)}) collective-permute-start(f32[2,32,512]{2,1,0:T(8,128)S(1)} %get-tuple-element.18), channel_id=1, source_target_pairs={{0,16},{16,0},{32,48},{48,32},{64,80},{80,64},{96,112},{112,96},{1... | collective-permute-start | bytes 393224 | tf_op jit(solution)/shard_map/ppermute | solution.py:297
  102.4 1.9 %collective-permute-start.10 = (f32[2,32,512]{2,1,0:T(8,128)S(1)}, f32[2,32,512]{2,1,0:T(8,128)S(1)}, u32[]{:S(2)}, u32[]{:S(2)}) collective-permute-start(f32[2,32,512]{2,1,0:T(8,128)S(1)} %get-tuple-element.19), channel_id=1, source_target_pairs={{0,32},{16,48},{32,0},{48,16},{64,96},{80,112},{96,64},{112,80},{1... | collective-permute-start | bytes 393224 | tf_op jit(solution)/shard_map/ppermute | solution.py:297
  104.4 3.5 %collective-permute-start.11 = (f32[2,32,512]{2,1,0:T(8,128)S(1)}, f32[2,32,512]{2,1,0:T(8,128)S(1)}, u32[]{:S(2)}, u32[]{:S(2)}) collective-permute-start(f32[2,32,512]{2,1,0:T(8,128)S(1)} %get-tuple-element.20), channel_id=1, source_target_pairs={{0,48},{16,32},{32,16},{48,0},{64,112},{80,96},{96,80},{112,64},{1... | collective-permute-start | bytes 393224 | tf_op jit(solution)/shard_map/ppermute | solution.py:297
  107.9 1.0 all-to-all-done.3.all_ref
  109.0 8.3 %shard_map.61 = (bf16[1,32,512]{2,1,0:T(8,128)(2,1)}, f32[8,128]{1,0:T(8,128)S(1)}) custom-call(s32[1]{0:T(128)} %bitcast.2.place_ref, f32[4,4,208,128]{3,2,1,0:T(8,128)S(1)} %all-to-all-done.3.all_ref, f32[2,32,512]{2,1,0:T(8,128)S(1)} %get-tuple-element.17.after_ref.got0), custom_call_target="tpu_custom_call" | custom-call | flops 5368709120 | bytes 2097152 | tf_op jit(solution)/shard_map/pallas_call | solution.py:28
  117.2 0.0 collective-permute-done.9.got1
  117.2 0.0 collective-permute-done.10.got2
  117.2 0.0 collective-permute-done.11.got3
  117.2 1.2 %shard_map.62 = f32[2,32,512]{2,1,0:T(8,128)} custom-call(s32[48]{0:T(128)S(1)} %copy-done.3, f32[2,32,512]{2,1,0:T(8,128)S(1)} %bitcast.7, f32[2,32,512]{2,1,0:T(8,128)S(1)} %get-tuple-element.17.after_ref.got0, f32[2,32,512]{2,1,0:T(8,128)S(1)} %collective-permute-done.9.got1, f32[2,32,512]{2,1,0:T(8,128)S(1)} %collective-permute-done.10.got2, ...), custom_call_target="tpu_custom_call" | custom-call | bytes 524288 | tf_op jit(solution)/shard_map/pallas_call | solution.py:28
  (3 shorter events, 0.1 us)
Async XLA Ops:
  0.6 12.1 %collective-permute-start = (f32[2,32,512]{2,1,0:T(8,128)}, f32[2,32,512]{2,1,0:T(8,128)S(1)}, u32[]{:S(2)}, u32[]{:S(2)}) collective-permute-start(f32[2,32,512]{2,1,0:T(8,128)} %bitcast.5), channel_id=1, source_target_pairs={{0,32},{16,48},{32,0},{48,16},{64,96},{80,112},{96,64},{112,80},{1... | collective-permute-start | bytes 393224 | tf_op jit(solution)/shard_map/ppermute | solution.py:297
  8.6 4.2 %copy-start = (f32[1,2,32,512]{3,2,1,0:T(8,128)S(1)}, f32[1,2,32,512]{3,2,1,0:T(8,128)}, u32[]{:S(2)}) copy-start(f32[1,2,32,512]{3,2,1,0:T(8,128)} %param.5) | copy-start | bytes 393220
  8.6 27.0 %all-to-all-start = ((f32[4,4,64,512]{3,2,1,0:T(8,128)}), f32[4,4,64,512]{3,2,1,0:T(8,128)S(1)}, u32[]{:S(2)}, u32[]{:S(2)}) async-start(f32[4,4,64,512]{3,2,1,0:T(8,128)} %shard_map.51), calls=%async_computation | async-start | bytes 4194304 | tf_op jit(solution)/shard_map/all_to_all | solution.py:304
  12.8 7.0 %collective-permute-start.1 = (f32[2,2,32,384]{3,2,1,0:T(8,128)S(1)}, f32[2,2,32,384]{3,2,1,0:T(8,128)S(1)}, u32[]{:S(2)}, u32[]{:S(2)}) collective-permute-start(f32[2,2,32,384]{3,2,1,0:T(8,128)S(1)} %shard_map.52.kept_ref), channel_id=1, source_target_pairs={{0,16},{16,0},{32,48},{48,32},{64,80},{80,64},{96,112},{112,96},{1... | collective-permute-start | bytes 589832 | tf_op jit(solution)/shard_map/ppermute | solution.py:297
  19.8 0.7 copy-start.1
  21.0 9.3 %collective-permute-start.2 = (f32[2,32,384]{2,1,0:T(8,128)S(1)}, f32[2,32,384]{2,1,0:T(8,128)S(1)}, u32[]{:S(2)}, u32[]{:S(2)}) collective-permute-start(f32[2,32,384]{2,1,0:T(8,128)S(1)} %get-tuple-element.13), channel_id=1, source_target_pairs={{0,64},{16,80},{32,96},{48,112},{64,0},{80,16},{96,32},{112,48},{1... | collective-permute-start | bytes 294920 | tf_op jit(solution)/shard_map/ppermute | solution.py:297
  22.9 9.3 %collective-permute-start.3 = (f32[2,32,384]{2,1,0:T(8,128)S(1)}, f32[2,32,384]{2,1,0:T(8,128)S(1)}, u32[]{:S(2)}, u32[]{:S(2)}) collective-permute-start(f32[2,32,384]{2,1,0:T(8,128)S(1)} %get-tuple-element.14), channel_id=1, source_target_pairs={{0,128},{16,144},{32,160},{48,176},{64,192},{80,208},{96,224},{112... | collective-permute-start | bytes 294920 | tf_op jit(solution)/shard_map/ppermute | solution.py:297
  26.1 36.8 %copy-start.3 = (s32[48]{0:T(128)S(1)}, s32[48]{0:T(128)}, u32[]{:S(2)}) copy-start(s32[48]{0:T(128)} %shard_map.50.table_ref) | copy-start | bytes 580
  26.1 7.6 %collective-permute-start.4 = (f32[2,32,384]{2,1,0:T(8,128)S(1)}, f32[2,32,384]{2,1,0:T(8,128)S(1)}, u32[]{:S(2)}, u32[]{:S(2)}) collective-permute-start(f32[2,32,384]{2,1,0:T(8,128)S(1)} %get-tuple-element.15), channel_id=1, source_target_pairs={{0,192},{16,208},{32,224},{48,240},{64,128},{80,144},{96,160},{112... | collective-permute-start | bytes 294920 | tf_op jit(solution)/shard_map/ppermute | solution.py:297
  33.7 0.7 copy-start.2
  36.5 26.4 %all-to-all-start.1 = ((f32[4,64,512]{2,1,0:T(8,128)}), f32[4,64,512]{2,1,0:T(8,128)S(1)}, u32[]{:S(2)}, u32[]{:S(2)}) async-start(f32[4,64,512]{2,1,0:T(8,128)} %shard_map.55), calls=%async_computation.1 | async-start | bytes 1048576 | tf_op jit(solution)/shard_map/all_to_all | solution.py:304
  47.9 9.0 %collective-permute-start.5 = (f32[32,384]{1,0:T(8,128)S(1)}, f32[32,384]{1,0:T(8,128)S(1)}, u32[]{:S(2)}, u32[]{:S(2)}) collective-permute-start(f32[32,384]{1,0:T(8,128)S(1)} %shard_map.54.after_ref), channel_id=1, source_target_pairs={{0,256},{16,272},{32,288},{48,304},{64,320},{80,336},{96,352},{112... | collective-permute-start | bytes 147464 | tf_op jit(solution)/shard_map/ppermute | solution.py:297
  64.3 19.1 %all-to-all-start.2 = ((f32[4,208,128]{2,1,0:T(8,128)}), f32[4,208,128]{2,1,0:T(8,128)S(1)}, u32[]{:S(2)}, u32[]{:S(2)}) async-start(f32[4,208,128]{2,1,0:T(8,128)} %get-tuple-element.21), calls=%async_computation.2 | async-start | bytes 851968 | tf_op jit(solution)/shard_map/all_to_all | solution.py:304
  68.6 9.2 %collective-permute-start.6 = (f32[1,32,512]{2,1,0:T(8,128)S(1)}, f32[1,32,512]{2,1,0:T(8,128)S(1)}, u32[]{:S(2)}, u32[]{:S(2)}) collective-permute-start(f32[1,32,512]{2,1,0:T(8,128)S(1)} %get-tuple-element.16.first_ref), channel_id=1, source_target_pairs={{0,256},{16,272},{32,288},{48,304},{64,320},{80,336},{96,352},{112... | collective-permute-start | bytes 196616 | tf_op jit(solution)/shard_map/ppermute | solution.py:297
  77.8 11.5 %collective-permute-start.7 = (f32[2,32,512]{2,1,0:T(8,128)S(1)}, f32[2,32,512]{2,1,0:T(8,128)S(1)}, u32[]{:S(2)}, u32[]{:S(2)}) collective-permute-start(f32[2,32,512]{2,1,0:T(8,128)S(1)} %shard_map.57.first_ref.after_ref), channel_id=1, source_target_pairs={{0,128},{16,144},{32,160},{48,176},{64,192},{80,208},{96,224},{112... | collective-permute-start | bytes 393224 | tf_op jit(solution)/shard_map/ppermute | solution.py:297
  84.7 24.2 %all-to-all-start.3 = ((f32[4,4,208,128]{3,2,1,0:T(8,128)}), f32[4,4,208,128]{3,2,1,0:T(8,128)S(1)}, u32[]{:S(2)}, u32[]{:S(2)}) async-start(f32[4,4,208,128]{3,2,1,0:T(8,128)} %shard_map.60), calls=%async_computation.3 | async-start | bytes 3407872 | tf_op jit(solution)/shard_map/all_to_all | solution.py:304
  89.3 8.8 %collective-permute-start.8 = (f32[4,32,512]{2,1,0:T(8,128)S(1)}, f32[4,32,512]{2,1,0:T(8,128)S(1)}, u32[]{:S(2)}, u32[]{:S(2)}) collective-permute-start(f32[4,32,512]{2,1,0:T(8,128)S(1)} %shard_map.58.line_ref), channel_id=1, source_target_pairs={{0,64},{16,80},{32,96},{48,112},{64,0},{80,16},{96,32},{112,48},{1... | collective-permute-start | bytes 786440 | tf_op jit(solution)/shard_map/ppermute | solution.py:297
  98.7 18.5 %collective-permute-start.9 = (f32[2,32,512]{2,1,0:T(8,128)S(1)}, f32[2,32,512]{2,1,0:T(8,128)S(1)}, u32[]{:S(2)}, u32[]{:S(2)}) collective-permute-start(f32[2,32,512]{2,1,0:T(8,128)S(1)} %get-tuple-element.18), channel_id=1, source_target_pairs={{0,16},{16,0},{32,48},{48,32},{64,80},{80,64},{96,112},{112,96},{1... | collective-permute-start | bytes 393224 | tf_op jit(solution)/shard_map/ppermute | solution.py:297
  102.4 14.8 %collective-permute-start.10 = (f32[2,32,512]{2,1,0:T(8,128)S(1)}, f32[2,32,512]{2,1,0:T(8,128)S(1)}, u32[]{:S(2)}, u32[]{:S(2)}) collective-permute-start(f32[2,32,512]{2,1,0:T(8,128)S(1)} %get-tuple-element.19), channel_id=1, source_target_pairs={{0,32},{16,48},{32,0},{48,16},{64,96},{80,112},{96,64},{112,80},{1... | collective-permute-start | bytes 393224 | tf_op jit(solution)/shard_map/ppermute | solution.py:297
  104.4 12.9 %collective-permute-start.11 = (f32[2,32,512]{2,1,0:T(8,128)S(1)}, f32[2,32,512]{2,1,0:T(8,128)S(1)}, u32[]{:S(2)}, u32[]{:S(2)}) collective-permute-start(f32[2,32,512]{2,1,0:T(8,128)S(1)} %get-tuple-element.20), channel_id=1, source_target_pairs={{0,48},{16,32},{32,16},{48,0},{64,112},{80,96},{96,80},{112,64},{1... | collective-permute-start | bytes 393224 | tf_op jit(solution)/shard_map/ppermute | solution.py:297

commit v10 on v9

--- a/solution.py
+++ b/solution.py
@@ -275,11 +275,16 @@
     thin = (1.25 * thin - 0.25 * last) * jnp.exp(-0.25 * jnp.log(scale))
     mean = [
         jnp.concatenate(
-            [all_ref[x, z, start + m * rows : start + (m + 1) * rows] for z in range(zs) for x in range(xs)], axis=0
+            [
+                (all_ref[x, z, start + m * rows : start + (m + 1) * rows] * (1.0 / count)).astype(bf16)
+                for z in range(zs)
+                for x in range(xs)
+            ],
+            axis=0,
         )
         for m in range(size // LANES)
     ]
-    mean = (jnp.concatenate(mean, axis=1) * (1.0 / count)).astype(bf16)
+    mean = jnp.concatenate(mean, axis=1)
     out_ref[0] = jnp.dot(thin.astype(bf16), mean, preferred_element_type=f32).astype(bf16)
 
 

time: 119 us -> 119 us (level)
  no operation moved by 1% of the time
where the time goes in v10:
time: 119 us; the launch traced here: 118 us
  starting transfers between devices  74.7 us (63%)
  waiting for transfers between devices  22.1 us (19%)
  Pallas kernels  19.5 us (16%)
  local copies, waits for them, and re-layouts  1.32 us (1%)
    ppermute x12, starting transfers between devices, across(): return lax.ppermute(x, 'pre', [(i, i ^ k) for i in range(blocks)])  51.2 us
    all_to_all x4, starting transfers between devices, exchange(): return lax.all_to_all(x, 'rep', 0, 0, tiled=True, axis_index_groups=which)  23.4 us
    pallas_call x12, Pallas kernels, call(): pl.pallas_call(kernel, out_shape=out_shape, in_specs=in_specs, out_specs=...  18 us
    ppermute x12, waiting for transfers between devices, across(): return lax.ppermute(x, 'pre', [(i, i ^ k) for i in range(blocks)])  14.4 us
    all_to_all x4, waiting for transfers between devices, exchange(): return lax.all_to_all(x, 'rep', 0, 0, tiled=True, axis_index_groups=which)  7.72 us
  transfers between devices with their start and end apart: 16, of which 9 were waited for; matrix products, arithmetic and copies ran while one was open for 0% of the time, Pallas kernels for 13%

profile of v10, /device:TPU:1, one launch (start us, length us, event | category | flops | bytes accessed | tf_op | source)
XLA Modules:
  0.0 118.5 jit_solution(12151615379543078530)
XLA Ops:
  0.6 4.8 %collective-permute-start = (f32[2,32,512]{2,1,0:T(8,128)}, f32[2,32,512]{2,1,0:T(8,128)S(1)}, u32[]{:S(2)}, u32[]{:S(2)}) collective-permute-start(f32[2,32,512]{2,1,0:T(8,128)} %bitcast.5), channel_id=1, source_target_pairs={{0,32},{16,48},{32,0},{48,16},{64,96},{80,112},{96,64},{112,80},{1... | collective-permute-start | bytes 393224 | tf_op jit(solution)/shard_map/ppermute | solution.py:302
  5.5 3.1 %shard_map.51 = f32[4,4,64,512]{3,2,1,0:T(8,128)} custom-call(bf16[2,512,512]{2,1,0:T(8,128)(2,1)} %bitcast.8), custom_call_target="tpu_custom_call" | custom-call | flops 536870912 | bytes 4194304 | tf_op jit(solution)/shard_map/pallas_call | solution.py:28
  8.6 0.0 copy-start
  8.6 4.2 %all-to-all-start = ((f32[4,4,64,512]{3,2,1,0:T(8,128)}), f32[4,4,64,512]{3,2,1,0:T(8,128)S(1)}, u32[]{:S(2)}, u32[]{:S(2)}) async-start(f32[4,4,64,512]{3,2,1,0:T(8,128)} %shard_map.51), calls=%async_computation | async-start | bytes 4194304 | tf_op jit(solution)/shard_map/all_to_all | solution.py:309
  12.7 0.0 collective-permute-done.held_z_ref
  12.7 0.0 copy-done
  12.8 5.5 %collective-permute-start.1 = (f32[2,2,32,384]{3,2,1,0:T(8,128)S(1)}, f32[2,2,32,384]{3,2,1,0:T(8,128)S(1)}, u32[]{:S(2)}, u32[]{:S(2)}) collective-permute-start(f32[2,2,32,384]{3,2,1,0:T(8,128)S(1)} %shard_map.52.kept_ref), channel_id=1, source_target_pairs={{0,16},{16,0},{32,48},{48,32},{64,80},{80,64},{96,112},{112,96},{1... | collective-permute-start | bytes 589832 | tf_op jit(solution)/shard_map/ppermute | solution.py:302
  18.3 1.4 %shard_map.50.table_ref = s32[48]{0:T(128)} custom-call(s32[1]{0:T(128)} %bitcast.me_ref, s32[32]{0:T(128)} %owner_ref.1), custom_call_target="tpu_custom_call" | custom-call | tf_op jit(solution)/shard_map/pallas_call | solution.py:313
  19.7 0.0 collective-permute-done.1.core_ref
  19.8 0.0 copy-start.1
  19.8 0.6 copy-done.1
  20.4 0.6 shard_map.53
  21.0 1.9 %collective-permute-start.2 = (f32[2,32,384]{2,1,0:T(8,128)S(1)}, f32[2,32,384]{2,1,0:T(8,128)S(1)}, u32[]{:S(2)}, u32[]{:S(2)}) collective-permute-start(f32[2,32,384]{2,1,0:T(8,128)S(1)} %get-tuple-element.13), channel_id=1, source_target_pairs={{0,64},{16,80},{32,96},{48,112},{64,0},{80,16},{96,32},{112,48},{1... | collective-permute-start | bytes 294920 | tf_op jit(solution)/shard_map/ppermute | solution.py:302
  22.9 3.2 %collective-permute-start.3 = (f32[2,32,384]{2,1,0:T(8,128)S(1)}, f32[2,32,384]{2,1,0:T(8,128)S(1)}, u32[]{:S(2)}, u32[]{:S(2)}) collective-permute-start(f32[2,32,384]{2,1,0:T(8,128)S(1)} %get-tuple-element.14), channel_id=1, source_target_pairs={{0,128},{16,144},{32,160},{48,176},{64,192},{80,208},{96,224},{112... | collective-permute-start | bytes 294920 | tf_op jit(solution)/shard_map/ppermute | solution.py:302
  26.1 0.0 copy-start.3
  26.1 4.2 %collective-permute-start.4 = (f32[2,32,384]{2,1,0:T(8,128)S(1)}, f32[2,32,384]{2,1,0:T(8,128)S(1)}, u32[]{:S(2)}, u32[]{:S(2)}) collective-permute-start(f32[2,32,384]{2,1,0:T(8,128)S(1)} %get-tuple-element.15), channel_id=1, source_target_pairs={{0,192},{16,208},{32,224},{48,240},{64,128},{80,144},{96,160},{112... | collective-permute-start | bytes 294920 | tf_op jit(solution)/shard_map/ppermute | solution.py:302
  30.3 0.0 collective-permute-done.2.near1.refs_0_
  30.3 1.9 %collective-permute-done.3.near2.refs_1_ = f32[2,32,384]{2,1,0:T(8,128)S(1)} collective-permute-done((f32[2,32,384]{2,1,0:T(8,128)S(1)}, f32[2,32,384]{2,1,0:T(8,128)S(1)}, u32[]{:S(2)}, u32[]{:S(2)}) %collective-permute-start.3) | collective-permute-done | bytes 98336 | tf_op jit(solution)/shard_map/ppermute | solution.py:302
  32.3 1.4 %collective-permute-done.4.near3.refs_2_ = f32[2,32,384]{2,1,0:T(8,128)S(1)} collective-permute-done((f32[2,32,384]{2,1,0:T(8,128)S(1)}, f32[2,32,384]{2,1,0:T(8,128)S(1)}, u32[]{:S(2)}, u32[]{:S(2)}) %collective-permute-start.4) | collective-permute-done | bytes 98336 | tf_op jit(solution)/shard_map/ppermute | solution.py:302
  33.7 0.0 copy-start.2
  33.7 0.7 copy-done.2
  34.3 0.6 shard_map.54.after_ref
  34.9 0.7 all-to-all-done.parts_ref
  35.6 0.9 shard_map.55
  36.5 11.4 %all-to-all-start.1 = ((f32[4,64,512]{2,1,0:T(8,128)}), f32[4,64,512]{2,1,0:T(8,128)S(1)}, u32[]{:S(2)}, u32[]{:S(2)}) async-start(f32[4,64,512]{2,1,0:T(8,128)} %shard_map.55), calls=%async_computation.1 | async-start | bytes 1048576 | tf_op jit(solution)/shard_map/all_to_all | solution.py:309
  47.9 7.5 %collective-permute-start.5 = (f32[32,384]{1,0:T(8,128)S(1)}, f32[32,384]{1,0:T(8,128)S(1)}, u32[]{:S(2)}, u32[]{:S(2)}) collective-permute-start(f32[32,384]{1,0:T(8,128)S(1)} %shard_map.54.after_ref), channel_id=1, source_target_pairs={{0,256},{16,272},{32,288},{48,304},{64,320},{80,336},{96,352},{112... | collective-permute-start | bytes 147464 | tf_op jit(solution)/shard_map/ppermute | solution.py:302
  55.3 1.5 %collective-permute-done.5.refs_3_ = f32[32,384]{1,0:T(8,128)S(1)} collective-permute-done((f32[32,384]{1,0:T(8,128)S(1)}, f32[32,384]{1,0:T(8,128)S(1)}, u32[]{:S(2)}, u32[]{:S(2)}) %collective-permute-start.5) | collective-permute-done | bytes 49184 | tf_op jit(solution)/shard_map/ppermute | solution.py:302
  56.8 6.0 %all-to-all-done.1.sums_ref = f32[4,64,512]{2,1,0:T(8,128)S(1)} async-done(((f32[4,64,512]{2,1,0:T(8,128)}), f32[4,64,512]{2,1,0:T(8,128)S(1)}, u32[]{:S(2)}, u32[]{:S(2)}) %all-to-all-start.1) | async-done | bytes 524320 | tf_op jit(solution)/shard_map/all_to_all | solution.py:309
  62.9 0.0 copy-done.3
  62.9 1.5 %shard_map.56 = (f32[4,208,128]{2,1,0:T(8,128)}, f32[1,32,512]{2,1,0:T(8,128)S(1)}) custom-call(s32[48]{0:T(128)S(1)} %copy-done.3, s32[1]{0:T(128)} %bitcast.2.place_ref, f32[4,64,512]{2,1,0:T(8,128)S(1)} %all-to-all-done.1.sums_ref, f32[2,2,32,384]{3,2,1,0:T(8,128)S(1)} %shard_map.52.kept_ref, f32[2,2,32,384]{3,2,1,0:T(8,128)S(1)} %collective-permute-done.1.core_ref, ...), custom_call_target="tpu_custom_call" | custom-call | bytes 2949120 | tf_op jit(solution)/shard_map/pallas_call | solution.py:28
  64.3 4.3 %all-to-all-start.2 = ((f32[4,208,128]{2,1,0:T(8,128)}), f32[4,208,128]{2,1,0:T(8,128)S(1)}, u32[]{:S(2)}, u32[]{:S(2)}) async-start(f32[4,208,128]{2,1,0:T(8,128)} %get-tuple-element.21), calls=%async_computation.2 | async-start | bytes 851968 | tf_op jit(solution)/shard_map/all_to_all | solution.py:309
  68.6 7.4 %collective-permute-start.6 = (f32[1,32,512]{2,1,0:T(8,128)S(1)}, f32[1,32,512]{2,1,0:T(8,128)S(1)}, u32[]{:S(2)}, u32[]{:S(2)}) collective-permute-start(f32[1,32,512]{2,1,0:T(8,128)S(1)} %get-tuple-element.16.first_ref), channel_id=1, source_target_pairs={{0,256},{16,272},{32,288},{48,304},{64,320},{80,336},{96,352},{112... | collective-permute-start | bytes 196616 | tf_op jit(solution)/shard_map/ppermute | solution.py:302
  76.1 1.7 %collective-permute-done.6.second_ref = f32[1,32,512]{2,1,0:T(8,128)S(1)} collective-permute-done((f32[1,32,512]{2,1,0:T(8,128)S(1)}, f32[1,32,512]{2,1,0:T(8,128)S(1)}, u32[]{:S(2)}, u32[]{:S(2)}) %collective-permute-start.6) | collective-permute-done | bytes 65568 | tf_op jit(solution)/shard_map/ppermute | solution.py:302
  77.8 5.6 %collective-permute-start.7 = (f32[2,32,512]{2,1,0:T(8,128)S(1)}, f32[2,32,512]{2,1,0:T(8,128)S(1)}, u32[]{:S(2)}, u32[]{:S(2)}) collective-permute-start(f32[2,32,512]{2,1,0:T(8,128)S(1)} %shard_map.57.first_ref.after_ref), channel_id=1, source_target_pairs={{0,128},{16,144},{32,160},{48,176},{64,192},{80,208},{96,224},{112... | collective-permute-start | bytes 393224 | tf_op jit(solution)/shard_map/ppermute | solution.py:302
  83.4 0.0 all-to-all-done.2.part_ref
  83.5 1.3 %shard_map.60 = f32[4,4,208,128]{3,2,1,0:T(8,128)} custom-call(f32[4,208,128]{2,1,0:T(8,128)S(1)} %all-to-all-done.2.part_ref, f32[2,32,512]{2,1,0:T(8,128)S(1)} %shard_map.57.first_ref.after_ref), custom_call_target="tpu_custom_call" | custom-call | bytes 2621440 | tf_op jit(solution)/shard_map/pallas_call | solution.py:28
  84.7 3.6 %all-to-all-start.3 = ((f32[4,4,208,128]{3,2,1,0:T(8,128)}), f32[4,4,208,128]{3,2,1,0:T(8,128)S(1)}, u32[]{:S(2)}, u32[]{:S(2)}) async-start(f32[4,4,208,128]{3,2,1,0:T(8,128)} %shard_map.60), calls=%async_computation.3 | async-start | bytes 3407872 | tf_op jit(solution)/shard_map/all_to_all | solution.py:309
  88.3 1.0 collective-permute-done.7.second_ref
  89.3 1.9 %collective-permute-start.8 = (f32[4,32,512]{2,1,0:T(8,128)S(1)}, f32[4,32,512]{2,1,0:T(8,128)S(1)}, u32[]{:S(2)}, u32[]{:S(2)}) collective-permute-start(f32[4,32,512]{2,1,0:T(8,128)S(1)} %shard_map.58.line_ref), channel_id=1, source_target_pairs={{0,64},{16,80},{32,96},{48,112},{64,0},{80,16},{96,32},{112,48},{1... | collective-permute-start | bytes 786440 | tf_op jit(solution)/shard_map/ppermute | solution.py:302
  91.2 6.9 %collective-permute-done.8.far_ref = f32[4,32,512]{2,1,0:T(8,128)S(1)} collective-permute-done((f32[4,32,512]{2,1,0:T(8,128)S(1)}, f32[4,32,512]{2,1,0:T(8,128)S(1)}, u32[]{:S(2)}, u32[]{:S(2)}) %collective-permute-start.8) | collective-permute-done | bytes 262176 | tf_op jit(solution)/shard_map/ppermute | solution.py:302
  98.1 0.6 shard_map.59
  98.7 3.7 %collective-permute-start.9 = (f32[2,32,512]{2,1,0:T(8,128)S(1)}, f32[2,32,512]{2,1,0:T(8,128)S(1)}, u32[]{:S(2)}, u32[]{:S(2)}) collective-permute-start(f32[2,32,512]{2,1,0:T(8,128)S(1)} %get-tuple-element.18), channel_id=1, source_target_pairs={{0,16},{16,0},{32,48},{48,32},{64,80},{80,64},{96,112},{112,96},{1... | collective-permute-start | bytes 393224 | tf_op jit(solution)/shard_map/ppermute | solution.py:302
  102.4 1.9 %collective-permute-start.10 = (f32[2,32,512]{2,1,0:T(8,128)S(1)}, f32[2,32,512]{2,1,0:T(8,128)S(1)}, u32[]{:S(2)}, u32[]{:S(2)}) collective-permute-start(f32[2,32,512]{2,1,0:T(8,128)S(1)} %get-tuple-element.19), channel_id=1, source_target_pairs={{0,32},{16,48},{32,0},{48,16},{64,96},{80,112},{96,64},{112,80},{1... | collective-permute-start | bytes 393224 | tf_op jit(solution)/shard_map/ppermute | solution.py:302
  104.4 3.5 %collective-permute-start.11 = (f32[2,32,512]{2,1,0:T(8,128)S(1)}, f32[2,32,512]{2,1,0:T(8,128)S(1)}, u32[]{:S(2)}, u32[]{:S(2)}) collective-permute-start(f32[2,32,512]{2,1,0:T(8,128)S(1)} %get-tuple-element.20), channel_id=1, source_target_pairs={{0,48},{16,32},{32,16},{48,0},{64,112},{80,96},{96,80},{112,64},{1... | collective-permute-start | bytes 393224 | tf_op jit(solution)/shard_map/ppermute | solution.py:302
  107.9 1.0 all-to-all-done.3.all_ref
  109.0 8.3 %shard_map.61 = (bf16[1,32,512]{2,1,0:T(8,128)(2,1)}, f32[8,128]{1,0:T(8,128)S(1)}) custom-call(s32[1]{0:T(128)} %bitcast.2.place_ref, f32[4,4,208,128]{3,2,1,0:T(8,128)S(1)} %all-to-all-done.3.all_ref, f32[2,32,512]{2,1,0:T(8,128)S(1)} %get-tuple-element.17.after_ref.got0), custom_call_target="tpu_custom_call" | custom-call | flops 5368709120 | bytes 2097152 | tf_op jit(solution)/shard_map/pallas_call | solution.py:28
  117.2 0.0 collective-permute-done.9.got1
  117.2 0.0 collective-permute-done.10.got2
  117.2 0.0 collective-permute-done.11.got3
  117.2 1.2 %shard_map.62 = f32[2,32,512]{2,1,0:T(8,128)} custom-call(s32[48]{0:T(128)S(1)} %copy-done.3, f32[2,32,512]{2,1,0:T(8,128)S(1)} %bitcast.7, f32[2,32,512]{2,1,0:T(8,128)S(1)} %get-tuple-element.17.after_ref.got0, f32[2,32,512]{2,1,0:T(8,128)S(1)} %collective-permute-done.9.got1, f32[2,32,512]{2,1,0:T(8,128)S(1)} %collective-permute-done.10.got2, ...), custom_call_target="tpu_custom_call" | custom-call | bytes 524288 | tf_op jit(solution)/shard_map/pallas_call | solution.py:28
  (3 shorter events, 0.1 us)
Async XLA Ops:
  0.6 12.1 %collective-permute-start = (f32[2,32,512]{2,1,0:T(8,128)}, f32[2,32,512]{2,1,0:T(8,128)S(1)}, u32[]{:S(2)}, u32[]{:S(2)}) collective-permute-start(f32[2,32,512]{2,1,0:T(8,128)} %bitcast.5), channel_id=1, source_target_pairs={{0,32},{16,48},{32,0},{48,16},{64,96},{80,112},{96,64},{112,80},{1... | collective-permute-start | bytes 393224 | tf_op jit(solution)/shard_map/ppermute | solution.py:302
  8.6 4.2 %copy-start = (f32[1,2,32,512]{3,2,1,0:T(8,128)S(1)}, f32[1,2,32,512]{3,2,1,0:T(8,128)}, u32[]{:S(2)}) copy-start(f32[1,2,32,512]{3,2,1,0:T(8,128)} %param.5) | copy-start | bytes 393220
  8.6 27.0 %all-to-all-start = ((f32[4,4,64,512]{3,2,1,0:T(8,128)}), f32[4,4,64,512]{3,2,1,0:T(8,128)S(1)}, u32[]{:S(2)}, u32[]{:S(2)}) async-start(f32[4,4,64,512]{3,2,1,0:T(8,128)} %shard_map.51), calls=%async_computation | async-start | bytes 4194304 | tf_op jit(solution)/shard_map/all_to_all | solution.py:309
  12.8 7.0 %collective-permute-start.1 = (f32[2,2,32,384]{3,2,1,0:T(8,128)S(1)}, f32[2,2,32,384]{3,2,1,0:T(8,128)S(1)}, u32[]{:S(2)}, u32[]{:S(2)}) collective-permute-start(f32[2,2,32,384]{3,2,1,0:T(8,128)S(1)} %shard_map.52.kept_ref), channel_id=1, source_target_pairs={{0,16},{16,0},{32,48},{48,32},{64,80},{80,64},{96,112},{112,96},{1... | collective-permute-start | bytes 589832 | tf_op jit(solution)/shard_map/ppermute | solution.py:302
  19.8 0.7 copy-start.1
  21.0 9.3 %collective-permute-start.2 = (f32[2,32,384]{2,1,0:T(8,128)S(1)}, f32[2,32,384]{2,1,0:T(8,128)S(1)}, u32[]{:S(2)}, u32[]{:S(2)}) collective-permute-start(f32[2,32,384]{2,1,0:T(8,128)S(1)} %get-tuple-element.13), channel_id=1, source_target_pairs={{0,64},{16,80},{32,96},{48,112},{64,0},{80,16},{96,32},{112,48},{1... | collective-permute-start | bytes 294920 | tf_op jit(solution)/shard_map/ppermute | solution.py:302
  22.9 9.3 %collective-permute-start.3 = (f32[2,32,384]{2,1,0:T(8,128)S(1)}, f32[2,32,384]{2,1,0:T(8,128)S(1)}, u32[]{:S(2)}, u32[]{:S(2)}) collective-permute-start(f32[2,32,384]{2,1,0:T(8,128)S(1)} %get-tuple-element.14), channel_id=1, source_target_pairs={{0,128},{16,144},{32,160},{48,176},{64,192},{80,208},{96,224},{112... | collective-permute-start | bytes 294920 | tf_op jit(solution)/shard_map/ppermute | solution.py:302
  26.1 36.8 %copy-start.3 = (s32[48]{0:T(128)S(1)}, s32[48]{0:T(128)}, u32[]{:S(2)}) copy-start(s32[48]{0:T(128)} %shard_map.50.table_ref) | copy-start | bytes 580
  26.1 7.6 %collective-permute-start.4 = (f32[2,32,384]{2,1,0:T(8,128)S(1)}, f32[2,32,384]{2,1,0:T(8,128)S(1)}, u32[]{:S(2)}, u32[]{:S(2)}) collective-permute-start(f32[2,32,384]{2,1,0:T(8,128)S(1)} %get-tuple-element.15), channel_id=1, source_target_pairs={{0,192},{16,208},{32,224},{48,240},{64,128},{80,144},{96,160},{112... | collective-permute-start | bytes 294920 | tf_op jit(solution)/shard_map/ppermute | solution.py:302
  33.7 0.7 copy-start.2
  36.5 26.4 %all-to-all-start.1 = ((f32[4,64,512]{2,1,0:T(8,128)}), f32[4,64,512]{2,1,0:T(8,128)S(1)}, u32[]{:S(2)}, u32[]{:S(2)}) async-start(f32[4,64,512]{2,1,0:T(8,128)} %shard_map.55), calls=%async_computation.1 | async-start | bytes 1048576 | tf_op jit(solution)/shard_map/all_to_all | solution.py:309
  47.9 9.0 %collective-permute-start.5 = (f32[32,384]{1,0:T(8,128)S(1)}, f32[32,384]{1,0:T(8,128)S(1)}, u32[]{:S(2)}, u32[]{:S(2)}) collective-permute-start(f32[32,384]{1,0:T(8,128)S(1)} %shard_map.54.after_ref), channel_id=1, source_target_pairs={{0,256},{16,272},{32,288},{48,304},{64,320},{80,336},{96,352},{112... | collective-permute-start | bytes 147464 | tf_op jit(solution)/shard_map/ppermute | solution.py:302
  64.3 19.1 %all-to-all-start.2 = ((f32[4,208,128]{2,1,0:T(8,128)}), f32[4,208,128]{2,1,0:T(8,128)S(1)}, u32[]{:S(2)}, u32[]{:S(2)}) async-start(f32[4,208,128]{2,1,0:T(8,128)} %get-tuple-element.21), calls=%async_computation.2 | async-start | bytes 851968 | tf_op jit(solution)/shard_map/all_to_all | solution.py:309
  68.6 9.2 %collective-permute-start.6 = (f32[1,32,512]{2,1,0:T(8,128)S(1)}, f32[1,32,512]{2,1,0:T(8,128)S(1)}, u32[]{:S(2)}, u32[]{:S(2)}) collective-permute-start(f32[1,32,512]{2,1,0:T(8,128)S(1)} %get-tuple-element.16.first_ref), channel_id=1, source_target_pairs={{0,256},{16,272},{32,288},{48,304},{64,320},{80,336},{96,352},{112... | collective-permute-start | bytes 196616 | tf_op jit(solution)/shard_map/ppermute | solution.py:302
  77.8 11.5 %collective-permute-start.7 = (f32[2,32,512]{2,1,0:T(8,128)S(1)}, f32[2,32,512]{2,1,0:T(8,128)S(1)}, u32[]{:S(2)}, u32[]{:S(2)}) collective-permute-start(f32[2,32,512]{2,1,0:T(8,128)S(1)} %shard_map.57.first_ref.after_ref), channel_id=1, source_target_pairs={{0,128},{16,144},{32,160},{48,176},{64,192},{80,208},{96,224},{112... | collective-permute-start | bytes 393224 | tf_op jit(solution)/shard_map/ppermute | solution.py:302
  84.7 24.2 %all-to-all-start.3 = ((f32[4,4,208,128]{3,2,1,0:T(8,128)}), f32[4,4,208,128]{3,2,1,0:T(8,128)S(1)}, u32[]{:S(2)}, u32[]{:S(2)}) async-start(f32[4,4,208,128]{3,2,1,0:T(8,128)} %shard_map.60), calls=%async_computation.3 | async-start | bytes 3407872 | tf_op jit(solution)/shard_map/all_to_all | solution.py:309
  89.3 8.8 %collective-permute-start.8 = (f32[4,32,512]{2,1,0:T(8,128)S(1)}, f32[4,32,512]{2,1,0:T(8,128)S(1)}, u32[]{:S(2)}, u32[]{:S(2)}) collective-permute-start(f32[4,32,512]{2,1,0:T(8,128)S(1)} %shard_map.58.line_ref), channel_id=1, source_target_pairs={{0,64},{16,80},{32,96},{48,112},{64,0},{80,16},{96,32},{112,48},{1... | collective-permute-start | bytes 786440 | tf_op jit(solution)/shard_map/ppermute | solution.py:302
  98.7 18.5 %collective-permute-start.9 = (f32[2,32,512]{2,1,0:T(8,128)S(1)}, f32[2,32,512]{2,1,0:T(8,128)S(1)}, u32[]{:S(2)}, u32[]{:S(2)}) collective-permute-start(f32[2,32,512]{2,1,0:T(8,128)S(1)} %get-tuple-element.18), channel_id=1, source_target_pairs={{0,16},{16,0},{32,48},{48,32},{64,80},{80,64},{96,112},{112,96},{1... | collective-permute-start | bytes 393224 | tf_op jit(solution)/shard_map/ppermute | solution.py:302
  102.4 14.8 %collective-permute-start.10 = (f32[2,32,512]{2,1,0:T(8,128)S(1)}, f32[2,32,512]{2,1,0:T(8,128)S(1)}, u32[]{:S(2)}, u32[]{:S(2)}) collective-permute-start(f32[2,32,512]{2,1,0:T(8,128)S(1)} %get-tuple-element.19), channel_id=1, source_target_pairs={{0,32},{16,48},{32,0},{48,16},{64,96},{80,112},{96,64},{112,80},{1... | collective-permute-start | bytes 393224 | tf_op jit(solution)/shard_map/ppermute | solution.py:302
  104.4 12.9 %collective-permute-start.11 = (f32[2,32,512]{2,1,0:T(8,128)S(1)}, f32[2,32,512]{2,1,0:T(8,128)S(1)}, u32[]{:S(2)}, u32[]{:S(2)}) collective-permute-start(f32[2,32,512]{2,1,0:T(8,128)S(1)} %get-tuple-element.20), channel_id=1, source_target_pairs={{0,48},{16,32},{32,16},{48,0},{64,112},{80,96},{96,80},{112,64},{1... | collective-permute-start | bytes 393224 | tf_op jit(solution)/shard_map/ppermute | solution.py:302
